TPU v7x, 128 devices: a whole 4x4x4 slice. The times are simulated.
128 devices in a mesh: along: 64 (over z, x_lo, y, core), cross: 2 (over x_hi).
Axes of the slice: x: 4 (x_hi: 2, x_lo: 2; x = x_hi * 2 + x_lo), y: 4, z: 4, core: 2. Of those that a mesh axis runs over, the one named last changes fastest.
Arguments:
- velocity: float32 [4, 2048, 3072], P(None, 'along', 'cross'), may hold values from -6 to 6
- surface: float32 [2048, 3072], P('along', 'cross'), may hold values from -0.25 to 0.25
- wet_mask: int32 [2048, 3072], P('along', 'cross'), may hold values from 0 to 1
- bathy_class: int32 [2048, 3072], P('along', 'cross'), may hold values from 0 to 15
- depth_table: float32 [16], replicated, may hold values from 0.5 to 4
- hull_ranges: int32 [8, 4], replicated, may hold values from 0 to 3072, as said below
- hull_pressure: float32 [8], replicated, may hold values from 0.2 to 1
Outputs:
- new_velocity: float32 [4, 2048, 3072], P(None, 'along', 'cross')
- new_surface: float32 [2048, 3072], P('along', 'cross')
- pressure: float32 [2, 2048, 3072], P(None, 'along', 'cross')
Inputs may be any that keep to these rules, and one draw needn't show every extreme that they name: `hull_ranges`: every ship covers 100 // 2 to 100 cells along the channel and 10 to 20 cells across it, inside the grid. Ship 0 lies at the channel's far end, ship 1 at its far bank, ship 2 at its near bank.
All inputs are finite; a program needn't handle non-finite values.
Results may differ from a plain program's by a relative error of at most 0.0003.
Values sent between devices are 32-bit elements; how exact they have to be, the bound alone decides.
No kernel may reach another device: no remote copies, remote signals or barrier semaphores. Data moves between devices by JAX's collectives and lax.ppermute only.
A program may use at most 64 MiB of HBM per device.

v0:
```python
import jax
import jax.numpy as jnp
from jax import lax
from jax.sharding import PartitionSpec as P

LAYERS = 2
ITERS = 3
STEPS = 2
CLASSES = 16


gravity = 9.81
time_step = 0.1
viscosity = 0.5
layer_drag = 0.5
bottom_drag = 0.5
storage = 0.1
vertical = 0.5
corner_weight = 0.25
link_table = (
    (1, 0, 1.0),
    (-1, 0, 1.0),
    (0, 1, 1.0),
    (0, -1, 1.0),
    (1, 1, corner_weight),
    (-1, -1, corner_weight),
    (1, -1, corner_weight),
    (-1, 1, corner_weight),
)


def padded(x, sides, width):
    for axis, dim in sides:
        size, length = (lax.axis_size(axis), x.shape[dim])
        up = [(i, (i + 1) % size) for i in range(size - 1)]
        down = [(j, i) for i, j in up]
        last = lax.slice_in_dim(x, length - width, length, axis=dim)
        leading = lax.slice_in_dim(x, 0, width, axis=dim)
        before = lax.ppermute(last, axis, up)
        after = lax.ppermute(leading, axis, down)
        x = jnp.concatenate([before, x, after], axis=dim)
    return x


def shifted(values, step_along, step_cross, margin):
    row_count = values.shape[-2] - 2 * margin
    col_count = values.shape[-1] - 2 * margin
    return values[
        ...,
        margin + step_along : margin + step_along + row_count,
        margin + step_cross : margin + step_cross + col_count,
    ]


def depth_of(bathy_class, depth_table):
    result = jnp.zeros(bathy_class.shape, jnp.float32)
    for number in range(CLASSES):
        result = jnp.where(bathy_class == number, depth_table[number], result)
    return result


def hull_heads(hull_ranges, hull_pressure, along_first, along_count, cross_first, cross_count):
    along_index = along_first + jnp.arange(along_count, dtype=jnp.int32)
    cross_index = cross_first + jnp.arange(cross_count, dtype=jnp.int32)
    inside_along = jnp.logical_and(
        along_index[None, :] >= hull_ranges[:, 0:1], along_index[None, :] < hull_ranges[:, 1:2]
    ).astype(jnp.float32)
    inside_cross = jnp.logical_and(
        cross_index[None, :] >= hull_ranges[:, 2:3], cross_index[None, :] < hull_ranges[:, 3:4]
    ).astype(jnp.float32)
    return jnp.einsum(
        "si,sj->ij",
        inside_along * hull_pressure[:, None],
        inside_cross,
        precision=lax.Precision.HIGHEST,
    )


def predict(fields_ext, heads_ext, layer_thick, wet_cells):
    potential = gravity * (fields_ext[4] + heads_ext)
    grad_along = 0.5 * (shifted(potential, 1, 0, 2) - shifted(potential, -1, 0, 2))
    grad_cross = 0.5 * (shifted(potential, 0, 1, 2) - shifted(potential, 0, -1, 2))
    along_vel = fields_ext[0:2]
    cross_vel = fields_ext[2:4]
    centre_u = shifted(along_vel, 0, 0, 2)
    centre_v = shifted(cross_vel, 0, 0, 2)
    layer_mask = jnp.array([0.0, 1.0], jnp.float32)[:, None, None]

    def tendency(values, gradient):
        center = shifted(values, 0, 0, 2)
        back_a = 0.5 * (3.0 * center - 4.0 * shifted(values, -1, 0, 2) + shifted(values, -2, 0, 2))
        fore_a = 0.5 * (-3.0 * center + 4.0 * shifted(values, 1, 0, 2) - shifted(values, 2, 0, 2))
        back_c = 0.5 * (3.0 * center - 4.0 * shifted(values, 0, -1, 2) + shifted(values, 0, -2, 2))
        fore_c = 0.5 * (-3.0 * center + 4.0 * shifted(values, 0, 1, 2) - shifted(values, 0, 2, 2))
        advect = (
            jnp.maximum(centre_u, 0.0) * back_a
            + jnp.minimum(centre_u, 0.0) * fore_a
            + jnp.maximum(centre_v, 0.0) * back_c
            + jnp.minimum(centre_v, 0.0) * fore_c
        )
        spread = (
            shifted(values, 1, 0, 2)
            + shifted(values, -1, 0, 2)
            + shifted(values, 0, 1, 2)
            + shifted(values, 0, -1, 2)
            - 4.0 * center
        )
        coupling = (center[::-1] - center) / layer_thick
        change = (
            -gradient
            - advect
            + viscosity * spread
            + layer_drag * coupling
            - bottom_drag * layer_mask * center / layer_thick
        )
        return wet_cells * (center + time_step * change)

    return jnp.concatenate(
        [tendency(along_vel, grad_along), tendency(cross_vel, grad_cross)], axis=0
    )


def divergence(ustar_ext, conduct_ext):
    flux_a = conduct_ext * ustar_ext[0:2]
    flux_c = conduct_ext * ustar_ext[2:4]
    return -(
        shifted(flux_a, 1, 0, 1)
        - shifted(flux_a, -1, 0, 1)
        + (shifted(flux_c, 0, 1, 1) - shifted(flux_c, 0, -1, 1))
    ) / (2.0 * time_step)


def apply_operator(search_ext, conduct_ext, layer_thick):
    middle = shifted(search_ext, 0, 0, 1)
    conduct_mid = shifted(conduct_ext, 0, 0, 1)
    result = storage * layer_thick * middle + vertical / layer_thick * (middle - middle[::-1])
    for step_along, step_cross, weight in link_table:
        link_coef = weight * 0.5 * (conduct_mid + shifted(conduct_ext, step_along, step_cross, 1))
        result = result + link_coef * (middle - shifted(search_ext, step_along, step_cross, 1))
    return result


def diagonal_of(conduct_ext, layer_thick):
    conduct_mid = shifted(conduct_ext, 0, 0, 1)
    result = storage * layer_thick + vertical / layer_thick
    for step_along, step_cross, weight in link_table:
        result = result + weight * 0.5 * (
            conduct_mid + shifted(conduct_ext, step_along, step_cross, 1)
        )
    return result


def extend(search):
    result = padded(search, (("along", 1), ("cross", 2)), 1)
    return result


def weighted_norm(residual, precond):
    return lax.psum(jnp.sum(residual * precond), ("along", "cross"))


def solve(source, conduct_ext, diagonal, layer_thick):
    solution = jnp.zeros_like(source)
    residual = source
    precond = residual / diagonal
    search = precond
    norm_now = weighted_norm(residual, precond)
    for iteration in range(ITERS):
        applied = apply_operator(extend(search), conduct_ext, layer_thick)
        step_size = norm_now / lax.psum(jnp.sum(search * applied), ("along", "cross"))
        solution = solution + step_size * search
        residual = residual - step_size * applied
        if iteration + 1 < ITERS:
            precond = residual / diagonal
            norm_next = weighted_norm(residual, precond)
            search = precond + norm_next / norm_now * search
            norm_now = norm_next
    return solution


def correct(surface_now, ustar_ext, pressure_ext, conduct_ext, wet_cells):
    slope_a = 0.5 * (shifted(pressure_ext, 1, 0, 1) - shifted(pressure_ext, -1, 0, 1))
    slope_c = 0.5 * (shifted(pressure_ext, 0, 1, 1) - shifted(pressure_ext, 0, -1, 1))
    moved_a = ustar_ext[0:2] - time_step * slope_a
    moved_c = ustar_ext[2:4] - time_step * slope_c
    flux_a = jnp.sum(conduct_ext * moved_a, axis=0)
    flux_c = jnp.sum(conduct_ext * moved_c, axis=0)
    new_surface = surface_now - time_step * 0.5 * (
        shifted(flux_a, 1, 0, 1)
        - shifted(flux_a, -1, 0, 1)
        + (shifted(flux_c, 0, 1, 1) - shifted(flux_c, 0, -1, 1))
    )
    new_vel = wet_cells * jnp.concatenate(
        [shifted(moved_a, 0, 0, 1), shifted(moved_c, 0, 0, 1)], axis=0
    )
    return jnp.concatenate([new_vel, new_surface[None]], axis=0)


def shards(velocity, surface, wet_mask, bathy_class, depth_table, hull_ranges, hull_pressure):
    span_a = surface.shape[0]
    span_c = surface.shape[1]
    wet_cells = wet_mask.astype(jnp.float32)
    layer_thick = 0.5 * depth_of(bathy_class, depth_table)
    wet_ext, thick_ext = (
        padded(wet_cells, (("along", 0), ("cross", 1)), 1),
        padded(layer_thick, (("along", 0), ("cross", 1)), 1),
    )
    conduct_ext = wet_ext * thick_ext
    diagonal = diagonal_of(conduct_ext, layer_thick)
    along_first = lax.axis_index("along") * span_a
    cross_first = lax.axis_index("cross") * span_c
    heads_ext = hull_heads(
        hull_ranges, hull_pressure, along_first - 2, span_a + 4, cross_first - 2, span_c + 4
    )
    fields = jnp.concatenate([velocity * wet_cells, surface[None]], axis=0)
    pressure = jnp.zeros((LAYERS, span_a, span_c), jnp.float32)
    for step_number in range(STEPS):
        fields_ext = padded(fields, (("along", 1), ("cross", 2)), 2)
        predicted = predict(fields_ext, heads_ext, layer_thick, wet_cells)
        ustar_ext = padded(predicted, (("along", 1), ("cross", 2)), 1)
        source = divergence(ustar_ext, conduct_ext)
        pressure = solve(source, conduct_ext, diagonal, layer_thick)
        pressure_ext = padded(pressure, (("along", 1), ("cross", 2)), 2)
        fields = correct(fields[4], ustar_ext, pressure_ext, conduct_ext, wet_cells)
    return (fields[0:4], fields[4], pressure)


def solution(mesh):
    in_specs = (
        P(None, "along", "cross"),
        P("along", "cross"),
        P("along", "cross"),
        P("along", "cross"),
        P(),
        P(),
        P(),
    )
    out_specs = (P(None, "along", "cross"), P("along", "cross"), P(None, "along", "cross"))
    return jax.shard_map(shards, mesh=mesh, in_specs=in_specs, out_specs=out_specs, check_vma=False)
```

profile of v0, /device:TPU:1, one launch (start us, length us, event | category | flops | bytes accessed | tf_op | source)
XLA Modules:
  0.0 1007.4 jit_solution(3715393190998449001)
XLA Ops:
  3.0 4.6 collective-permute-start
  10.2 10.1 %broadcast_multiply_fusion.1 = (f32[32,1536]{1,0:T(8,128)S(1)}, f32[32,1536]{1,0:T(8,128)S(1)}) fusion(f32[]{:T(128)} %bitcast.21, s32[32,1536]{1,0:T(8,128)S(1)} %copy-done.42, f32[]{:T(128)} %bitcast.20, f32[]{:T(128)} %bitcast.19, f32[]{:T(128)} %bitcast.18, f32[]{:T(128)} %bitcast.17, f32[]{:T(128)} %bitcast.16, f32[]{:T(128)} %bitcast.15, f32[]{:T(128)} %bitcast.14, ...), kind=kLoop, calls=%fused_computation.419 | loop fusion | flops 1622016 | bytes 589888 | tf_op jit(solution)/shard_map/mul | solution.py:145
  20.4 3.6 collective-permute-start.12
  26.0 3.6 collective-permute-start.8
  33.6 4.6 collective-permute-start.14
  40.6 6.1 collective-permute-start.2
  49.3 5.0 collective-permute-done.3
  54.2 2.5 concatenate.256
  56.7 2.1 fusion.223
  62.8 5.2 collective-permute-start.4
  74.3 3.8 collective-permute-done.11
  82.1 5.0 collective-permute-done.7
  87.0 2.3 concatenate.263
  92.9 6.0 collective-permute-start.17
  101.1 5.5 collective-permute-start.19
  108.0 2.1 multiply_reduce_fusion.12
  110.1 81.2 %all-reduce.1 = (f32[]{:T(128)}, f32[]{:T(128)}) all-reduce(f32[]{:T(128)} %get-tuple-element.6, f32[]{:T(128)} %get-tuple-element.5), channel_id=1, replica_groups=mesh['along'=64,'cross'=2] {'along','cross'}, use_global_device_ids=true, to_apply=%region_1.2 | all-reduce | flops 2 | bytes 16 | tf_op jit(solution)/shard_map/psum | solution.py:159
  192.5 2.4 multiply_reduce_fusion.11
  195.0 64.4 %psum.86 = f32[]{:T(128)} all-reduce(f32[]{:T(128)} %get-tuple-element.28), channel_id=1, replica_groups=mesh['along'=64,'cross'=2] {'along','cross'}, use_global_device_ids=true, to_apply=%region_5.6 | all-reduce | flops 1 | bytes 8 | tf_op jit(solution)/shard_map/psum | solution.py:159
  261.8 3.0 collective-permute-start.20
  264.8 2.5 collective-permute-start.21
  269.5 5.7 collective-permute-start.23
  276.4 2.0 multiply_reduce_fusion.10
  278.4 69.9 %psum.87 = f32[]{:T(128)} all-reduce(f32[]{:T(128)} %get-tuple-element.26), channel_id=1, replica_groups=mesh['along'=64,'cross'=2] {'along','cross'}, use_global_device_ids=true, to_apply=%region_7.8 | all-reduce | flops 1 | bytes 8 | tf_op jit(solution)/shard_map/psum | solution.py:170
  351.5 62.5 %psum.88 = f32[]{:T(128)} all-reduce(f32[]{:T(128)} %multiply_reduce_fusion.9), channel_id=1, replica_groups=mesh['along'=64,'cross'=2] {'along','cross'}, use_global_device_ids=true, to_apply=%region_9.10 | all-reduce | flops 1 | bytes 8 | tf_op jit(solution)/shard_map/psum | solution.py:159
  416.6 2.6 collective-permute-start.24
  419.2 3.1 collective-permute-start.25
  424.5 5.5 collective-permute-start.27
  432.8 69.4 %psum.89 = f32[]{:T(128)} all-reduce(f32[]{:T(128)} %fusion.215), channel_id=1, replica_groups=mesh['along'=64,'cross'=2] {'along','cross'}, use_global_device_ids=true, to_apply=%region_11.12 | all-reduce | flops 1 | bytes 8 | tf_op jit(solution)/shard_map/psum | solution.py:170
  503.6 3.9 collective-permute-start.28
  509.5 3.2 collective-permute-done.29
  513.7 3.4 collective-permute-start.30
  518.4 4.9 collective-permute-done.31
  523.3 2.0 concatenate.284
  525.3 2.1 multiply_reduce_fusion.3
  528.7 3.4 collective-permute-start.32
  534.8 2.8 collective-permute-done.33
  539.0 2.0 collective-permute-start.34
  543.9 4.0 collective-permute-done.35
  548.0 2.5 concatenate.290
  555.6 3.3 collective-permute-start.36
  560.9 3.2 collective-permute-done.37
  567.3 5.2 collective-permute-done.39
  575.6 2.1 collective-permute-start.40
  577.7 3.6 collective-permute-start.41
  583.5 5.5 collective-permute-start.43
  590.4 2.1 multiply_reduce_fusion.7
  592.5 79.5 %all-reduce = (f32[]{:T(128)}, f32[]{:T(128)}) all-reduce(f32[]{:T(128)} %get-tuple-element.4, f32[]{:T(128)} %get-tuple-element.3), channel_id=1, replica_groups=mesh['along'=64,'cross'=2] {'along','cross'}, use_global_device_ids=true, to_apply=%region_15.16 | all-reduce | flops 2 | bytes 16 | tf_op jit(solution)/shard_map/psum | solution.py:159
  673.4 2.4 multiply_reduce_fusion.6
  675.8 64.4 %psum.92 = f32[]{:T(128)} all-reduce(f32[]{:T(128)} %get-tuple-element.19), channel_id=1, replica_groups=mesh['along'=64,'cross'=2] {'along','cross'}, use_global_device_ids=true, to_apply=%region_19.20 | all-reduce | flops 1 | bytes 8 | tf_op jit(solution)/shard_map/psum | solution.py:159
  742.5 3.0 collective-permute-start.44
  745.5 2.6 collective-permute-start.45
  750.3 5.5 collective-permute-start.47
  757.2 2.0 multiply_reduce_fusion.5
  759.2 70.0 %psum.93 = f32[]{:T(128)} all-reduce(f32[]{:T(128)} %get-tuple-element.17), channel_id=1, replica_groups=mesh['along'=64,'cross'=2] {'along','cross'}, use_global_device_ids=true, to_apply=%region_21.22 | all-reduce | flops 1 | bytes 8 | tf_op jit(solution)/shard_map/psum | solution.py:170
  832.3 62.5 %psum.94 = f32[]{:T(128)} all-reduce(f32[]{:T(128)} %multiply_reduce_fusion.4), channel_id=1, replica_groups=mesh['along'=64,'cross'=2] {'along','cross'}, use_global_device_ids=true, to_apply=%region_23.24 | all-reduce | flops 1 | bytes 8 | tf_op jit(solution)/shard_map/psum | solution.py:159
  897.4 2.6 collective-permute-start.48
  900.1 3.1 collective-permute-start.49
  905.3 5.5 collective-permute-start.51
  913.6 69.4 %psum.95 = f32[]{:T(128)} all-reduce(f32[]{:T(128)} %fusion.214), channel_id=1, replica_groups=mesh['along'=64,'cross'=2] {'along','cross'}, use_global_device_ids=true, to_apply=%region_25.26 | all-reduce | flops 1 | bytes 8 | tf_op jit(solution)/shard_map/psum | solution.py:170
  984.5 3.9 collective-permute-start.52
  990.4 3.2 collective-permute-done.53
  993.7 3.4 collective-permute-start.54
  998.4 4.9 collective-permute-done.55
  (253 shorter events, 98.2 us)
Async XLA Ops:
  2.9 26.8 %copy-start.44 = (s32[8,4]{0,1:T(4,128)S(1)}, s32[8,4]{0,1:T(4,128)}, u32[]{:S(2)}) copy-start(s32[8,4]{0,1:T(4,128)} %param.14) | copy-start | bytes 388
  3.0 37.3 %collective-permute-start = (f32[5,2,1536]{2,1,0:T(2,128)S(1)}, f32[5,2,1536]{2,1,0:T(2,128)S(1)}, u32[]{:S(2)}, u32[]{:S(2)}) collective-permute-start(f32[5,2,1536]{2,1,0:T(2,128)S(1)} %get-tuple-element.66), channel_id=1, source_target_pairs={{0,2},{2,4},{4,6},{6,8},{8,10},{10,12},{12,14},{14,16},{16,18},{18... | collective-permute-start | bytes 184328 | tf_op jit(solution)/shard_map/ppermute | solution.py:39
  7.6 32.7 %collective-permute-start.1 = (f32[5,2,1536]{2,1,0:T(2,128)S(1)}, f32[5,2,1536]{2,1,0:T(2,128)S(1)}, u32[]{:S(2)}, u32[]{:S(2)}) collective-permute-start(f32[5,2,1536]{2,1,0:T(2,128)S(1)} %get-tuple-element.67), channel_id=1, source_target_pairs={{2,0},{4,2},{6,4},{8,6},{10,8},{12,10},{14,12},{16,14},{18,16},{20... | collective-permute-start | bytes 184328 | tf_op jit(solution)/shard_map/ppermute | solution.py:40
  20.4 20.1 %copy-start.29 = (f32[32,1536]{1,0:T(8,128)}, f32[32,1536]{1,0:T(8,128)S(1)}, u32[]{:S(2)}) copy-start(f32[32,1536]{1,0:T(8,128)S(1)} %get-tuple-element.32) | copy-start | bytes 589828
  20.4 41.3 %copy-start.11 = (f32[32,1536]{1,0:T(8,128)}, f32[32,1536]{1,0:T(8,128)S(1)}, u32[]{:S(2)}) copy-start(f32[32,1536]{1,0:T(8,128)S(1)} %broadcast_multiply_fusion.2) | copy-start | bytes 589828
  20.4 10.4 %collective-permute-start.12 = (f32[1,1536]{1,0:T(1,128)S(1)}, f32[1,1536]{1,0:T(1,128)S(1)}, u32[]{:S(2)}, u32[]{:S(2)}) collective-permute-start(f32[1,1536]{1,0:T(1,128)S(1)} %get-tuple-element.129), channel_id=1, source_target_pairs={{0,2},{2,4},{4,6},{6,8},{8,10},{10,12},{12,14},{14,16},{16,18},{18... | collective-permute-start | bytes 18440 | tf_op jit(solution)/shard_map/ppermute | solution.py:39
  24.1 8.7 collective-permute-start.13
  26.0 12.2 %collective-permute-start.8 = (f32[1,1536]{1,0:T(1,128)S(1)}, f32[1,1536]{1,0:T(1,128)S(1)}, u32[]{:S(2)}, u32[]{:S(2)}) collective-permute-start(f32[1,1536]{1,0:T(1,128)S(1)} %get-tuple-element.131), channel_id=1, source_target_pairs={{0,2},{2,4},{4,6},{6,8},{8,10},{10,12},{12,14},{14,16},{16,18},{18... | collective-permute-start | bytes 18440 | tf_op jit(solution)/shard_map/ppermute | solution.py:39
  30.9 8.7 collective-permute-start.9
  33.6 38.5 %collective-permute-start.14 = (f32[34,1]{1,0:T(8,128)}, f32[34,1]{1,0:T(8,128)S(1)}, u32[]{:S(2)}, u32[]{:S(2)}) collective-permute-start(f32[34,1]{1,0:T(8,128)} %get-tuple-element.125), channel_id=1, source_target_pairs={{0,1},{2,3},{4,5},{6,7},{8,9},{10,11},{12,13},{14,15},{16,17},{18,... | collective-permute-start | bytes 416 | tf_op jit(solution)/shard_map/ppermute | solution.py:39
  38.2 35.1 %collective-permute-start.15 = (f32[34,1]{1,0:T(8,128)}, f32[34,1]{1,0:T(8,128)}, u32[]{:S(2)}, u32[]{:S(2)}) collective-permute-start(f32[34,1]{1,0:T(8,128)} %get-tuple-element.124), channel_id=1, source_target_pairs={{1,0},{3,2},{5,4},{7,6},{9,8},{11,10},{13,12},{15,14},{17,16},{19,... | collective-permute-start | bytes 416 | tf_op jit(solution)/shard_map/ppermute | solution.py:40
  40.6 8.7 collective-permute-start.2
  46.7 7.6 collective-permute-start.3
  62.8 15.5 %collective-permute-start.4 = (f32[4,1,1536]{2,1,0:T(1,128)S(1)}, f32[4,1,1536]{2,1,0:T(1,128)S(1)}, u32[]{:S(2)}, u32[]{:S(2)}) collective-permute-start(f32[4,1,1536]{2,1,0:T(1,128)S(1)} %get-tuple-element.72), channel_id=1, source_target_pairs={{0,2},{2,4},{4,6},{6,8},{8,10},{10,12},{12,14},{14,16},{16,18},{18... | collective-permute-start | bytes 73736 | tf_op jit(solution)/shard_map/ppermute | solution.py:39
  68.0 10.3 %collective-permute-start.5 = (f32[4,1,1536]{2,1,0:T(1,128)S(1)}, f32[4,1,1536]{2,1,0:T(1,128)S(1)}, u32[]{:S(2)}, u32[]{:S(2)}) collective-permute-start(f32[4,1,1536]{2,1,0:T(1,128)S(1)} %get-tuple-element.73), channel_id=1, source_target_pairs={{2,0},{4,2},{6,4},{8,6},{10,8},{12,10},{14,12},{16,14},{18,16},{20... | collective-permute-start | bytes 73736 | tf_op jit(solution)/shard_map/ppermute | solution.py:40
  70.8 3.5 collective-permute-start.10
  72.1 6.0 collective-permute-start.11
  78.6 3.5 collective-permute-start.6
  80.3 6.7 collective-permute-start.7
  82.0 194.3 %copy-start = (f32[32,1536]{1,0:T(8,128)}, f32[32,1536]{1,0:T(8,128)S(1)}, u32[]{:S(2)}) copy-start(f32[32,1536]{1,0:T(8,128)S(1)} %get-tuple-element.43) | copy-start | bytes 589828
  82.0 194.3 %copy-start.4 = (f32[32,1536]{1,0:T(8,128)}, f32[32,1536]{1,0:T(8,128)S(1)}, u32[]{:S(2)}) copy-start(f32[32,1536]{1,0:T(8,128)S(1)} %get-tuple-element.128) | copy-start | bytes 589828
  91.0 7.9 collective-permute-start.16
  92.9 6.8 collective-permute-start.17
  99.8 6.8 collective-permute-start.18
  101.1 6.6 collective-permute-start.19
  261.8 5.6 collective-permute-start.20
  264.8 3.4 collective-permute-start.21
  268.2 7.0 collective-permute-start.22
  269.5 6.6 collective-permute-start.23
  416.6 5.7 collective-permute-start.24
  419.2 3.9 collective-permute-start.25
  423.2 6.8 collective-permute-start.26
  424.5 6.8 collective-permute-start.27
  503.6 21.7 %copy-start.10 = (f32[4,34,1538]{2,1,0:T(8,128)S(1)}, f32[4,34,1538]{2,1,0:T(8,128)}, u32[]{:S(2)}) copy-start(f32[4,34,1538]{2,1,0:T(8,128)} %concatenate.263) | copy-start | bytes 2510020
  503.6 5.9 collective-permute-start.28
  507.6 5.1 collective-permute-start.29
  513.7 4.7 collective-permute-start.30
  517.0 6.3 collective-permute-start.31
  528.6 23.2 %copy-start.13 = (f32[32,1536]{1,0:T(8,128)}, f32[32,1536]{1,0:T(8,128)S(1)}, u32[]{:S(2)}) copy-start(f32[32,1536]{1,0:T(8,128)S(1)} %fusion.233) | copy-start | bytes 589828
  528.7 6.1 collective-permute-start.32
  532.1 5.5 collective-permute-start.33
  539.0 4.9 collective-permute-start.34
  541.0 7.0 collective-permute-start.35
  555.6 5.2 collective-permute-start.36
  558.9 5.1 collective-permute-start.37
  564.3 3.0 collective-permute-start.38
  565.8 6.7 collective-permute-start.39
  575.6 5.7 collective-permute-start.40
  577.7 4.5 collective-permute-start.41
  582.2 6.8 collective-permute-start.42
  583.5 6.6 collective-permute-start.43
  742.5 5.6 collective-permute-start.44
  745.5 3.4 collective-permute-start.45
  749.0 6.8 collective-permute-start.46
  750.3 6.6 collective-permute-start.47
  897.4 5.7 collective-permute-start.48
  900.1 3.9 collective-permute-start.49
  904.0 6.8 collective-permute-start.50
  905.3 6.8 collective-permute-start.51
  984.4 19.8 %copy-start.24 = (f32[2,32,1536]{2,1,0:T(8,128)}, f32[2,32,1536]{2,1,0:T(8,128)S(1)}, u32[]{:S(2)}) copy-start(f32[2,32,1536]{2,1,0:T(8,128)S(1)} %multiply_add_fusion) | copy-start | bytes 1179652
  984.5 5.9 collective-permute-start.52
  988.4 5.1 collective-permute-start.53
  993.7 4.7 collective-permute-start.54
  997.1 6.3 collective-permute-start.55
  (37 other events, 248.2 us)
where the time goes:
time: 1020 us; the launch traced here: 1010 us
  blocking collectives  693 us (68%)
  starting transfers between devices  158 us (15%)
  other arithmetic  59.7 us (6%)
  waiting for transfers between devices  56.9 us (6%)
  local copies, waits for them, and re-layouts  21.6 us (2%)
  between operations  15.7 us (2%)
    psum x6, blocking collectives, weighted_norm(): return lax.psum(jnp.sum(residual * precond), ('along', 'cross'))  415 us
    psum x4, blocking collectives, solve(): lax.psum(jnp.sum(search * applied), ('along', 'cross'))  279 us
    ppermute x28, starting transfers between devices, padded(): before = lax.ppermute(last, axis, up)  110 us
    ppermute x28, starting transfers between devices, padded(): after = lax.ppermute(leading, axis, down)  48.7 us
    ppermute x28, waiting for transfers between devices, padded(): after = lax.ppermute(leading, axis, down)  45.3 us
  transfers between devices with their start and end apart: 56, of which 24 were waited for; matrix products, arithmetic and copies ran while one was open for 3% of the time, Pallas kernels for 0%

commit v1 on v0

--- a/solution.py
+++ b/solution.py
@@ -130,16 +130,6 @@
     ) / (2.0 * time_step)
 
 
-def apply_operator(search_ext, conduct_ext, layer_thick):
-    middle = shifted(search_ext, 0, 0, 1)
-    conduct_mid = shifted(conduct_ext, 0, 0, 1)
-    result = storage * layer_thick * middle + vertical / layer_thick * (middle - middle[::-1])
-    for step_along, step_cross, weight in link_table:
-        link_coef = weight * 0.5 * (conduct_mid + shifted(conduct_ext, step_along, step_cross, 1))
-        result = result + link_coef * (middle - shifted(search_ext, step_along, step_cross, 1))
-    return result
-
-
 def diagonal_of(conduct_ext, layer_thick):
     conduct_mid = shifted(conduct_ext, 0, 0, 1)
     result = storage * layer_thick + vertical / layer_thick
@@ -155,27 +145,78 @@
     return result
 
 
-def weighted_norm(residual, precond):
-    return lax.psum(jnp.sum(residual * precond), ("along", "cross"))
+def apply_links(values_ext, conduct_ext, layer_thick):
+    middle = shifted(values_ext, 0, 0, 1)
+    conduct_mid = shifted(conduct_ext, 0, 0, 1)
+    result = vertical / layer_thick * middle[::-1]
+    for step_along, step_cross, weight in link_table:
+        link_coef = weight * 0.5 * (conduct_mid + shifted(conduct_ext, step_along, step_cross, 1))
+        result = result + link_coef * shifted(values_ext, step_along, step_cross, 1)
+    return result
+
+
+def summed(partial):
+    count = lax.axis_size("along") * lax.axis_size("cross")
+    spread = jnp.broadcast_to(partial[None, :], (count, partial.shape[0]))
+    return jnp.sum(lax.all_to_all(spread, ("along", "cross"), 0, 0, tiled=True), axis=0)
+
+
+def coefficients(mu):
+    def norm(c):
+        return sum(c[i] * c[j] * mu[i + j] for i in range(len(c)) for j in range(len(c)))
+
+    def energy(c):
+        return sum(
+            c[i] * c[j] * (mu[i + j] - mu[i + j + 1]) for i in range(len(c)) for j in range(len(c))
+        )
+
+    floor = 2e-7 * mu[0]
+    z = [jnp.float32(1.0)]
+    search = [jnp.float32(1.0)]
+    total = [jnp.float32(0.0)] * ITERS
+    norm_now = mu[0]
+    for iteration in range(ITERS):
+        step = norm_now / energy(search)
+        if iteration:
+            step = jnp.where(norm_now > floor, step, 0.0)
+        for i, c in enumerate(search):
+            total[i] = total[i] + step * c
+        if iteration + 1 < ITERS:
+            applied = [
+                (search[i] if i < len(search) else 0.0) - (search[i - 1] if i else 0.0)
+                for i in range(len(search) + 1)
+            ]
+            z = [(z[i] if i < len(z) else 0.0) - step * applied[i] for i in range(len(applied))]
+            norm_next = norm(z)
+            ratio = norm_next / norm_now
+            if iteration:
+                ratio = jnp.where(norm_now > floor, ratio, 0.0)
+            search = [z[i] + (ratio * search[i] if i < len(search) else 0.0) for i in range(len(z))]
+            norm_now = norm_next
+    return total
 
 
 def solve(source, conduct_ext, diagonal, layer_thick):
-    solution = jnp.zeros_like(source)
-    residual = source
-    precond = residual / diagonal
-    search = precond
-    norm_now = weighted_norm(residual, precond)
-    for iteration in range(ITERS):
-        applied = apply_operator(extend(search), conduct_ext, layer_thick)
-        step_size = norm_now / lax.psum(jnp.sum(search * applied), ("along", "cross"))
-        solution = solution + step_size * search
-        residual = residual - step_size * applied
-        if iteration + 1 < ITERS:
-            precond = residual / diagonal
-            norm_next = weighted_norm(residual, precond)
-            search = precond + norm_next / norm_now * search
-            norm_now = norm_next
-    return solution
+    inverse = 1.0 / diagonal
+    y0 = source * inverse
+    n0 = apply_links(extend(y0), conduct_ext, layer_thick)
+    y1 = n0 * inverse
+    n1 = apply_links(extend(y1), conduct_ext, layer_thick)
+    y2 = n1 * inverse
+    n2 = apply_links(extend(y2), conduct_ext, layer_thick)
+    partial = jnp.stack(
+        [
+            jnp.sum(source * y0),
+            jnp.sum(y0 * n0),
+            jnp.sum(y1 * n0),
+            jnp.sum(y1 * n1),
+            jnp.sum(y2 * n1),
+            jnp.sum(y2 * n2),
+        ]
+    )
+    mu = summed(jnp.pad(partial, (0, 2)))
+    c = coefficients([mu[i] for i in range(2 * ITERS)])
+    return c[0] * y0 + c[1] * y1 + c[2] * y2
 
 
 def correct(surface_now, ustar_ext, pressure_ext, conduct_ext, wet_cells):

time: 1020 us -> 415 us (0.41)
  blocking collectives: 693 us -> 78.7 us
  between operations: 15.7 us -> 32.1 us
  local copies, waits for them, and re-layouts: 21.6 us -> 33.7 us
    psum x10 -> x0, blocking collectives: 693 us -> none  [the longest x6 415 us: weighted_norm(): return lax.psum(jnp.sum(residual * precond), ('along', 'cross'))]
    all_to_all x0 -> x2, blocking collectives: none -> 78.7 us  [summed(): lax.all_to_all(spread, ('along', 'cross'), 0, 0, tiled=True)]
    reduce_sum x10 -> x6, other arithmetic: 19.3 us -> 4.79 us  [the longest x2 2.44 us: solve(): jnp.sum(y2 * n2)]
  transfers between devices with their start and end apart: 56 -> 56, of which waited for: 24 -> 23; matrix products, arithmetic and copies ran while one was open for 3% -> 9% of each run, Pallas kernels for 0% -> 0%
where the time goes in v1:
time: 415 us; the launch traced here: 410 us
  starting transfers between devices  161 us (39%)
  blocking collectives  78.7 us (19%)
  other arithmetic  53.2 us (13%)
  waiting for transfers between devices  49.5 us (12%)
  local copies, waits for them, and re-layouts  33.7 us (8%)
  between operations  32.1 us (8%)
    ppermute x28, starting transfers between devices, padded(): before = lax.ppermute(last, axis, up)  116 us
    all_to_all x2, blocking collectives, summed(): lax.all_to_all(spread, ('along', 'cross'), 0, 0, tiled=True)  78.7 us
    ppermute x28, starting transfers between devices, padded(): after = lax.ppermute(leading, axis, down)  45 us
    ppermute x28, waiting for transfers between devices, padded(): after = lax.ppermute(leading, axis, down)  40.1 us
    mul x3, other arithmetic, solve(): y0 = source * inverse  12.2 us
    concatenate x8, local copies, waits for them, and re-layouts, padded(): x = jnp.concatenate([before, x, after], axis=dim)  11 us
    div x1, other arithmetic, diagonal_of(): result = storage * layer_thick + vertical / layer_thick  10.4 us
    ppermute x28, waiting for transfers between devices, padded(): before = lax.ppermute(last, axis, up)  9.38 us
  transfers between devices with their start and end apart: 56, of which 23 were waited for; matrix products, arithmetic and copies ran while one was open for 9% of the time, Pallas kernels for 0%

profile of v1, /device:TPU:1, one launch (start us, length us, event | category | flops | bytes accessed | tf_op | source)
XLA Modules:
  0.0 410.3 jit_solution(1106541076563683932)
XLA Ops:
  3.0 4.6 %collective-permute-start = (f32[5,2,1536]{2,1,0:T(2,128)S(1)}, f32[5,2,1536]{2,1,0:T(2,128)S(1)}, u32[]{:S(2)}, u32[]{:S(2)}) collective-permute-start(f32[5,2,1536]{2,1,0:T(2,128)S(1)} %get-tuple-element.65), channel_id=1, source_target_pairs={{0,2},{2,4},{4,6},{6,8},{8,10},{10,12},{12,14},{14,16},{16,18},{18... | collective-permute-start | bytes 184328 | tf_op jit(solution)/shard_map/ppermute | solution.py:39
  7.6 1.9 collective-permute-start.1
  10.3 10.4 %broadcast_divide_fusion = (f32[32,1536]{1,0:T(8,128)S(1)}, f32[32,1536]{1,0:T(8,128)S(1)}) fusion(f32[]{:T(128)} %bitcast.21, s32[32,1536]{1,0:T(8,128)S(1)} %copy-done.27, f32[]{:T(128)} %bitcast.20, f32[]{:T(128)} %bitcast.19, f32[]{:T(128)} %bitcast.18, f32[]{:T(128)} %bitcast.17, f32[]{:T(128)} %bitcast.16, f32[]{:T(128)} %bitcast.15, f32[]{:T(128)} %bitcast.14, ...), kind=kLoop, calls=%fused_computation.348 | loop fusion | flops 1671168 | bytes 589888 | tf_op jit(solution)/shard_map/div | solution.py:135
  20.7 3.6 collective-permute-start.12
  24.3 1.9 collective-permute-start.13
  26.3 3.6 collective-permute-start.8
  30.1 1.9 collective-permute-start.9
  32.7 4.6 %collective-permute-start.14 = (f32[34,1]{1,0:T(8,128)}, f32[34,1]{1,0:T(8,128)S(1)}, u32[]{:S(2)}, u32[]{:S(2)}) collective-permute-start(f32[34,1]{1,0:T(8,128)} %get-tuple-element.124), channel_id=1, source_target_pairs={{0,1},{2,3},{4,5},{6,7},{8,9},{10,11},{12,13},{14,15},{16,17},{18,... | collective-permute-start | bytes 416 | tf_op jit(solution)/shard_map/ppermute | solution.py:39
  40.1 5.5 %collective-permute-start.2 = (f32[5,36,2]{2,1,0:T(8,128)S(1)}, f32[5,36,2]{2,1,0:T(8,128)S(1)}, u32[]{:S(2)}, u32[]{:S(2)}) collective-permute-start(f32[5,36,2]{2,1,0:T(8,128)S(1)} %get-tuple-element.49), channel_id=1, source_target_pairs={{0,1},{2,3},{4,5},{6,7},{8,9},{10,11},{12,13},{14,15},{16,17},{18,... | collective-permute-start | bytes 4328 | tf_op jit(solution)/shard_map/ppermute | solution.py:39
  46.9 1.7 maximum_maximum_fusion.2
  48.6 4.5 %collective-permute-done.3 = f32[5,36,2]{2,1,0:T(8,128)S(1)} collective-permute-done((f32[5,36,2]{2,1,0:T(8,128)S(1)}, f32[5,36,2]{2,1,0:T(8,128)S(1)}, u32[]{:S(2)}, u32[]{:S(2)}) %collective-permute-start.3) | collective-permute-done | bytes 1472 | tf_op jit(solution)/shard_map/ppermute | solution.py:40
  53.0 2.5 concatenate.256
  55.5 2.1 fusion.161
  61.4 5.1 %collective-permute-start.4 = (f32[4,1,1536]{2,1,0:T(1,128)S(1)}, f32[4,1,1536]{2,1,0:T(1,128)S(1)}, u32[]{:S(2)}, u32[]{:S(2)}) collective-permute-start(f32[4,1,1536]{2,1,0:T(1,128)S(1)} %get-tuple-element.71), channel_id=1, source_target_pairs={{0,2},{2,4},{4,6},{6,8},{8,10},{10,12},{12,14},{14,16},{16,18},{18... | collective-permute-start | bytes 73736 | tf_op jit(solution)/shard_map/ppermute | solution.py:39
  66.5 1.9 collective-permute-start.5
  71.3 4.5 %collective-permute-done.11 = f32[34,1]{1,0:T(8,128)S(1)} collective-permute-done((f32[34,1]{1,0:T(8,128)S(1)}, f32[34,1]{1,0:T(8,128)S(1)}, u32[]{:S(2)}, u32[]{:S(2)}) %collective-permute-start.11) | collective-permute-done | bytes 168 | tf_op jit(solution)/shard_map/ppermute | solution.py:40
  79.3 11.4 %broadcast_multiply_fusion.7 = (f32[32,1536]{1,0:T(8,128)}, f32[32,1536]{1,0:T(8,128)S(1)}, f32[32,1536]{1,0:T(8,128)S(1)}, f32[32,1536]{1,0:T(8,128)S(1)}, f32[...) fusion(f32[]{:T(128)} %bitcast.21, ...), kind=kLoop, calls=%fused_computation.347 | loop fusion | flops 3047424 | bytes 3932224 | tf_op jit(solution)/shard_map/mul | solution.py:201
  91.3 1.7 concatenate.263
  94.6 1.9 collective-permute-start.16
  96.5 5.0 %collective-permute-start.17 = (f32[2,1,1536]{2,1,0:T(1,128)S(1)}, f32[2,1,1536]{2,1,0:T(1,128)S(1)}, u32[]{:S(2)}, u32[]{:S(2)}) collective-permute-start(f32[2,1,1536]{2,1,0:T(1,128)S(1)} %get-tuple-element.117), channel_id=1, source_target_pairs={{0,2},{2,4},{4,6},{6,8},{8,10},{10,12},{12,14},{14,16},{16,18},{18... | collective-permute-start | bytes 36872 | tf_op jit(solution)/shard_map/ppermute | solution.py:39
  103.7 6.4 %collective-permute-start.19 = (f32[2,34,1]{2,1,0:T(8,128)S(1)}, f32[2,34,1]{2,1,0:T(8,128)S(1)}, u32[]{:S(2)}, u32[]{:S(2)}) collective-permute-start(f32[2,34,1]{2,1,0:T(8,128)S(1)} %get-tuple-element.101), channel_id=1, source_target_pairs={{0,1},{2,3},{4,5},{6,7},{8,9},{10,11},{12,13},{14,15},{16,17},{18,... | collective-permute-start | bytes 824 | tf_op jit(solution)/shard_map/ppermute | solution.py:39
  112.0 1.9 collective-permute-start.20
  113.9 5.1 %collective-permute-start.21 = (f32[2,1,1536]{2,1,0:T(1,128)S(1)}, f32[2,1,1536]{2,1,0:T(1,128)S(1)}, u32[]{:S(2)}, u32[]{:S(2)}) collective-permute-start(f32[2,1,1536]{2,1,0:T(1,128)S(1)} %get-tuple-element.115), channel_id=1, source_target_pairs={{0,2},{2,4},{4,6},{6,8},{8,10},{10,12},{12,14},{14,16},{16,18},{18... | collective-permute-start | bytes 36872 | tf_op jit(solution)/shard_map/ppermute | solution.py:39
  121.2 5.5 %collective-permute-start.23 = (f32[2,34,1]{2,1,0:T(8,128)S(1)}, f32[2,34,1]{2,1,0:T(8,128)S(1)}, u32[]{:S(2)}, u32[]{:S(2)}) collective-permute-start(f32[2,34,1]{2,1,0:T(8,128)S(1)} %get-tuple-element.97), channel_id=1, source_target_pairs={{0,1},{2,3},{4,5},{6,7},{8,9},{10,11},{12,13},{14,15},{16,17},{18,... | collective-permute-start | bytes 824 | tf_op jit(solution)/shard_map/ppermute | solution.py:39
  128.6 1.9 collective-permute-start.24
  130.6 5.3 %collective-permute-start.25 = (f32[2,1,1536]{2,1,0:T(1,128)S(1)}, f32[2,1,1536]{2,1,0:T(1,128)S(1)}, u32[]{:S(2)}, u32[]{:S(2)}) collective-permute-start(f32[2,1,1536]{2,1,0:T(1,128)S(1)} %get-tuple-element.113), channel_id=1, source_target_pairs={{0,2},{2,4},{4,6},{6,8},{8,10},{10,12},{12,14},{14,16},{16,18},{18... | collective-permute-start | bytes 36872 | tf_op jit(solution)/shard_map/ppermute | solution.py:39
  138.1 5.5 %collective-permute-start.27 = (f32[2,34,1]{2,1,0:T(8,128)S(1)}, f32[2,34,1]{2,1,0:T(8,128)S(1)}, u32[]{:S(2)}, u32[]{:S(2)}) collective-permute-start(f32[2,34,1]{2,1,0:T(8,128)S(1)} %get-tuple-element.93), channel_id=1, source_target_pairs={{0,1},{2,3},{4,5},{6,7},{8,9},{10,11},{12,13},{14,15},{16,17},{18,... | collective-permute-start | bytes 824 | tf_op jit(solution)/shard_map/ppermute | solution.py:39
  146.2 4.1 stack.48
  150.3 40.8 %all_to_all.12 = f32[128,1,8]{2,1,0:T(1,128)S(1)} all-to-all(f32[128,1,8]{2,1,0:T(1,128)S(1)} %broadcast_in_dim.77), channel_id=1, replica_groups=mesh['along'=64,'cross'=2] {'along','cross'}, dimensions={0} | all-to-all | bytes 8192 | tf_op jit(solution)/shard_map/all_to_all | solution.py:161
  208.2 2.8 collective-permute-start.28
  211.0 1.9 collective-permute-start.29
  212.9 3.2 collective-permute-done.29
  217.1 3.2 collective-permute-start.30
  221.6 5.0 %collective-permute-done.31 = f32[2,36,2]{2,1,0:T(8,128)} collective-permute-done((f32[2,36,2]{2,1,0:T(8,128)S(1)}, f32[2,36,2]{2,1,0:T(8,128)}, u32[]{:S(2)}, u32[]{:S(2)}) %collective-permute-start.31) | collective-permute-done | bytes 608 | tf_op jit(solution)/shard_map/ppermute | solution.py:40
  226.6 2.0 concatenate.284
  228.6 2.2 multiply_reduce_fusion.3
  232.1 3.4 collective-permute-start.32
  235.5 1.9 collective-permute-start.33
  238.2 2.8 collective-permute-done.33
  242.4 1.9 collective-permute-start.34
  245.6 1.7 maximum_maximum_fusion.3
  247.3 4.0 collective-permute-done.35
  251.3 2.5 concatenate.290
  255.2 1.7 maximum_maximum_fusion.1
  259.0 3.9 collective-permute-start.36
  263.0 1.9 collective-permute-start.37
  264.9 3.2 collective-permute-done.37
  271.7 4.7 %collective-permute-done.39 = f32[4,34,1]{2,1,0:T(8,128)} collective-permute-done((f32[4,34,1]{2,1,0:T(8,128)S(1)}, f32[4,34,1]{2,1,0:T(8,128)}, u32[]{:S(2)}, u32[]{:S(2)}) %collective-permute-start.39) | collective-permute-done | bytes 576 | tf_op jit(solution)/shard_map/ppermute | solution.py:40
  279.7 1.9 collective-permute-start.40
  281.6 3.8 collective-permute-start.41
  287.6 5.5 %collective-permute-start.43 = (f32[2,34,1]{2,1,0:T(8,128)S(1)}, f32[2,34,1]{2,1,0:T(8,128)S(1)}, u32[]{:S(2)}, u32[]{:S(2)}) collective-permute-start(f32[2,34,1]{2,1,0:T(8,128)S(1)} %get-tuple-element.89), channel_id=1, source_target_pairs={{0,1},{2,3},{4,5},{6,7},{8,9},{10,11},{12,13},{14,15},{16,17},{18,... | collective-permute-start | bytes 824 | tf_op jit(solution)/shard_map/ppermute | solution.py:39
  295.1 1.9 collective-permute-start.44
  297.0 5.3 %collective-permute-start.45 = (f32[2,1,1536]{2,1,0:T(1,128)S(1)}, f32[2,1,1536]{2,1,0:T(1,128)S(1)}, u32[]{:S(2)}, u32[]{:S(2)}) collective-permute-start(f32[2,1,1536]{2,1,0:T(1,128)S(1)} %get-tuple-element.107), channel_id=1, source_target_pairs={{0,2},{2,4},{4,6},{6,8},{8,10},{10,12},{12,14},{14,16},{16,18},{18... | collective-permute-start | bytes 36872 | tf_op jit(solution)/shard_map/ppermute | solution.py:39
  304.5 5.5 %collective-permute-start.47 = (f32[2,34,1]{2,1,0:T(8,128)S(1)}, f32[2,34,1]{2,1,0:T(8,128)S(1)}, u32[]{:S(2)}, u32[]{:S(2)}) collective-permute-start(f32[2,34,1]{2,1,0:T(8,128)S(1)} %get-tuple-element.85), channel_id=1, source_target_pairs={{0,1},{2,3},{4,5},{6,7},{8,9},{10,11},{12,13},{14,15},{16,17},{18,... | collective-permute-start | bytes 824 | tf_op jit(solution)/shard_map/ppermute | solution.py:39
  312.0 1.9 collective-permute-start.48
  313.9 5.3 %collective-permute-start.49 = (f32[2,1,1536]{2,1,0:T(1,128)S(1)}, f32[2,1,1536]{2,1,0:T(1,128)S(1)}, u32[]{:S(2)}, u32[]{:S(2)}) collective-permute-start(f32[2,1,1536]{2,1,0:T(1,128)S(1)} %get-tuple-element.105), channel_id=1, source_target_pairs={{0,2},{2,4},{4,6},{6,8},{8,10},{10,12},{12,14},{14,16},{16,18},{18... | collective-permute-start | bytes 36872 | tf_op jit(solution)/shard_map/ppermute | solution.py:39
  321.4 5.5 %collective-permute-start.51 = (f32[2,34,1]{2,1,0:T(8,128)S(1)}, f32[2,34,1]{2,1,0:T(8,128)S(1)}, u32[]{:S(2)}, u32[]{:S(2)}) collective-permute-start(f32[2,34,1]{2,1,0:T(8,128)S(1)} %get-tuple-element.81), channel_id=1, source_target_pairs={{0,1},{2,3},{4,5},{6,7},{8,9},{10,11},{12,13},{14,15},{16,17},{18,... | collective-permute-start | bytes 824 | tf_op jit(solution)/shard_map/ppermute | solution.py:39
  329.5 4.1 stack.55
  333.6 37.8 %all_to_all.13 = f32[128,1,8]{2,1,0:T(1,128)S(1)} all-to-all(f32[128,1,8]{2,1,0:T(1,128)S(1)} %broadcast_in_dim.79), channel_id=1, replica_groups=mesh['along'=64,'cross'=2] {'along','cross'}, dimensions={0} | all-to-all | bytes 8192 | tf_op jit(solution)/shard_map/all_to_all | solution.py:161
  388.5 2.8 collective-permute-start.52
  391.3 1.9 collective-permute-start.53
  393.2 3.2 collective-permute-done.53
  396.6 3.2 collective-permute-start.54
  401.1 4.9 %collective-permute-done.55 = f32[2,36,2]{2,1,0:T(8,128)S(1)} collective-permute-done((f32[2,36,2]{2,1,0:T(8,128)S(1)}, f32[2,36,2]{2,1,0:T(8,128)S(1)}, u32[]{:S(2)}, u32[]{:S(2)}) %collective-permute-start.55) | collective-permute-done | bytes 608 | tf_op jit(solution)/shard_map/ppermute | solution.py:40
  (228 shorter events, 72.7 us)
Async XLA Ops:
  2.9 27.0 %copy-start.33 = (s32[8,4]{0,1:T(4,128)S(1)}, s32[8,4]{0,1:T(4,128)}, u32[]{:S(2)}) copy-start(s32[8,4]{0,1:T(4,128)} %param.14) | copy-start | bytes 388
  3.0 35.7 %collective-permute-start = (f32[5,2,1536]{2,1,0:T(2,128)S(1)}, f32[5,2,1536]{2,1,0:T(2,128)S(1)}, u32[]{:S(2)}, u32[]{:S(2)}) collective-permute-start(f32[5,2,1536]{2,1,0:T(2,128)S(1)} %get-tuple-element.65), channel_id=1, source_target_pairs={{0,2},{2,4},{4,6},{6,8},{8,10},{10,12},{12,14},{14,16},{16,18},{18... | collective-permute-start | bytes 184328 | tf_op jit(solution)/shard_map/ppermute | solution.py:39
  7.6 31.1 %collective-permute-start.1 = (f32[5,2,1536]{2,1,0:T(2,128)S(1)}, f32[5,2,1536]{2,1,0:T(2,128)S(1)}, u32[]{:S(2)}, u32[]{:S(2)}) collective-permute-start(f32[5,2,1536]{2,1,0:T(2,128)S(1)} %get-tuple-element.66), channel_id=1, source_target_pairs={{2,0},{4,2},{6,4},{8,6},{10,8},{12,10},{14,12},{16,14},{18,16},{20... | collective-permute-start | bytes 184328 | tf_op jit(solution)/shard_map/ppermute | solution.py:40
  20.7 39.8 %copy-start.4 = (f32[32,1536]{1,0:T(8,128)}, f32[32,1536]{1,0:T(8,128)S(1)}, u32[]{:S(2)}) copy-start(f32[32,1536]{1,0:T(8,128)S(1)} %get-tuple-element.128) | copy-start | bytes 589828
  20.7 9.4 %collective-permute-start.12 = (f32[1,1536]{1,0:T(1,128)S(1)}, f32[1,1536]{1,0:T(1,128)S(1)}, u32[]{:S(2)}, u32[]{:S(2)}) collective-permute-start(f32[1,1536]{1,0:T(1,128)S(1)} %get-tuple-element.129), channel_id=1, source_target_pairs={{0,2},{2,4},{4,6},{6,8},{8,10},{10,12},{12,14},{14,16},{16,18},{18... | collective-permute-start | bytes 18440 | tf_op jit(solution)/shard_map/ppermute | solution.py:39
  24.3 7.6 %collective-permute-start.13 = (f32[1,1536]{1,0:T(1,128)S(1)}, f32[1,1536]{1,0:T(1,128)S(1)}, u32[]{:S(2)}, u32[]{:S(2)}) collective-permute-start(f32[1,1536]{1,0:T(1,128)S(1)} %get-tuple-element.130), channel_id=1, source_target_pairs={{2,0},{4,2},{6,4},{8,6},{10,8},{12,10},{14,12},{16,14},{18,16},{20... | collective-permute-start | bytes 18440 | tf_op jit(solution)/shard_map/ppermute | solution.py:40
  26.3 11.1 %collective-permute-start.8 = (f32[1,1536]{1,0:T(1,128)S(1)}, f32[1,1536]{1,0:T(1,128)S(1)}, u32[]{:S(2)}, u32[]{:S(2)}) collective-permute-start(f32[1,1536]{1,0:T(1,128)S(1)} %get-tuple-element.131), channel_id=1, source_target_pairs={{0,2},{2,4},{4,6},{6,8},{8,10},{10,12},{12,14},{14,16},{16,18},{18... | collective-permute-start | bytes 18440 | tf_op jit(solution)/shard_map/ppermute | solution.py:39
  30.1 8.6 %collective-permute-start.9 = (f32[1,1536]{1,0:T(1,128)S(1)}, f32[1,1536]{1,0:T(1,128)S(1)}, u32[]{:S(2)}, u32[]{:S(2)}) collective-permute-start(f32[1,1536]{1,0:T(1,128)S(1)} %get-tuple-element.132), channel_id=1, source_target_pairs={{2,0},{4,2},{6,4},{8,6},{10,8},{12,10},{14,12},{16,14},{18,16},{20... | collective-permute-start | bytes 18440 | tf_op jit(solution)/shard_map/ppermute | solution.py:40
  32.7 37.1 %collective-permute-start.14 = (f32[34,1]{1,0:T(8,128)}, f32[34,1]{1,0:T(8,128)S(1)}, u32[]{:S(2)}, u32[]{:S(2)}) collective-permute-start(f32[34,1]{1,0:T(8,128)} %get-tuple-element.124), channel_id=1, source_target_pairs={{0,1},{2,3},{4,5},{6,7},{8,9},{10,11},{12,13},{14,15},{16,17},{18,... | collective-permute-start | bytes 416 | tf_op jit(solution)/shard_map/ppermute | solution.py:39
  37.4 33.7 %collective-permute-start.15 = (f32[34,1]{1,0:T(8,128)}, f32[34,1]{1,0:T(8,128)S(1)}, u32[]{:S(2)}, u32[]{:S(2)}) collective-permute-start(f32[34,1]{1,0:T(8,128)} %get-tuple-element.123), channel_id=1, source_target_pairs={{1,0},{3,2},{5,4},{7,6},{9,8},{11,10},{13,12},{15,14},{17,16},{19,... | collective-permute-start | bytes 416 | tf_op jit(solution)/shard_map/ppermute | solution.py:40
  40.1 8.5 %collective-permute-start.2 = (f32[5,36,2]{2,1,0:T(8,128)S(1)}, f32[5,36,2]{2,1,0:T(8,128)S(1)}, u32[]{:S(2)}, u32[]{:S(2)}) collective-permute-start(f32[5,36,2]{2,1,0:T(8,128)S(1)} %get-tuple-element.49), channel_id=1, source_target_pairs={{0,1},{2,3},{4,5},{6,7},{8,9},{10,11},{12,13},{14,15},{16,17},{18,... | collective-permute-start | bytes 4328 | tf_op jit(solution)/shard_map/ppermute | solution.py:39
  45.6 7.5 %collective-permute-start.3 = (f32[5,36,2]{2,1,0:T(8,128)S(1)}, f32[5,36,2]{2,1,0:T(8,128)S(1)}, u32[]{:S(2)}, u32[]{:S(2)}) collective-permute-start(f32[5,36,2]{2,1,0:T(8,128)S(1)} %get-tuple-element.50), channel_id=1, source_target_pairs={{1,0},{3,2},{5,4},{7,6},{9,8},{11,10},{13,12},{15,14},{17,16},{19,... | collective-permute-start | bytes 4328 | tf_op jit(solution)/shard_map/ppermute | solution.py:40
  61.4 14.6 %collective-permute-start.4 = (f32[4,1,1536]{2,1,0:T(1,128)S(1)}, f32[4,1,1536]{2,1,0:T(1,128)S(1)}, u32[]{:S(2)}, u32[]{:S(2)}) collective-permute-start(f32[4,1,1536]{2,1,0:T(1,128)S(1)} %get-tuple-element.71), channel_id=1, source_target_pairs={{0,2},{2,4},{4,6},{6,8},{8,10},{10,12},{12,14},{14,16},{16,18},{18... | collective-permute-start | bytes 73736 | tf_op jit(solution)/shard_map/ppermute | solution.py:39
  66.5 9.6 %collective-permute-start.5 = (f32[4,1,1536]{2,1,0:T(1,128)S(1)}, f32[4,1,1536]{2,1,0:T(1,128)S(1)}, u32[]{:S(2)}, u32[]{:S(2)}) collective-permute-start(f32[4,1,1536]{2,1,0:T(1,128)S(1)} %get-tuple-element.72), channel_id=1, source_target_pairs={{2,0},{4,2},{6,4},{8,6},{10,8},{12,10},{14,12},{16,14},{18,16},{20... | collective-permute-start | bytes 73736 | tf_op jit(solution)/shard_map/ppermute | solution.py:40
  68.5 2.8 collective-permute-start.10
  69.8 6.0 %collective-permute-start.11 = (f32[34,1]{1,0:T(8,128)S(1)}, f32[34,1]{1,0:T(8,128)S(1)}, u32[]{:S(2)}, u32[]{:S(2)}) collective-permute-start(f32[34,1]{1,0:T(8,128)S(1)} %get-tuple-element.125), channel_id=1, source_target_pairs={{1,0},{3,2},{5,4},{7,6},{9,8},{11,10},{13,12},{15,14},{17,16},{19,... | collective-permute-start | bytes 416 | tf_op jit(solution)/shard_map/ppermute | solution.py:40
  76.3 14.4 %collective-permute-start.6 = (f32[4,34,1]{2,1,0:T(8,128)S(1)}, f32[4,34,1]{2,1,0:T(8,128)S(1)}, u32[]{:S(2)}, u32[]{:S(2)}) collective-permute-start(f32[4,34,1]{2,1,0:T(8,128)S(1)} %get-tuple-element.62), channel_id=1, source_target_pairs={{0,1},{2,3},{4,5},{6,7},{8,9},{10,11},{12,13},{14,15},{16,17},{18,... | collective-permute-start | bytes 1640 | tf_op jit(solution)/shard_map/ppermute | solution.py:39
  78.0 13.3 %collective-permute-start.7 = (f32[4,34,1]{2,1,0:T(8,128)S(1)}, f32[4,34,1]{2,1,0:T(8,128)}, u32[]{:S(2)}, u32[]{:S(2)}) collective-permute-start(f32[4,34,1]{2,1,0:T(8,128)S(1)} %get-tuple-element.61), channel_id=1, source_target_pairs={{1,0},{3,2},{5,4},{7,6},{9,8},{11,10},{13,12},{15,14},{17,16},{19,... | collective-permute-start | bytes 1640 | tf_op jit(solution)/shard_map/ppermute | solution.py:40
  94.6 6.9 %collective-permute-start.16 = (f32[2,1,1536]{2,1,0:T(1,128)S(1)}, f32[2,1,1536]{2,1,0:T(1,128)S(1)}, u32[]{:S(2)}, u32[]{:S(2)}) collective-permute-start(f32[2,1,1536]{2,1,0:T(1,128)S(1)} %get-tuple-element.118), channel_id=1, source_target_pairs={{2,0},{4,2},{6,4},{8,6},{10,8},{12,10},{14,12},{16,14},{18,16},{20... | collective-permute-start | bytes 36872 | tf_op jit(solution)/shard_map/ppermute | solution.py:40
  96.5 5.8 %collective-permute-start.17 = (f32[2,1,1536]{2,1,0:T(1,128)S(1)}, f32[2,1,1536]{2,1,0:T(1,128)S(1)}, u32[]{:S(2)}, u32[]{:S(2)}) collective-permute-start(f32[2,1,1536]{2,1,0:T(1,128)S(1)} %get-tuple-element.117), channel_id=1, source_target_pairs={{0,2},{2,4},{4,6},{6,8},{8,10},{10,12},{12,14},{14,16},{16,18},{18... | collective-permute-start | bytes 36872 | tf_op jit(solution)/shard_map/ppermute | solution.py:39
  102.4 7.7 %collective-permute-start.18 = (f32[2,34,1]{2,1,0:T(8,128)S(1)}, f32[2,34,1]{2,1,0:T(8,128)S(1)}, u32[]{:S(2)}, u32[]{:S(2)}) collective-permute-start(f32[2,34,1]{2,1,0:T(8,128)S(1)} %get-tuple-element.102), channel_id=1, source_target_pairs={{1,0},{3,2},{5,4},{7,6},{9,8},{11,10},{13,12},{15,14},{17,16},{19,... | collective-permute-start | bytes 824 | tf_op jit(solution)/shard_map/ppermute | solution.py:40
  103.7 7.5 %collective-permute-start.19 = (f32[2,34,1]{2,1,0:T(8,128)S(1)}, f32[2,34,1]{2,1,0:T(8,128)S(1)}, u32[]{:S(2)}, u32[]{:S(2)}) collective-permute-start(f32[2,34,1]{2,1,0:T(8,128)S(1)} %get-tuple-element.101), channel_id=1, source_target_pairs={{0,1},{2,3},{4,5},{6,7},{8,9},{10,11},{12,13},{14,15},{16,17},{18,... | collective-permute-start | bytes 824 | tf_op jit(solution)/shard_map/ppermute | solution.py:39
  112.0 7.0 %collective-permute-start.20 = (f32[2,1,1536]{2,1,0:T(1,128)S(1)}, f32[2,1,1536]{2,1,0:T(1,128)S(1)}, u32[]{:S(2)}, u32[]{:S(2)}) collective-permute-start(f32[2,1,1536]{2,1,0:T(1,128)S(1)} %get-tuple-element.116), channel_id=1, source_target_pairs={{2,0},{4,2},{6,4},{8,6},{10,8},{12,10},{14,12},{16,14},{18,16},{20... | collective-permute-start | bytes 36872 | tf_op jit(solution)/shard_map/ppermute | solution.py:40
  113.9 5.9 %collective-permute-start.21 = (f32[2,1,1536]{2,1,0:T(1,128)S(1)}, f32[2,1,1536]{2,1,0:T(1,128)S(1)}, u32[]{:S(2)}, u32[]{:S(2)}) collective-permute-start(f32[2,1,1536]{2,1,0:T(1,128)S(1)} %get-tuple-element.115), channel_id=1, source_target_pairs={{0,2},{2,4},{4,6},{6,8},{8,10},{10,12},{12,14},{14,16},{16,18},{18... | collective-permute-start | bytes 36872 | tf_op jit(solution)/shard_map/ppermute | solution.py:39
  119.9 6.8 %collective-permute-start.22 = (f32[2,34,1]{2,1,0:T(8,128)S(1)}, f32[2,34,1]{2,1,0:T(8,128)S(1)}, u32[]{:S(2)}, u32[]{:S(2)}) collective-permute-start(f32[2,34,1]{2,1,0:T(8,128)S(1)} %get-tuple-element.98), channel_id=1, source_target_pairs={{1,0},{3,2},{5,4},{7,6},{9,8},{11,10},{13,12},{15,14},{17,16},{19,... | collective-permute-start | bytes 824 | tf_op jit(solution)/shard_map/ppermute | solution.py:40
  121.2 6.6 %collective-permute-start.23 = (f32[2,34,1]{2,1,0:T(8,128)S(1)}, f32[2,34,1]{2,1,0:T(8,128)S(1)}, u32[]{:S(2)}, u32[]{:S(2)}) collective-permute-start(f32[2,34,1]{2,1,0:T(8,128)S(1)} %get-tuple-element.97), channel_id=1, source_target_pairs={{0,1},{2,3},{4,5},{6,7},{8,9},{10,11},{12,13},{14,15},{16,17},{18,... | collective-permute-start | bytes 824 | tf_op jit(solution)/shard_map/ppermute | solution.py:39
  128.6 16.0 %copy-start.22 = (f32[2,32,1536]{2,1,0:T(8,128)}, f32[2,32,1536]{2,1,0:T(8,128)S(1)}, u32[]{:S(2)}) copy-start(f32[2,32,1536]{2,1,0:T(8,128)S(1)} %get-tuple-element.28) | copy-start | bytes 1179652
  128.6 7.3 %collective-permute-start.24 = (f32[2,1,1536]{2,1,0:T(1,128)S(1)}, f32[2,1,1536]{2,1,0:T(1,128)S(1)}, u32[]{:S(2)}, u32[]{:S(2)}) collective-permute-start(f32[2,1,1536]{2,1,0:T(1,128)S(1)} %get-tuple-element.114), channel_id=1, source_target_pairs={{2,0},{4,2},{6,4},{8,6},{10,8},{12,10},{14,12},{16,14},{18,16},{20... | collective-permute-start | bytes 36872 | tf_op jit(solution)/shard_map/ppermute | solution.py:40
  130.6 6.1 %collective-permute-start.25 = (f32[2,1,1536]{2,1,0:T(1,128)S(1)}, f32[2,1,1536]{2,1,0:T(1,128)S(1)}, u32[]{:S(2)}, u32[]{:S(2)}) collective-permute-start(f32[2,1,1536]{2,1,0:T(1,128)S(1)} %get-tuple-element.113), channel_id=1, source_target_pairs={{0,2},{2,4},{4,6},{6,8},{8,10},{10,12},{12,14},{14,16},{16,18},{18... | collective-permute-start | bytes 36872 | tf_op jit(solution)/shard_map/ppermute | solution.py:39
  136.8 7.8 %collective-permute-start.26 = (f32[2,34,1]{2,1,0:T(8,128)S(1)}, f32[2,34,1]{2,1,0:T(8,128)S(1)}, u32[]{:S(2)}, u32[]{:S(2)}) collective-permute-start(f32[2,34,1]{2,1,0:T(8,128)S(1)} %get-tuple-element.94), channel_id=1, source_target_pairs={{1,0},{3,2},{5,4},{7,6},{9,8},{11,10},{13,12},{15,14},{17,16},{19,... | collective-permute-start | bytes 824 | tf_op jit(solution)/shard_map/ppermute | solution.py:40
  138.1 6.6 %collective-permute-start.27 = (f32[2,34,1]{2,1,0:T(8,128)S(1)}, f32[2,34,1]{2,1,0:T(8,128)S(1)}, u32[]{:S(2)}, u32[]{:S(2)}) collective-permute-start(f32[2,34,1]{2,1,0:T(8,128)S(1)} %get-tuple-element.93), channel_id=1, source_target_pairs={{0,1},{2,3},{4,5},{6,7},{8,9},{10,11},{12,13},{14,15},{16,17},{18,... | collective-permute-start | bytes 824 | tf_op jit(solution)/shard_map/ppermute | solution.py:39
  208.1 20.5 %copy-start.3 = (f32[4,34,1538]{2,1,0:T(8,128)S(1)}, f32[4,34,1538]{2,1,0:T(8,128)}, u32[]{:S(2)}) copy-start(f32[4,34,1538]{2,1,0:T(8,128)} %copy-done.2) | copy-start | bytes 2510020
  208.2 4.7 %collective-permute-start.28 = (f32[2,2,1536]{2,1,0:T(2,128)S(1)}, f32[2,2,1536]{2,1,0:T(2,128)S(1)}, u32[]{:S(2)}, u32[]{:S(2)}) collective-permute-start(f32[2,2,1536]{2,1,0:T(2,128)S(1)} %get-tuple-element.111), channel_id=1, source_target_pairs={{0,2},{2,4},{4,6},{6,8},{8,10},{10,12},{12,14},{14,16},{16,18},{18... | collective-permute-start | bytes 73736 | tf_op jit(solution)/shard_map/ppermute | solution.py:39
  211.0 5.1 %collective-permute-start.29 = (f32[2,2,1536]{2,1,0:T(2,128)S(1)}, f32[2,2,1536]{2,1,0:T(2,128)S(1)}, u32[]{:S(2)}, u32[]{:S(2)}) collective-permute-start(f32[2,2,1536]{2,1,0:T(2,128)S(1)} %get-tuple-element.112), channel_id=1, source_target_pairs={{2,0},{4,2},{6,4},{8,6},{10,8},{12,10},{14,12},{16,14},{18,16},{20... | collective-permute-start | bytes 73736 | tf_op jit(solution)/shard_map/ppermute | solution.py:40
  217.1 4.5 %collective-permute-start.30 = (f32[2,36,2]{2,1,0:T(8,128)S(1)}, f32[2,36,2]{2,1,0:T(8,128)S(1)}, u32[]{:S(2)}, u32[]{:S(2)}) collective-permute-start(f32[2,36,2]{2,1,0:T(8,128)S(1)} %get-tuple-element.78), channel_id=1, source_target_pairs={{0,1},{2,3},{4,5},{6,7},{8,9},{10,11},{12,13},{14,15},{16,17},{18,... | collective-permute-start | bytes 1736 | tf_op jit(solution)/shard_map/ppermute | solution.py:39
  220.2 6.4 %collective-permute-start.31 = (f32[2,36,2]{2,1,0:T(8,128)S(1)}, f32[2,36,2]{2,1,0:T(8,128)}, u32[]{:S(2)}, u32[]{:S(2)}) collective-permute-start(f32[2,36,2]{2,1,0:T(8,128)S(1)} %get-tuple-element.77), channel_id=1, source_target_pairs={{1,0},{3,2},{5,4},{7,6},{9,8},{11,10},{13,12},{15,14},{17,16},{19,... | collective-permute-start | bytes 1736 | tf_op jit(solution)/shard_map/ppermute | solution.py:40
  232.0 23.2 %copy-start.6 = (f32[32,1536]{1,0:T(8,128)}, f32[32,1536]{1,0:T(8,128)S(1)}, u32[]{:S(2)}) copy-start(f32[32,1536]{1,0:T(8,128)S(1)} %fusion.171) | copy-start | bytes 589828
  232.1 6.1 %collective-permute-start.32 = (f32[5,2,1536]{2,1,0:T(2,128)S(1)}, f32[5,2,1536]{2,1,0:T(2,128)S(1)}, u32[]{:S(2)}, u32[]{:S(2)}) collective-permute-start(f32[5,2,1536]{2,1,0:T(2,128)S(1)} %get-tuple-element.59), channel_id=1, source_target_pairs={{0,2},{2,4},{4,6},{6,8},{8,10},{10,12},{12,14},{14,16},{16,18},{18... | collective-permute-start | bytes 184328 | tf_op jit(solution)/shard_map/ppermute | solution.py:39
  235.5 5.5 %collective-permute-start.33 = (f32[5,2,1536]{2,1,0:T(2,128)S(1)}, f32[5,2,1536]{2,1,0:T(2,128)S(1)}, u32[]{:S(2)}, u32[]{:S(2)}) collective-permute-start(f32[5,2,1536]{2,1,0:T(2,128)S(1)} %get-tuple-element.60), channel_id=1, source_target_pairs={{2,0},{4,2},{6,4},{8,6},{10,8},{12,10},{14,12},{16,14},{18,16},{20... | collective-permute-start | bytes 184328 | tf_op jit(solution)/shard_map/ppermute | solution.py:40
  242.4 4.9 %collective-permute-start.34 = (f32[5,36,2]{2,1,0:T(8,128)S(1)}, f32[5,36,2]{2,1,0:T(8,128)}, u32[]{:S(2)}, u32[]{:S(2)}) collective-permute-start(f32[5,36,2]{2,1,0:T(8,128)S(1)} %get-tuple-element.47), channel_id=1, source_target_pairs={{0,1},{2,3},{4,5},{6,7},{8,9},{10,11},{12,13},{14,15},{16,17},{18,... | collective-permute-start | bytes 4328 | tf_op jit(solution)/shard_map/ppermute | solution.py:39
  244.3 7.0 %collective-permute-start.35 = (f32[5,36,2]{2,1,0:T(8,128)S(1)}, f32[5,36,2]{2,1,0:T(8,128)}, u32[]{:S(2)}, u32[]{:S(2)}) collective-permute-start(f32[5,36,2]{2,1,0:T(8,128)S(1)} %get-tuple-element.48), channel_id=1, source_target_pairs={{1,0},{3,2},{5,4},{7,6},{9,8},{11,10},{13,12},{15,14},{17,16},{19,... | collective-permute-start | bytes 4328 | tf_op jit(solution)/shard_map/ppermute | solution.py:40
  259.0 5.9 %collective-permute-start.36 = (f32[4,1,1536]{2,1,0:T(1,128)S(1)}, f32[4,1,1536]{2,1,0:T(1,128)S(1)}, u32[]{:S(2)}, u32[]{:S(2)}) collective-permute-start(f32[4,1,1536]{2,1,0:T(1,128)S(1)} %get-tuple-element.67), channel_id=1, source_target_pairs={{0,2},{2,4},{4,6},{6,8},{8,10},{10,12},{12,14},{14,16},{16,18},{18... | collective-permute-start | bytes 73736 | tf_op jit(solution)/shard_map/ppermute | solution.py:39
  263.0 5.1 %collective-permute-start.37 = (f32[4,1,1536]{2,1,0:T(1,128)S(1)}, f32[4,1,1536]{2,1,0:T(1,128)S(1)}, u32[]{:S(2)}, u32[]{:S(2)}) collective-permute-start(f32[4,1,1536]{2,1,0:T(1,128)S(1)} %get-tuple-element.68), channel_id=1, source_target_pairs={{2,0},{4,2},{6,4},{8,6},{10,8},{12,10},{14,12},{16,14},{18,16},{20... | collective-permute-start | bytes 73736 | tf_op jit(solution)/shard_map/ppermute | solution.py:40
  268.3 2.8 collective-permute-start.38
  269.6 6.8 %collective-permute-start.39 = (f32[4,34,1]{2,1,0:T(8,128)S(1)}, f32[4,34,1]{2,1,0:T(8,128)}, u32[]{:S(2)}, u32[]{:S(2)}) collective-permute-start(f32[4,34,1]{2,1,0:T(8,128)S(1)} %get-tuple-element.55), channel_id=1, source_target_pairs={{1,0},{3,2},{5,4},{7,6},{9,8},{11,10},{13,12},{15,14},{17,16},{19,... | collective-permute-start | bytes 1640 | tf_op jit(solution)/shard_map/ppermute | solution.py:40
  279.7 5.8 %collective-permute-start.40 = (f32[2,1,1536]{2,1,0:T(1,128)S(1)}, f32[2,1,1536]{2,1,0:T(1,128)S(1)}, u32[]{:S(2)}, u32[]{:S(2)}) collective-permute-start(f32[2,1,1536]{2,1,0:T(1,128)S(1)} %get-tuple-element.110), channel_id=1, source_target_pairs={{2,0},{4,2},{6,4},{8,6},{10,8},{12,10},{14,12},{16,14},{18,16},{20... | collective-permute-start | bytes 36872 | tf_op jit(solution)/shard_map/ppermute | solution.py:40
  281.6 4.6 %collective-permute-start.41 = (f32[2,1,1536]{2,1,0:T(1,128)S(1)}, f32[2,1,1536]{2,1,0:T(1,128)S(1)}, u32[]{:S(2)}, u32[]{:S(2)}) collective-permute-start(f32[2,1,1536]{2,1,0:T(1,128)S(1)} %get-tuple-element.109), channel_id=1, source_target_pairs={{0,2},{2,4},{4,6},{6,8},{8,10},{10,12},{12,14},{14,16},{16,18},{18... | collective-permute-start | bytes 36872 | tf_op jit(solution)/shard_map/ppermute | solution.py:39
  286.3 6.8 %collective-permute-start.42 = (f32[2,34,1]{2,1,0:T(8,128)S(1)}, f32[2,34,1]{2,1,0:T(8,128)S(1)}, u32[]{:S(2)}, u32[]{:S(2)}) collective-permute-start(f32[2,34,1]{2,1,0:T(8,128)S(1)} %get-tuple-element.90), channel_id=1, source_target_pairs={{1,0},{3,2},{5,4},{7,6},{9,8},{11,10},{13,12},{15,14},{17,16},{19,... | collective-permute-start | bytes 824 | tf_op jit(solution)/shard_map/ppermute | solution.py:40
  287.6 6.6 %collective-permute-start.43 = (f32[2,34,1]{2,1,0:T(8,128)S(1)}, f32[2,34,1]{2,1,0:T(8,128)S(1)}, u32[]{:S(2)}, u32[]{:S(2)}) collective-permute-start(f32[2,34,1]{2,1,0:T(8,128)S(1)} %get-tuple-element.89), channel_id=1, source_target_pairs={{0,1},{2,3},{4,5},{6,7},{8,9},{10,11},{12,13},{14,15},{16,17},{18,... | collective-permute-start | bytes 824 | tf_op jit(solution)/shard_map/ppermute | solution.py:39
  295.1 7.3 %collective-permute-start.44 = (f32[2,1,1536]{2,1,0:T(1,128)S(1)}, f32[2,1,1536]{2,1,0:T(1,128)S(1)}, u32[]{:S(2)}, u32[]{:S(2)}) collective-permute-start(f32[2,1,1536]{2,1,0:T(1,128)S(1)} %get-tuple-element.108), channel_id=1, source_target_pairs={{2,0},{4,2},{6,4},{8,6},{10,8},{12,10},{14,12},{16,14},{18,16},{20... | collective-permute-start | bytes 36872 | tf_op jit(solution)/shard_map/ppermute | solution.py:40
  297.0 6.1 %collective-permute-start.45 = (f32[2,1,1536]{2,1,0:T(1,128)S(1)}, f32[2,1,1536]{2,1,0:T(1,128)S(1)}, u32[]{:S(2)}, u32[]{:S(2)}) collective-permute-start(f32[2,1,1536]{2,1,0:T(1,128)S(1)} %get-tuple-element.107), channel_id=1, source_target_pairs={{0,2},{2,4},{4,6},{6,8},{8,10},{10,12},{12,14},{14,16},{16,18},{18... | collective-permute-start | bytes 36872 | tf_op jit(solution)/shard_map/ppermute | solution.py:39
  303.2 6.8 %collective-permute-start.46 = (f32[2,34,1]{2,1,0:T(8,128)S(1)}, f32[2,34,1]{2,1,0:T(8,128)S(1)}, u32[]{:S(2)}, u32[]{:S(2)}) collective-permute-start(f32[2,34,1]{2,1,0:T(8,128)S(1)} %get-tuple-element.86), channel_id=1, source_target_pairs={{1,0},{3,2},{5,4},{7,6},{9,8},{11,10},{13,12},{15,14},{17,16},{19,... | collective-permute-start | bytes 824 | tf_op jit(solution)/shard_map/ppermute | solution.py:40
  304.5 6.6 %collective-permute-start.47 = (f32[2,34,1]{2,1,0:T(8,128)S(1)}, f32[2,34,1]{2,1,0:T(8,128)S(1)}, u32[]{:S(2)}, u32[]{:S(2)}) collective-permute-start(f32[2,34,1]{2,1,0:T(8,128)S(1)} %get-tuple-element.85), channel_id=1, source_target_pairs={{0,1},{2,3},{4,5},{6,7},{8,9},{10,11},{12,13},{14,15},{16,17},{18,... | collective-permute-start | bytes 824 | tf_op jit(solution)/shard_map/ppermute | solution.py:39
  311.9 16.0 %copy-start.21 = (f32[2,32,1536]{2,1,0:T(8,128)}, f32[2,32,1536]{2,1,0:T(8,128)S(1)}, u32[]{:S(2)}) copy-start(f32[2,32,1536]{2,1,0:T(8,128)S(1)} %get-tuple-element.20) | copy-start | bytes 1179652
  312.0 7.3 %collective-permute-start.48 = (f32[2,1,1536]{2,1,0:T(1,128)S(1)}, f32[2,1,1536]{2,1,0:T(1,128)S(1)}, u32[]{:S(2)}, u32[]{:S(2)}) collective-permute-start(f32[2,1,1536]{2,1,0:T(1,128)S(1)} %get-tuple-element.106), channel_id=1, source_target_pairs={{2,0},{4,2},{6,4},{8,6},{10,8},{12,10},{14,12},{16,14},{18,16},{20... | collective-permute-start | bytes 36872 | tf_op jit(solution)/shard_map/ppermute | solution.py:40
  313.9 6.1 %collective-permute-start.49 = (f32[2,1,1536]{2,1,0:T(1,128)S(1)}, f32[2,1,1536]{2,1,0:T(1,128)S(1)}, u32[]{:S(2)}, u32[]{:S(2)}) collective-permute-start(f32[2,1,1536]{2,1,0:T(1,128)S(1)} %get-tuple-element.105), channel_id=1, source_target_pairs={{0,2},{2,4},{4,6},{6,8},{8,10},{10,12},{12,14},{14,16},{16,18},{18... | collective-permute-start | bytes 36872 | tf_op jit(solution)/shard_map/ppermute | solution.py:39
  320.1 7.8 %collective-permute-start.50 = (f32[2,34,1]{2,1,0:T(8,128)S(1)}, f32[2,34,1]{2,1,0:T(8,128)S(1)}, u32[]{:S(2)}, u32[]{:S(2)}) collective-permute-start(f32[2,34,1]{2,1,0:T(8,128)S(1)} %get-tuple-element.82), channel_id=1, source_target_pairs={{1,0},{3,2},{5,4},{7,6},{9,8},{11,10},{13,12},{15,14},{17,16},{19,... | collective-permute-start | bytes 824 | tf_op jit(solution)/shard_map/ppermute | solution.py:40
  321.4 6.6 %collective-permute-start.51 = (f32[2,34,1]{2,1,0:T(8,128)S(1)}, f32[2,34,1]{2,1,0:T(8,128)S(1)}, u32[]{:S(2)}, u32[]{:S(2)}) collective-permute-start(f32[2,34,1]{2,1,0:T(8,128)S(1)} %get-tuple-element.81), channel_id=1, source_target_pairs={{0,1},{2,3},{4,5},{6,7},{8,9},{10,11},{12,13},{14,15},{16,17},{18,... | collective-permute-start | bytes 824 | tf_op jit(solution)/shard_map/ppermute | solution.py:39
  388.4 12.6 %copy-start.18 = (f32[2,32,1536]{2,1,0:T(8,128)}, f32[2,32,1536]{2,1,0:T(8,128)S(1)}, u32[]{:S(2)}) copy-start(f32[2,32,1536]{2,1,0:T(8,128)S(1)} %multiply_add_fusion) | copy-start | bytes 1179652
  388.4 17.9 %copy-start.1 = (f32[4,34,1538]{2,1,0:T(8,128)S(1)}, f32[4,34,1538]{2,1,0:T(8,128)}, u32[]{:S(2)}) copy-start(f32[4,34,1538]{2,1,0:T(8,128)} %copy-done) | copy-start | bytes 2510020
  388.5 4.7 %collective-permute-start.52 = (f32[2,2,1536]{2,1,0:T(2,128)S(1)}, f32[2,2,1536]{2,1,0:T(2,128)S(1)}, u32[]{:S(2)}, u32[]{:S(2)}) collective-permute-start(f32[2,2,1536]{2,1,0:T(2,128)S(1)} %get-tuple-element.103), channel_id=1, source_target_pairs={{0,2},{2,4},{4,6},{6,8},{8,10},{10,12},{12,14},{14,16},{16,18},{18... | collective-permute-start | bytes 73736 | tf_op jit(solution)/shard_map/ppermute | solution.py:39
  391.3 5.1 %collective-permute-start.53 = (f32[2,2,1536]{2,1,0:T(2,128)S(1)}, f32[2,2,1536]{2,1,0:T(2,128)S(1)}, u32[]{:S(2)}, u32[]{:S(2)}) collective-permute-start(f32[2,2,1536]{2,1,0:T(2,128)S(1)} %get-tuple-element.104), channel_id=1, source_target_pairs={{2,0},{4,2},{6,4},{8,6},{10,8},{12,10},{14,12},{16,14},{18,16},{20... | collective-permute-start | bytes 73736 | tf_op jit(solution)/shard_map/ppermute | solution.py:40
  396.6 4.5 %collective-permute-start.54 = (f32[2,36,2]{2,1,0:T(8,128)S(1)}, f32[2,36,2]{2,1,0:T(8,128)S(1)}, u32[]{:S(2)}, u32[]{:S(2)}) collective-permute-start(f32[2,36,2]{2,1,0:T(8,128)S(1)} %get-tuple-element.76), channel_id=1, source_target_pairs={{0,1},{2,3},{4,5},{6,7},{8,9},{10,11},{12,13},{14,15},{16,17},{18,... | collective-permute-start | bytes 1736 | tf_op jit(solution)/shard_map/ppermute | solution.py:39
  399.7 6.3 %collective-permute-start.55 = (f32[2,36,2]{2,1,0:T(8,128)S(1)}, f32[2,36,2]{2,1,0:T(8,128)S(1)}, u32[]{:S(2)}, u32[]{:S(2)}) collective-permute-start(f32[2,36,2]{2,1,0:T(8,128)S(1)} %get-tuple-element.75), channel_id=1, source_target_pairs={{1,0},{3,2},{5,4},{7,6},{9,8},{11,10},{13,12},{15,14},{17,16},{19,... | collective-permute-start | bytes 1736 | tf_op jit(solution)/shard_map/ppermute | solution.py:40
  (27 other events, 73.9 us)

commit v2 on v1

v2 whole, which is shorter than its diff:
```python
import functools

import jax
import jax.numpy as jnp
from jax import lax
from jax.experimental import pallas as pl
from jax.experimental.pallas import tpu as pltpu
from jax.sharding import PartitionSpec as P

ITERS = 3
CLASSES = 16
SHIPS = 8

gravity = 9.81
time_step = 0.1
storage = 0.1
corner_weight = 0.25

LANES = 128
TILE = 8
GUARD = 8
HALO = 16
VMEM_BYTES = 56 * 1024 * 1024


class Shape:
    def __init__(self, rows, cols):
        self.rows = rows
        self.own = cols // LANES
        self.chunks = self.own + 1
        self.first = GUARD + HALO
        self.total = rows + 2 * (GUARD + HALO)


class Ring:
    def __init__(self, make, chunks, lane):
        self.make = make
        self.chunks = chunks
        self.lane = lane
        self.held = {}

    def at(self, chunk):
        entry = self.held.setdefault(chunk, {})
        if 0 not in entry:
            entry[0] = self.make(chunk)
        return entry[0]

    def rolled(self, chunk, amount):
        value = self.at(chunk)
        entry = self.held[chunk]
        if amount not in entry:
            entry[amount] = pltpu.roll(value, amount, 1)
        return entry[amount]

    def before(self, chunk, step):
        other = (chunk - 1) % self.chunks
        return jnp.where(self.lane < step, self.rolled(other, step), self.rolled(chunk, step))

    def after(self, chunk, step):
        other = (chunk + 1) % self.chunks
        amount = LANES - step
        return jnp.where(self.lane >= amount, self.rolled(other, amount), self.rolled(chunk, amount))

    def done(self, chunk):
        self.held.pop((chunk - 1) % self.chunks, None)


def lanes_of():
    return lax.broadcasted_iota(jnp.int32, (TILE, LANES), 1)


def sweep(first, tiles, body):
    def turn(number, carry):
        body(first + number * TILE)
        return carry

    lax.fori_loop(0, tiles, turn, 0)


def load(ref, index, chunk, row):
    return ref[index, chunk, pl.ds(row, TILE), :]


def store(ref, index, chunk, row, value):
    ref[index, chunk, pl.ds(row, TILE), :] = value


CONDUCT, HALF_RATE, INVERSE, HEAD, DIAGONAL = range(5)


def predict_rows(shape, vel, head_pressure, static, moved, row):
    lane = lanes_of()
    rings = [
        Ring(lambda c, k=k: load(vel, k, c, row), shape.chunks, lane) for k in range(4)
    ]
    potential = Ring(lambda c: load(head_pressure, 0, c, row), shape.chunks, lane)
    for c in range(shape.chunks):
        wet = load(static, CONDUCT, c, row) > 0.0
        rate = time_step * load(static, HALF_RATE, c, row)
        slope_a = (0.5 * time_step) * (
            load(head_pressure, 0, c, row + 1) - load(head_pressure, 0, c, row - 1)
        )
        slope_c = (0.5 * time_step) * (potential.after(c, 1) - potential.before(c, 1))
        for layer in range(2):
            along = rings[layer].at(c)
            cross = rings[2 + layer].at(c)
            up_a = (0.5 * time_step) * jnp.maximum(along, 0.0)
            dn_a = (0.5 * time_step) * jnp.minimum(along, 0.0)
            up_c = (0.5 * time_step) * jnp.maximum(cross, 0.0)
            dn_c = (0.5 * time_step) * jnp.minimum(cross, 0.0)
            centre = (
                0.8 - 3.0 * ((up_a - dn_a) + (up_c - dn_c)) - (rate if layer == 0 else 2.0 * rate)
            )
            back_a = 0.05 + 4.0 * up_a
            fore_a = 0.05 - 4.0 * dn_a
            back_c = 0.05 + 4.0 * up_c
            fore_c = 0.05 - 4.0 * dn_c
            for part, slope in ((layer, slope_a), (2 + layer, slope_c)):
                ring = rings[part]
                other = rings[part + 1 - 2 * layer].at(c)
                value = centre * ring.at(c) + rate * other - slope
                value = value + (
                    back_a * load(vel, part, c, row - 1) - up_a * load(vel, part, c, row - 2)
                )
                value = value + (
                    fore_a * load(vel, part, c, row + 1) + dn_a * load(vel, part, c, row + 2)
                )
                value = value + (back_c * ring.before(c, 1) - up_c * ring.before(c, 2))
                value = value + (fore_c * ring.after(c, 1) + dn_c * ring.after(c, 2))
                store(moved, part, c, row, jnp.where(wet, value, 0.0))
        for ring in rings:
            ring.done(c)
        potential.done(c)


def source_rows(shape, moved, static, krylov, row):
    lane = lanes_of()
    rings = [
        Ring(
            lambda c, k=k: load(static, CONDUCT, c, row) * load(moved, 2 + k, c, row),
            shape.chunks,
            lane,
        )
        for k in range(2)
    ]
    for c in range(shape.chunks):
        above = load(static, CONDUCT, c, row - 1)
        below = load(static, CONDUCT, c, row + 1)
        scale = (-0.5 / time_step) * load(static, INVERSE, c, row)
        for layer in range(2):
            flow = (
                below * load(moved, layer, c, row + 1)
                - above * load(moved, layer, c, row - 1)
                + (rings[layer].after(c, 1) - rings[layer].before(c, 1))
            )
            store(krylov, layer, c, row, scale * flow)
            rings[layer].done(c)


def link_rows(shape, krylov, static, level, row, own_only):
    lane = lanes_of()

    def plain(layer, c):
        values = [load(krylov, 2 * level + layer, c, row + d) for d in (-1, 0, 1)]
        return values[1], values[0] + values[2]

    def weighted(layer, c):
        values = [
            load(static, CONDUCT, c, row + d) * load(krylov, 2 * level + layer, c, row + d)
            for d in (-1, 0, 1)
        ]
        return values[1], values[0] + values[2]

    sides = {}

    def ring_of(kind, layer):
        def make(c):
            middle, sums = kind(layer, c)
            sides[kind, layer, c] = sums
            return middle + corner_weight * sums

        return Ring(make, shape.chunks, lane)

    rings = [(ring_of(plain, layer), ring_of(weighted, layer)) for layer in range(2)]
    for c in range(shape.own if own_only else shape.chunks):
        conduct = load(static, CONDUCT, c, row)
        rate = load(static, HALF_RATE, c, row)
        centre = [load(krylov, 2 * level + layer, c, row) for layer in range(2)]
        results = []
        for layer in range(2):
            ring, scaled = rings[layer]
            around = (ring.before(c, 1) + ring.after(c, 1)) + sides[plain, layer, c]
            flows = (scaled.before(c, 1) + scaled.after(c, 1)) + sides[weighted, layer, c]
            results.append(0.5 * (conduct * around + flows) + rate * centre[1 - layer])
            ring.done(c)
            scaled.done(c)
        yield c, centre, results


def krylov_rows(shape, krylov, static, level, row):
    for c, _, results in link_rows(shape, krylov, static, level, row, False):
        inverse = load(static, INVERSE, c, row)
        for layer in range(2):
            store(krylov, 2 * level + 2 + layer, c, row, inverse * results[layer])


def moments_of(shape, krylov, static):
    zeros = (jnp.zeros((TILE, LANES), jnp.float32),) * (2 * ITERS)

    def turn(number, sums):
        row = shape.first + number * TILE
        sums = list(sums)
        for c, top, results in link_rows(shape, krylov, static, 2, row, True):
            diagonal = load(static, DIAGONAL, c, row)
            for layer in range(2):
                low = load(krylov, layer, c, row)
                mid = load(krylov, 2 + layer, c, row)
                low_d, mid_d, top_d = diagonal * low, diagonal * mid, diagonal * top[layer]
                terms = (
                    low * low_d,
                    low * mid_d,
                    mid * mid_d,
                    mid * top_d,
                    top[layer] * top_d,
                    top[layer] * results[layer],
                )
                sums = [a + b for a, b in zip(sums, terms)]
        return tuple(sums)

    return lax.fori_loop(0, shape.rows // TILE, turn, zeros)


def put_moments(out, sums):
    lane = lanes_of()
    result = jnp.zeros((TILE, LANES), jnp.float32)
    for number, part in enumerate(sums):
        result = jnp.where(lane == number, jnp.sum(part), result)
    out[...] = result


def project(shape, vel, potential, static, moved, krylov, moments, first, tiles):
    sweep(first[0], tiles[0], functools.partial(predict_rows, shape, vel, potential, static, moved))
    sweep(first[1], tiles[1], functools.partial(source_rows, shape, moved, static, krylov))
    for level in range(2):
        sweep(
            first[2 + level],
            tiles[2 + level],
            functools.partial(krylov_rows, shape, krylov, static, level),
        )
    put_moments(moments, moments_of(shape, krylov, static))


def pack_kernel(shape, vel, surface, wet, bathy, table, lo, hi, side, clo, chi):
    half = lax.axis_index("cross")
    lane = lanes_of()
    for t in range(shape.rows // TILE):
        rows = pl.ds(t * TILE, TILE)
        target, corner = (lo, clo) if t * TILE < HALO else (hi, chi)
        at = pl.ds(t * TILE % HALO, TILE)
        edges = []
        for c in range(shape.own):
            cols = pl.ds(c * LANES, LANES)
            flag = wet[rows, cols]
            number = bathy[rows, cols]
            thick = jnp.zeros((TILE, LANES), jnp.float32)
            for entry in range(CLASSES):
                thick = jnp.where(number == entry, 0.5 * table[entry], thick)
            values = [jnp.where(flag > 0, vel[k, rows, cols], 0.0) for k in range(4)]
            values += [surface[rows, cols], flag.astype(jnp.float32), thick]
            for k, value in enumerate(values):
                target[k, at, cols] = value
            if c in (0, shape.own - 1):
                edges.append(values)
        for k in range(7):
            value = jnp.where(
                half == 0,
                jnp.where(lane >= LANES // 2, edges[1][k], 0.0),
                jnp.where(lane < LANES // 2, edges[0][k], 0.0),
            )
            side[k, rows, :] = value
            corner[k, at, :] = value


def first_kernel(
    shape, lo, hi, top, bot, side, ctop, cbot, ranges, heads,
    moved, static, surface, krylov, moments,
    vel, potential, thick, columns,
):
    along = lax.axis_index("along")
    half = lax.axis_index("cross")
    lane = lanes_of()
    line = lax.broadcasted_iota(jnp.int32, (TILE, LANES), 0)
    for c in range(shape.chunks):
        if c < shape.own:
            index = half * (shape.own * LANES) + c * LANES + lane
        else:
            index = jnp.where(half == 0, shape.own * LANES, (shape.own - 1) * LANES) + lane
        for s in range(SHIPS):
            inside = jnp.logical_and(index >= ranges[s, 2], index < ranges[s, 3])
            columns[s, c] = jnp.where(inside, gravity * heads[s], 0.0)
    pieces = [(GUARD, top, ctop, 0), (shape.first, lo, side, 0)]
    pieces += [(shape.first + HALO, hi, side, HALO), (shape.first + shape.rows, bot, cbot, 0)]
    for base, wide, narrow, offset in pieces:

        def turn(number, carry, base=base, wide=wide, narrow=narrow, offset=offset):
            at = pl.multiple_of(number * TILE, TILE)
            row = base + number * TILE
            global_row = along * shape.rows + (row - shape.first) + line
            covered = [
                jnp.logical_and(global_row >= ranges[s, 0], global_row < ranges[s, 1])
                for s in range(SHIPS)
            ]
            for c in range(shape.chunks):
                if c < shape.own:
                    values = [
                        wide[k, pl.ds(at, TILE), pl.ds(c * LANES, LANES)] for k in range(7)
                    ]
                else:
                    values = [narrow[k, pl.ds(offset + at, TILE), :] for k in range(7)]
                for k in range(4):
                    store(vel, k, c, row, values[k])
                depth = values[6]
                inside = depth > 0.0
                depth = jnp.where(inside, depth, 1.0)
                head = jnp.zeros((TILE, LANES), jnp.float32)
                for s in range(SHIPS):
                    head = head + jnp.where(covered[s], columns[s, c], 0.0)
                head = jnp.where(inside, head, 0.0)
                store(surface, 0, c, row, values[4])
                store(potential, 0, c, row, gravity * values[4] + head)
                store(thick, 0, c, row, values[6])
                store(static, CONDUCT, c, row, values[5] * values[6])
                store(static, HALF_RATE, c, row, 0.5 / depth)
                store(static, HEAD, c, row, head)
            return carry

        lax.fori_loop(0, HALO // TILE, turn, 0)

    def diagonal_rows(row):
        sides = {}

        def make(c):
            sums = load(static, CONDUCT, c, row - 1) + load(static, CONDUCT, c, row + 1)
            sides[c] = sums
            return load(static, CONDUCT, c, row) + corner_weight * sums

        ring = Ring(make, shape.chunks, lane)
        for c in range(shape.chunks):
            around = ring.before(c, 1) + ring.after(c, 1) + sides[c]
            depth = load(thick, 0, c, row)
            diagonal = (
                0.5 * (around + 5.0 * load(static, CONDUCT, c, row))
                + storage * depth
                + load(static, HALF_RATE, c, row)
            )
            store(static, DIAGONAL, c, row, diagonal)
            store(static, INVERSE, c, row, jnp.where(depth > 0.0, 1.0 / diagonal, 0.0))
            ring.done(c)

    start = GUARD
    sweep(start + 4, 7, diagonal_rows)
    project(
        shape, vel, potential, static, moved, krylov, moments,
        (start + 4, start + 5, start + 6, start + 7), (7, 7, 7, 7),
    )


def coefficients(shares):
    total = jnp.sum(shares[...], axis=0, keepdims=True)
    mu = [jnp.broadcast_to(total[:, k : k + 1], (TILE, LANES)) for k in range(2 * ITERS)]

    def norm(c):
        return sum(c[i] * c[j] * mu[i + j] for i in range(len(c)) for j in range(len(c)))

    def energy(c):
        return sum(
            c[i] * c[j] * (mu[i + j] - mu[i + j + 1]) for i in range(len(c)) for j in range(len(c))
        )

    floor = 2e-7 * mu[0]
    one = jnp.ones((TILE, LANES), jnp.float32)
    z = [one]
    search = [one]
    result = [jnp.zeros((TILE, LANES), jnp.float32)] * ITERS
    norm_now = mu[0]
    for iteration in range(ITERS):
        step = norm_now / energy(search)
        if iteration:
            step = jnp.where(norm_now > floor, step, 0.0)
        for i, c in enumerate(search):
            result[i] = result[i] + step * c
        if iteration + 1 < ITERS:
            applied = [
                (search[i] if i < len(search) else 0.0) - (search[i - 1] if i else 0.0)
                for i in range(len(search) + 1)
            ]
            z = [(z[i] if i < len(z) else 0.0) - step * applied[i] for i in range(len(applied))]
            norm_next = norm(z)
            ratio = norm_next / norm_now
            if iteration:
                ratio = jnp.where(norm_now > floor, ratio, 0.0)
            search = [z[i] + (ratio * search[i] if i < len(search) else 0.0) for i in range(len(z))]
            norm_now = norm_next
    return result


def pressure_rows(shape, factors, krylov, pressure, row):
    for c in range(shape.chunks):
        for layer in range(2):
            value = factors[0] * load(krylov, layer, c, row)
            value = value + factors[1] * load(krylov, 2 + layer, c, row)
            value = value + factors[2] * load(krylov, 4 + layer, c, row)
            store(pressure, layer, c, row, value)


def along_moved(moved, pressure, layer, c, row):
    return load(moved, layer, c, row) - (0.5 * time_step) * (
        load(pressure, layer, c, row + 1) - load(pressure, layer, c, row - 1)
    )


def move_rows(shape, moved, pressure, static, flux, put, row):
    lane = lanes_of()
    rings = [
        Ring(lambda c, k=k: load(pressure, k, c, row), shape.chunks, lane) for k in range(2)
    ]
    for c in range(shape.chunks):
        conduct = load(static, CONDUCT, c, row)
        wet = conduct > 0.0
        along = [along_moved(moved, pressure, layer, c, row) for layer in range(2)]
        cross = [
            load(moved, 2 + layer, c, row)
            - (0.5 * time_step) * (rings[layer].after(c, 1) - rings[layer].before(c, 1))
            for layer in range(2)
        ]
        for part, value in enumerate(along + cross):
            put(part, c, row, jnp.where(wet, value, 0.0))
        store(flux, 0, c, row, conduct * (along[0] + along[1]))
        store(flux, 1, c, row, conduct * (cross[0] + cross[1]))
        for ring in rings:
            ring.done(c)


def surface_rows(shape, surface, flux, chunks, put, row):
    ring = Ring(lambda c: load(flux, 1, c, row), shape.chunks, lanes_of())
    for c in range(chunks):
        value = load(surface, 0, c, row) - (0.5 * time_step) * (
            load(flux, 0, c, row + 1)
            - load(flux, 0, c, row - 1)
            + (ring.after(c, 1) - ring.before(c, 1))
        )
        put(c, row, value)
        ring.done(c)


def second_kernel(
    shape, shares, moved_in, static, surface_in, krylov_in,
    moved, surface, krylov, moments,
    vel, potential, pressure, flux,
):
    factors = coefficients(shares)
    start = GUARD
    sweep(start + 7, 7, functools.partial(pressure_rows, shape, factors, krylov_in, pressure))
    sweep(
        start + 8,
        6,
        functools.partial(
            move_rows, shape, moved_in, pressure, static, flux, functools.partial(store, vel)
        ),
    )

    def put(c, row, value):
        value = jnp.where(load(static, INVERSE, c, row) > 0.0, value, 0.0)
        store(surface, 0, c, row, value)
        store(potential, 0, c, row, gravity * value + load(static, HEAD, c, row))

    sweep(
        start + 9,
        6,
        functools.partial(surface_rows, shape, surface_in, flux, shape.chunks, put),
    )
    project(
        shape, vel, potential, static, moved, krylov, moments,
        (start + 11, start + 12, start + 13, start + 14), (6, 5, 5, 5),
    )


def last_kernel(
    shape, shares, moved, static, surface, krylov,
    new_vel, new_surface, new_pressure,
    pressure, flux,
):
    factors = coefficients(shares)
    start = shape.first
    sweep(start - 2, 5, functools.partial(pressure_rows, shape, factors, krylov, pressure))

    def put_vel(part, c, row, value):
        if c < shape.own:
            at = pl.multiple_of(row - start, TILE)
            new_vel[part, pl.ds(at, TILE), pl.ds(c * LANES, LANES)] = value
            if part < 2:
                new_pressure[part, pl.ds(at, TILE), pl.ds(c * LANES, LANES)] = load(
                    pressure, part, c, row
                )

    sweep(
        start,
        shape.rows // TILE,
        functools.partial(move_rows, shape, moved, pressure, static, flux, put_vel),
    )
    for row in (start - 1, start + shape.rows):
        for c in range(shape.own):
            one = slice(row, row + 1)
            total = jnp.zeros((1, LANES), jnp.float32)
            for layer in range(2):
                total = total + (
                    moved[layer, c, one, :]
                    - (0.5 * time_step)
                    * (
                        pressure[layer, c, row + 1 : row + 2, :]
                        - pressure[layer, c, row - 1 : row, :]
                    )
                )
            flux[0, c, one, :] = static[CONDUCT, c, one, :] * total

    def put(c, row, value):
        at = pl.multiple_of(row - start, TILE)
        new_surface[pl.ds(at, TILE), pl.ds(c * LANES, LANES)] = value

    sweep(
        start,
        shape.rows // TILE,
        functools.partial(surface_rows, shape, surface, flux, shape.own, put),
    )


def call(kernel, shape, kinds, outs, scratch, operands):
    f32 = jnp.float32
    return pl.pallas_call(
        functools.partial(kernel, shape),
        out_shape=[jax.ShapeDtypeStruct(s, f32) for s in outs],
        in_specs=[pl.BlockSpec(memory_space=kind) for kind in kinds],
        out_specs=[pl.BlockSpec(memory_space=pltpu.VMEM)] * len(outs),
        scratch_shapes=[pltpu.VMEM(s, f32) for s in scratch],
        compiler_params=pltpu.CompilerParams(vmem_limit_bytes=VMEM_BYTES),
    )(*operands)


def shared(moments):
    count = lax.axis_size("along") * lax.axis_size("cross")
    spread = jnp.broadcast_to(moments[0:1, 0:8], (count, 8))
    return lax.all_to_all(spread, ("along", "cross"), 0, 0, tiled=True)


def shards(velocity, surface, wet_mask, bathy_class, depth_table, hull_ranges, hull_pressure):
    shape = Shape(*surface.shape)
    vmem, smem = pltpu.VMEM, pltpu.SMEM
    cols = surface.shape[1]
    wide, narrow = (7, HALO, cols), (7, HALO, LANES)
    lo, hi, side, clo, chi = call(
        pack_kernel, shape, [vmem] * 4 + [smem],
        [wide, wide, (7, shape.rows, LANES), narrow, narrow], [],
        (velocity, surface, wet_mask, bathy_class, depth_table),
    )
    size = lax.axis_size("along")
    both = ("along", "cross")
    up = [(i, i + 1) for i in range(size - 1)]
    down = [(j, i) for i, j in up]
    turned = [(0, 1), (1, 0)]
    top = lax.ppermute(hi, "along", up)
    bot = lax.ppermute(lo, "along", down)
    far = lax.ppermute(side, "cross", turned)
    ctop = lax.ppermute(chi, both, [(2 * i + a, 2 * j + b) for i, j in up for a, b in turned])
    cbot = lax.ppermute(clo, both, [(2 * i + a, 2 * j + b) for i, j in down for a, b in turned])

    field = (shape.chunks, shape.total, LANES)
    fields = lambda count: (count,) + field
    sums = (TILE, LANES)
    moved, static, level, krylov, moments = call(
        first_kernel, shape, [vmem] * 7 + [smem] * 2,
        [fields(4), fields(5), fields(1), fields(6), sums],
        [fields(4), fields(1), fields(1), (SHIPS, shape.chunks, TILE, LANES)],
        (lo, hi, top, bot, far, ctop, cbot, hull_ranges, hull_pressure),
    )
    moved, level, krylov, moments = call(
        second_kernel, shape, [vmem] * 5,
        [fields(4), fields(1), fields(6), sums],
        [fields(4), fields(1), fields(2), fields(2)],
        (shared(moments), moved, static, level, krylov),
    )
    return tuple(
        call(
            last_kernel, shape, [vmem] * 5,
            [velocity.shape, surface.shape, (2,) + surface.shape],
            [fields(2), fields(2)],
            (shared(moments), moved, static, level, krylov),
        )
    )


def solution(mesh):
    cell = P("along", "cross")
    layered = P(None, "along", "cross")
    in_specs = (layered, cell, cell, cell, P(), P(), P())
    return jax.shard_map(
        shards, mesh=mesh, in_specs=in_specs, out_specs=(layered, cell, layered), check_vma=False
    )
```

time: 415 us -> 96.7 us (0.23); the launches traced: 410 us -> 96.4 us
  starting transfers between devices: 161 us -> 16.4 us
  other arithmetic: 53.2 us -> 0 us
  waiting for transfers between devices: 49.5 us -> 2.33 us
  blocking collectives: 78.7 us -> 37.5 us
  Pallas kernels: 0 us -> 34.9 us
  between operations: 32.1 us -> 0.71 us
  local copies, waits for them, and re-layouts: 33.7 us -> 4.52 us
    ppermute x56 -> x5, starting transfers between devices: 161 us -> 16.4 us  [the longest x1 4.44 us: shards(): lax.ppermute(clo, both, [(2 * i + a, 2 * j + b) for i, j in down for a, b...]
    ppermute x56 -> x5, waiting for transfers between devices: 49.5 us -> 2.33 us  [the longest x1 2.31 us: shards(): lax.ppermute(clo, both, [(2 * i + a, 2 * j + b) for i, j in down for a, b...]
    all_to_all x2, blocking collectives: 78.7 us -> 37.5 us  [shared(): return lax.all_to_all(spread, ('along', 'cross'), 0, 0, tiled=True)]
    pallas_call x0 -> x4, Pallas kernels: none -> 34.9 us  [call(): pl.pallas_call(functools.partial(kernel, shape), out_shape=[jax.ShapeDtyp...]
    mul x19 -> x0, other arithmetic: 21.6 us -> none  [the longest x3 12.2 us: solve(): y0 = source * inverse]
    concatenate x8 -> x0, local copies, waits for them, and re-layouts: 11 us -> none  [padded(): x = jnp.concatenate([before, x, after], axis=dim)]
    div x1 -> x0, other arithmetic: 10.4 us -> none  [diagonal_of(): result = storage * layer_thick + vertical / layer_thick]
    concatenate x24 -> x0, other arithmetic: 8.6 us -> none  [padded(): x = jnp.concatenate([before, x, after], axis=dim)]
  transfers between devices with their start and end apart: 56 -> 5, of which waited for: 23 -> 1; matrix products, arithmetic and copies ran while one was open for 9% -> 1% of each run, Pallas kernels for 0% -> 0%
where the time goes in v2:
time: 96.7 us; the launch traced here: 96.4 us
  blocking collectives  37.5 us (39%)
  Pallas kernels  34.9 us (36%)
  starting transfers between devices  16.4 us (17%)
  local copies, waits for them, and re-layouts  4.52 us (5%)
  waiting for transfers between devices  2.33 us (2%)
    all_to_all x2, blocking collectives, shared(): return lax.all_to_all(spread, ('along', 'cross'), 0, 0, tiled=True)  37.5 us
    pallas_call x4, Pallas kernels, call(): pl.pallas_call(functools.partial(kernel, shape), out_shape=[jax.ShapeDtyp...  34.9 us
    ppermute x1, starting transfers between devices, shards(): lax.ppermute(clo, both, [(2 * i + a, 2 * j + b) for i, j in down for a, b...  4.44 us
    ppermute x1, starting transfers between devices, shards(): bot = lax.ppermute(lo, 'along', down)  3.32 us
    ppermute x1, starting transfers between devices, shards(): top = lax.ppermute(hi, 'along', up)  3.18 us
    unnamed x11, local copies, waits for them, and re-layouts  3.07 us
    ppermute x1, starting transfers between devices, shards(): far = lax.ppermute(side, 'cross', turned)  2.82 us
    ppermute x1, starting transfers between devices, shards(): lax.ppermute(chi, both, [(2 * i + a, 2 * j + b) for i, j in up for a, b i...  2.62 us
  transfers between devices with their start and end apart: 5, of which 1 were waited for; matrix products, arithmetic and copies ran while one was open for 1% of the time, Pallas kernels for 0%

profile of v2, /device:TPU:1, one launch (start us, length us, event | category | flops | bytes accessed | tf_op | source)
XLA Modules:
  0.0 96.4 jit_solution(1915209853959314879)
XLA Ops:
  0.6 2.7 %shard_map.94 = (f32[7,16,1536]{2,1,0:T(8,128)}, f32[7,16,1536]{2,1,0:T(8,128)}, f32[7,32,128]{2,1,0:T(8,128)}, f32[7,16,128]{2,1,0:T(8,128)}, f32[7,16,128]{2,1,0:T(8,128)}) custom-call(f32[4,32,1536]{2,1,0:T(8,128)} %vel.1, f32[32,1536]{1,0:T(8,128)} %surface.1, s32[32,1536]{1,0:T(8,128)} %wet.1, s32[32,1536]{1,0:T(8,128)} %bathy.1, f32[16]{0:T(128)} %table.1), custom_call_target="tpu_custom_call" | custom-call | tf_op jit(solution)/shard_map/pallas_call | solution.py:539
  3.3 3.3 %collective-permute-start.1 = (f32[7,16,1536]{2,1,0:T(8,128)}, f32[7,16,1536]{2,1,0:T(8,128)S(1)}, u32[]{:S(2)}, u32[]{:S(2)}) collective-permute-start(f32[7,16,1536]{2,1,0:T(8,128)} %get-tuple-element.17.lo), channel_id=1, source_target_pairs={{2,0},{4,2},{6,4},{8,6},{10,8},{12,10},{14,12},{16,14},{18,16},{20... | collective-permute-start | bytes 2064392 | tf_op jit(solution)/shard_map/ppermute | solution.py:571
  6.6 3.2 %collective-permute-start = (f32[7,16,1536]{2,1,0:T(8,128)}, f32[7,16,1536]{2,1,0:T(8,128)S(1)}, u32[]{:S(2)}, u32[]{:S(2)}) collective-permute-start(f32[7,16,1536]{2,1,0:T(8,128)} %get-tuple-element.18.hi), channel_id=1, source_target_pairs={{0,2},{2,4},{4,6},{6,8},{8,10},{10,12},{12,14},{14,16},{16,18},{18... | collective-permute-start | bytes 2064392 | tf_op jit(solution)/shard_map/ppermute | solution.py:570
  9.8 2.8 %collective-permute-start.2 = (f32[7,32,128]{2,1,0:T(8,128)}, f32[7,32,128]{2,1,0:T(8,128)S(1)}, u32[]{:S(2)}, u32[]{:S(2)}) collective-permute-start(f32[7,32,128]{2,1,0:T(8,128)} %get-tuple-element.19), channel_id=1, source_target_pairs={{0,1},{1,0},{2,3},{3,2},{4,5},{5,4},{6,7},{7,6},{8,9},{9,8},{10,11... | collective-permute-start | bytes 344072 | tf_op jit(solution)/shard_map/ppermute | solution.py:572
  12.7 2.6 %collective-permute-start.3 = (f32[7,16,128]{2,1,0:T(8,128)}, f32[7,16,128]{2,1,0:T(8,128)S(1)}, u32[]{:S(2)}, u32[]{:S(2)}) collective-permute-start(f32[7,16,128]{2,1,0:T(8,128)} %get-tuple-element.20), channel_id=1, source_target_pairs={{0,3},{1,2},{2,5},{3,4},{4,7},{5,6},{6,9},{7,8},{8,11},{9,10},{10,... | collective-permute-start | bytes 172040 | tf_op jit(solution)/shard_map/ppermute | solution.py:573
  15.3 4.4 %collective-permute-start.4 = (f32[7,16,128]{2,1,0:T(8,128)}, f32[7,16,128]{2,1,0:T(8,128)S(1)}, u32[]{:S(2)}, u32[]{:S(2)}) collective-permute-start(f32[7,16,128]{2,1,0:T(8,128)} %get-tuple-element.21), channel_id=1, source_target_pairs={{2,1},{3,0},{4,3},{5,2},{6,5},{7,4},{8,7},{9,6},{10,9},{11,8},{12,... | collective-permute-start | bytes 172040 | tf_op jit(solution)/shard_map/ppermute | solution.py:574
  19.7 1.3 %copy.11.ranges = s32[8,4]{1,0:T(8,128)} copy(s32[8,4]{0,1:T(4,128)} %param.12) | data formatting | bytes 256 | tf_op args[5]
  21.1 0.0 collective-permute-done.3.ctop
  21.1 0.0 copy-start.3
  21.1 2.3 %collective-permute-done.4.cbot = f32[7,16,128]{2,1,0:T(8,128)S(1)} collective-permute-done((f32[7,16,128]{2,1,0:T(8,128)}, f32[7,16,128]{2,1,0:T(8,128)S(1)}, u32[]{:S(2)}, u32[]{:S(2)}) %collective-permute-start.4) | collective-permute-done | bytes 57376 | tf_op jit(solution)/shard_map/ppermute | solution.py:574
  23.4 0.0 copy-start.4
  23.4 0.0 collective-permute-done.2.side
  23.4 0.0 copy-start.2
  23.4 0.0 collective-permute-done.1.bot
  23.4 0.0 copy-start
  23.4 0.0 collective-permute-done.top
  23.4 0.0 copy-done.3
  23.4 0.6 copy-done.4
  24.0 0.0 copy-done.2
  24.1 0.2 copy-done
  24.3 0.0 copy-start.1
  24.3 0.8 copy-done.1
  25.1 13.2 %shard_map.95 = (f32[4,13,80,128]{3,2,1,0:T(8,128)}, f32[5,13,80,128]{3,2,1,0:T(8,128)}, f32[1,13,80,128]{3,2,1,0:T(8,128)}, f32[6,13,80,128]{3,2,1,0:T(8,128)}, f32[8,128]{1,0:T(8,128)}) custom-call(f32[7,16,1536]{2,1,0:T(8,128)} %get-tuple-element.17.lo, f32[7,16,1536]{2,1,0:T(8,128)} %get-tuple-element.18.hi, f32[7,16,1536]{2,1,0:T(8,128)} %copy-done.1, ...), custom_call_target="tpu_custom_call" | custom-call | tf_op jit(solution)/shard_map/pallas_call | solution.py:539
  38.3 0.7 slice_bitcast_fusion.1
  39.0 23.3 %all_to_all.16 = f32[128,1,8]{2,1,0:T(1,128)} all-to-all(f32[128,1,8]{2,1,0:T(1,128)S(1)} %broadcast_in_dim.4), channel_id=1, replica_groups=mesh['along'=64,'cross'=2] {'along','cross'}, dimensions={0} | all-to-all | bytes 8192 | tf_op jit(solution)/shard_map/all_to_all | solution.py:552
  62.3 13.3 %shard_map.96 = (f32[4,13,80,128]{3,2,1,0:T(8,128)}, f32[1,13,80,128]{3,2,1,0:T(8,128)}, f32[6,13,80,128]{3,2,1,0:T(8,128)}, f32[8,128]{1,0:T(8,128)}) custom-call(f32[128,8]{1,0:T(8,128)} %bitcast.6, f32[4,13,80,128]{3,2,1,0:T(8,128)} %get-tuple-element.23.moved_in, f32[5,13,80,128]{3,2,1,0:T(8,128)} %get-tuple-element.24.static, ...), custom_call_target="tpu_custom_call" | custom-call | tf_op jit(solution)/shard_map/pallas_call | solution.py:539
  75.6 0.7 slice_bitcast_fusion
  76.3 14.3 %all_to_all.17 = f32[128,1,8]{2,1,0:T(1,128)} all-to-all(f32[128,1,8]{2,1,0:T(1,128)S(1)} %broadcast_in_dim.5), channel_id=1, replica_groups=mesh['along'=64,'cross'=2] {'along','cross'}, dimensions={0} | all-to-all | bytes 8192 | tf_op jit(solution)/shard_map/all_to_all | solution.py:552
  90.6 5.7 %shard_map.97 = (f32[4,32,1536]{2,1,0:T(8,128)}, f32[32,1536]{1,0:T(8,128)}, f32[2,32,1536]{2,1,0:T(8,128)}) custom-call(f32[128,8]{1,0:T(8,128)} %bitcast.7, f32[4,13,80,128]{3,2,1,0:T(8,128)} %get-tuple-element.28.moved, f32[5,13,80,128]{3,2,1,0:T(8,128)} %get-tuple-element.24.static, f32[1,13,80,128]{3,2,1,0:T(8,128)} %get-tuple-element.29.surface, ...), custom_call_target="tpu_custom_call" | custom-call | tf_op jit(solution)/shard_map/pallas_call | solution.py:539
  (2 shorter events, 0.1 us)
Async XLA Ops:
  3.3 20.1 %collective-permute-start.1 = (f32[7,16,1536]{2,1,0:T(8,128)}, f32[7,16,1536]{2,1,0:T(8,128)S(1)}, u32[]{:S(2)}, u32[]{:S(2)}) collective-permute-start(f32[7,16,1536]{2,1,0:T(8,128)} %get-tuple-element.17.lo), channel_id=1, source_target_pairs={{2,0},{4,2},{6,4},{8,6},{10,8},{12,10},{14,12},{16,14},{18,16},{20... | collective-permute-start | bytes 2064392 | tf_op jit(solution)/shard_map/ppermute | solution.py:571
  6.6 16.8 %collective-permute-start = (f32[7,16,1536]{2,1,0:T(8,128)}, f32[7,16,1536]{2,1,0:T(8,128)S(1)}, u32[]{:S(2)}, u32[]{:S(2)}) collective-permute-start(f32[7,16,1536]{2,1,0:T(8,128)} %get-tuple-element.18.hi), channel_id=1, source_target_pairs={{0,2},{2,4},{4,6},{6,8},{8,10},{10,12},{12,14},{14,16},{16,18},{18... | collective-permute-start | bytes 2064392 | tf_op jit(solution)/shard_map/ppermute | solution.py:570
  9.8 13.6 %collective-permute-start.2 = (f32[7,32,128]{2,1,0:T(8,128)}, f32[7,32,128]{2,1,0:T(8,128)S(1)}, u32[]{:S(2)}, u32[]{:S(2)}) collective-permute-start(f32[7,32,128]{2,1,0:T(8,128)} %get-tuple-element.19), channel_id=1, source_target_pairs={{0,1},{1,0},{2,3},{3,2},{4,5},{5,4},{6,7},{7,6},{8,9},{9,8},{10,11... | collective-permute-start | bytes 344072 | tf_op jit(solution)/shard_map/ppermute | solution.py:572
  12.7 8.4 %collective-permute-start.3 = (f32[7,16,128]{2,1,0:T(8,128)}, f32[7,16,128]{2,1,0:T(8,128)S(1)}, u32[]{:S(2)}, u32[]{:S(2)}) collective-permute-start(f32[7,16,128]{2,1,0:T(8,128)} %get-tuple-element.20), channel_id=1, source_target_pairs={{0,3},{1,2},{2,5},{3,4},{4,7},{5,6},{6,9},{7,8},{8,11},{9,10},{10,... | collective-permute-start | bytes 172040 | tf_op jit(solution)/shard_map/ppermute | solution.py:573
  15.3 8.1 %collective-permute-start.4 = (f32[7,16,128]{2,1,0:T(8,128)}, f32[7,16,128]{2,1,0:T(8,128)S(1)}, u32[]{:S(2)}, u32[]{:S(2)}) collective-permute-start(f32[7,16,128]{2,1,0:T(8,128)} %get-tuple-element.21), channel_id=1, source_target_pairs={{2,1},{3,0},{4,3},{5,2},{6,5},{7,4},{8,7},{9,6},{10,9},{11,8},{12,... | collective-permute-start | bytes 172040 | tf_op jit(solution)/shard_map/ppermute | solution.py:574
  21.1 2.4 %copy-start.3 = (f32[7,16,128]{2,1,0:T(8,128)}, f32[7,16,128]{2,1,0:T(8,128)S(1)}, u32[]{:S(2)}) copy-start(f32[7,16,128]{2,1,0:T(8,128)S(1)} %collective-permute-done.3.ctop) | copy-start | bytes 172036
  23.4 0.6 copy-start.4
  23.4 0.7 copy-start.2
  23.4 0.9 copy-start
  24.3 0.9 copy-start.1

commit v3 on v2

--- a/solution.py
+++ b/solution.py
@@ -20,7 +20,7 @@
 TILE = 8
 GUARD = 8
 HALO = 16
-VMEM_BYTES = 56 * 1024 * 1024
+VMEM_BYTES = 24 * 1024 * 1024
 
 
 class Shape:
@@ -235,7 +235,7 @@
     result = jnp.zeros((TILE, LANES), jnp.float32)
     for number, part in enumerate(sums):
         result = jnp.where(lane == number, jnp.sum(part), result)
-    out[...] = result
+    out[...] = jnp.broadcast_to(result[0:1, None, 0 : out.shape[2]], out.shape)
 
 
 def project(shape, vel, potential, static, moved, krylov, moments, first, tiles):
@@ -296,7 +296,7 @@
         else:
             index = jnp.where(half == 0, shape.own * LANES, (shape.own - 1) * LANES) + lane
         for s in range(SHIPS):
-            inside = jnp.logical_and(index >= ranges[s, 2], index < ranges[s, 3])
+            inside = jnp.logical_and(index >= ranges[2, s], index < ranges[3, s])
             columns[s, c] = jnp.where(inside, gravity * heads[s], 0.0)
     pieces = [(GUARD, top, ctop, 0), (shape.first, lo, side, 0)]
     pieces += [(shape.first + HALO, hi, side, HALO), (shape.first + shape.rows, bot, cbot, 0)]
@@ -307,7 +307,7 @@
             row = base + number * TILE
             global_row = along * shape.rows + (row - shape.first) + line
             covered = [
-                jnp.logical_and(global_row >= ranges[s, 0], global_row < ranges[s, 1])
+                jnp.logical_and(global_row >= ranges[0, s], global_row < ranges[1, s])
                 for s in range(SHIPS)
             ]
             for c in range(shape.chunks):
@@ -366,7 +366,7 @@
 
 
 def coefficients(shares):
-    total = jnp.sum(shares[...], axis=0, keepdims=True)
+    total = jnp.sum(shares[...], axis=0)
     mu = [jnp.broadcast_to(total[:, k : k + 1], (TILE, LANES)) for k in range(2 * ITERS)]
 
     def norm(c):
@@ -538,7 +538,7 @@
     f32 = jnp.float32
     return pl.pallas_call(
         functools.partial(kernel, shape),
-        out_shape=[jax.ShapeDtypeStruct(s, f32) for s in outs],
+        out_shape=outs,
         in_specs=[pl.BlockSpec(memory_space=kind) for kind in kinds],
         out_specs=[pl.BlockSpec(memory_space=pltpu.VMEM)] * len(outs),
         scratch_shapes=[pltpu.VMEM(s, f32) for s in scratch],
@@ -546,10 +546,12 @@
     )(*operands)
 
 
+def held(*arrays):
+    return tuple(pltpu.with_memory_space_constraint(x, pltpu.VMEM) for x in arrays)
+
+
 def shared(moments):
-    count = lax.axis_size("along") * lax.axis_size("cross")
-    spread = jnp.broadcast_to(moments[0:1, 0:8], (count, 8))
-    return lax.all_to_all(spread, ("along", "cross"), 0, 0, tiled=True)
+    return lax.all_to_all(moments, ("along", "cross"), 0, 0, tiled=True)
 
 
 def shards(velocity, surface, wet_mask, bathy_class, depth_table, hull_ranges, hull_pressure):
@@ -559,7 +561,8 @@
     wide, narrow = (7, HALO, cols), (7, HALO, LANES)
     lo, hi, side, clo, chi = call(
         pack_kernel, shape, [vmem] * 4 + [smem],
-        [wide, wide, (7, shape.rows, LANES), narrow, narrow], [],
+        [pltpu.VMEM(each, jnp.float32) for each in (wide, wide, (7, shape.rows, LANES), narrow, narrow)],
+        [],
         (velocity, surface, wet_mask, bathy_class, depth_table),
     )
     size = lax.axis_size("along")
@@ -574,26 +577,29 @@
     cbot = lax.ppermute(clo, both, [(2 * i + a, 2 * j + b) for i, j in down for a, b in turned])
 
     field = (shape.chunks, shape.total, LANES)
+    f32 = jnp.float32
     fields = lambda count: (count,) + field
-    sums = (TILE, LANES)
+    kept = lambda count: pltpu.VMEM(fields(count), f32)
+    sums = jax.ShapeDtypeStruct((2 * size, 1, 8), f32)
     moved, static, level, krylov, moments = call(
         first_kernel, shape, [vmem] * 7 + [smem] * 2,
-        [fields(4), fields(5), fields(1), fields(6), sums],
+        [kept(4), kept(5), kept(1), kept(6), sums],
         [fields(4), fields(1), fields(1), (SHIPS, shape.chunks, TILE, LANES)],
-        (lo, hi, top, bot, far, ctop, cbot, hull_ranges, hull_pressure),
+        held(lo, hi, top, bot, far, ctop, cbot) + (hull_ranges.T, hull_pressure),
     )
     moved, level, krylov, moments = call(
         second_kernel, shape, [vmem] * 5,
-        [fields(4), fields(1), fields(6), sums],
+        [kept(4), kept(1), kept(6), sums],
         [fields(4), fields(1), fields(2), fields(2)],
-        (shared(moments), moved, static, level, krylov),
-    )
+        (shared(moments),) + held(moved, static, level, krylov),
+    )
+    whole = lambda like: jax.ShapeDtypeStruct(like, f32)
     return tuple(
         call(
             last_kernel, shape, [vmem] * 5,
-            [velocity.shape, surface.shape, (2,) + surface.shape],
+            [whole(velocity.shape), whole(surface.shape), whole((2,) + surface.shape)],
             [fields(2), fields(2)],
-            (shared(moments), moved, static, level, krylov),
+            (shared(moments),) + held(moved, static, level, krylov),
         )
     )
 

time: 96.7 us -> 83.6 us (0.86)
  Pallas kernels: 34.9 us -> 20.1 us
  local copies, waits for them, and re-layouts: 4.52 us -> 5.89 us
  waiting for transfers between devices: 2.33 us -> 3.46 us
    pallas_call x4, Pallas kernels: 34.9 us -> 20.1 us  [call(): pl.pallas_call(functools.partial(kernel, shape), out_shape=outs, in_specs...]
    unnamed x11 -> x14, local copies, waits for them, and re-layouts: 3.07 us -> 5.89 us
    slice x2 -> x0, local copies, waits for them, and re-layouts: 1.37 us -> none  [shared(): spread = jnp.broadcast_to(moments[0:1, 0:8], (count, 8))]
  transfers between devices with their start and end apart: 5 -> 5, of which waited for: 1 -> 2; matrix products, arithmetic and copies ran while one was open for 1% -> 0% of each run, Pallas kernels for 0% -> 0%
where the time goes in v3:
time: 83.6 us; the launch traced here: 83.2 us
  blocking collectives  36.6 us (44%)
  Pallas kernels  20.1 us (24%)
  starting transfers between devices  16.4 us (20%)
  local copies, waits for them, and re-layouts  5.89 us (7%)
  waiting for transfers between devices  3.46 us (4%)
    all_to_all x2, blocking collectives, shared(): return lax.all_to_all(moments, ('along', 'cross'), 0, 0, tiled=True)  36.6 us
    pallas_call x4, Pallas kernels, call(): pl.pallas_call(functools.partial(kernel, shape), out_shape=outs, in_specs...  20.1 us
    unnamed x14, local copies, waits for them, and re-layouts  5.89 us
    ppermute x1, starting transfers between devices, shards(): lax.ppermute(clo, both, [(2 * i + a, 2 * j + b) for i, j in down for a, b...  4.44 us
    ppermute x1, starting transfers between devices, shards(): bot = lax.ppermute(lo, 'along', down)  3.33 us
    ppermute x1, starting transfers between devices, shards(): top = lax.ppermute(hi, 'along', up)  3.19 us
    ppermute x1, waiting for transfers between devices, shards(): lax.ppermute(clo, both, [(2 * i + a, 2 * j + b) for i, j in down for a, b...  3 us
    ppermute x1, starting transfers between devices, shards(): far = lax.ppermute(side, 'cross', turned)  2.82 us
  transfers between devices with their start and end apart: 5, of which 2 were waited for; matrix products, arithmetic and copies ran while one was open for 0% of the time, Pallas kernels for 0%

profile of v3, /device:TPU:1, one launch (start us, length us, event | category | flops | bytes accessed | tf_op | source)
XLA Modules:
  0.0 83.2 jit_solution(8485747046629101832)
XLA Ops:
  0.6 0.0 copy-start
  0.6 1.1 %copy-done = f32[4,32,1536]{2,1,0:T(8,128)S(1)} copy-done((f32[4,32,1536]{2,1,0:T(8,128)S(1)}, f32[4,32,1536]{2,1,0:T(8,128)}, u32[]{:S(2)}) %copy-start) | copy-done | bytes 786456
  1.8 0.0 copy-start.1
  1.8 0.9 %copy-done.1 = f32[32,1536]{1,0:T(8,128)S(1)} copy-done((f32[32,1536]{1,0:T(8,128)S(1)}, f32[32,1536]{1,0:T(8,128)}, u32[]{:S(2)}) %copy-start.1) | copy-done | bytes 196632
  2.7 0.0 copy-start.2
  2.7 0.9 %copy-done.2 = s32[32,1536]{1,0:T(8,128)S(1)} copy-done((s32[32,1536]{1,0:T(8,128)S(1)}, s32[32,1536]{1,0:T(8,128)}, u32[]{:S(2)}) %copy-start.2) | copy-done | bytes 196632
  3.6 0.0 copy-start.3
  3.6 0.9 %copy-done.3 = s32[32,1536]{1,0:T(8,128)S(1)} copy-done((s32[32,1536]{1,0:T(8,128)S(1)}, s32[32,1536]{1,0:T(8,128)}, u32[]{:S(2)}) %copy-start.3) | copy-done | bytes 196632
  4.5 0.0 copy-start.5
  4.5 0.7 copy-done.5
  5.2 0.8 shard_map.94
  6.0 3.3 %collective-permute-start.1 = (f32[7,16,1536]{2,1,0:T(8,128)S(1)}, f32[7,16,1536]{2,1,0:T(8,128)S(1)}, u32[]{:S(2)}, u32[]{:S(2)}) collective-permute-start(f32[7,16,1536]{2,1,0:T(8,128)S(1)} %get-tuple-element.17.lo), channel_id=1, source_target_pairs={{2,0},{4,2},{6,4},{8,6},{10,8},{12,10},{14,12},{16,14},{18,16},{20... | collective-permute-start | bytes 2064392 | tf_op jit(solution)/shard_map/ppermute | solution.py:574
  9.4 3.2 %collective-permute-start = (f32[7,16,1536]{2,1,0:T(8,128)S(1)}, f32[7,16,1536]{2,1,0:T(8,128)S(1)}, u32[]{:S(2)}, u32[]{:S(2)}) collective-permute-start(f32[7,16,1536]{2,1,0:T(8,128)S(1)} %get-tuple-element.18.hi), channel_id=1, source_target_pairs={{0,2},{2,4},{4,6},{6,8},{8,10},{10,12},{12,14},{14,16},{16,18},{18... | collective-permute-start | bytes 2064392 | tf_op jit(solution)/shard_map/ppermute | solution.py:573
  12.6 2.8 %collective-permute-start.2 = (f32[7,32,128]{2,1,0:T(8,128)S(1)}, f32[7,32,128]{2,1,0:T(8,128)S(1)}, u32[]{:S(2)}, u32[]{:S(2)}) collective-permute-start(f32[7,32,128]{2,1,0:T(8,128)S(1)} %get-tuple-element.19), channel_id=1, source_target_pairs={{0,1},{1,0},{2,3},{3,2},{4,5},{5,4},{6,7},{7,6},{8,9},{9,8},{10,11... | collective-permute-start | bytes 344072 | tf_op jit(solution)/shard_map/ppermute | solution.py:575
  15.4 2.6 %collective-permute-start.3 = (f32[7,16,128]{2,1,0:T(8,128)S(1)}, f32[7,16,128]{2,1,0:T(8,128)S(1)}, u32[]{:S(2)}, u32[]{:S(2)}) collective-permute-start(f32[7,16,128]{2,1,0:T(8,128)S(1)} %get-tuple-element.20), channel_id=1, source_target_pairs={{0,3},{1,2},{2,5},{3,4},{4,7},{5,6},{6,9},{7,8},{8,11},{9,10},{10,... | collective-permute-start | bytes 172040 | tf_op jit(solution)/shard_map/ppermute | solution.py:576
  18.0 4.4 %collective-permute-start.4 = (f32[7,16,128]{2,1,0:T(8,128)S(1)}, f32[7,16,128]{2,1,0:T(8,128)S(1)}, u32[]{:S(2)}, u32[]{:S(2)}) collective-permute-start(f32[7,16,128]{2,1,0:T(8,128)S(1)} %get-tuple-element.21), channel_id=1, source_target_pairs={{2,1},{3,0},{4,3},{5,2},{6,5},{7,4},{8,7},{9,6},{10,9},{11,8},{12,... | collective-permute-start | bytes 172040 | tf_op jit(solution)/shard_map/ppermute | solution.py:577
  22.4 0.5 collective-permute-done.3.ctop
  22.9 3.0 %collective-permute-done.4.cbot = f32[7,16,128]{2,1,0:T(8,128)S(1)} collective-permute-done((f32[7,16,128]{2,1,0:T(8,128)S(1)}, f32[7,16,128]{2,1,0:T(8,128)S(1)}, u32[]{:S(2)}, u32[]{:S(2)}) %collective-permute-start.4) | collective-permute-done | bytes 57376 | tf_op jit(solution)/shard_map/ppermute | solution.py:577
  25.9 0.0 collective-permute-done.2.side
  25.9 0.0 collective-permute-done.1.bot
  25.9 0.0 collective-permute-done.top
  25.9 0.0 copy-start.4
  25.9 0.7 copy-done.4
  26.6 0.0 copy-start.6
  26.6 0.7 copy-done.6
  27.3 9.2 %shard_map.95 = (f32[4,13,80,128]{3,2,1,0:T(8,128)S(1)}, f32[5,13,80,128]{3,2,1,0:T(8,128)S(1)}, f32[1,13,80,128]{3,2,1,0:T(8,128)S(1)}, f32[6,13,80,128]{3,2,1,0:T(8,128)S(1)}, f32[128,1,8]{2,1,0:T(1,128)S(1)}) custom-call(f32[7,16,1536]{2,1,0:T(8,128)S(1)} %get-tuple-element.17.lo, f32[7,16,1536]{2,1,0:T(8,128)S(1)} %get-tuple-element.18.hi, ...), custom_call_target="tpu_custom_call" | custom-call | tf_op jit(solution)/shard_map/pallas_call | solution.py:539
  36.5 22.8 %all_to_all.10.shares = f32[128,1,8]{2,1,0:T(1,128)S(1)} all-to-all(f32[128,1,8]{2,1,0:T(1,128)S(1)} %get-tuple-element.22), channel_id=1, replica_groups=mesh['along'=64,'cross'=2] {'along','cross'}, dimensions={0} | all-to-all | bytes 8192 | tf_op jit(solution)/shard_map/all_to_all | solution.py:554
  59.3 7.7 %shard_map.96 = (f32[4,13,80,128]{3,2,1,0:T(8,128)S(1)}, f32[1,13,80,128]{3,2,1,0:T(8,128)S(1)}, f32[6,13,80,128]{3,2,1,0:T(8,128)S(1)}, f32[128,1,8]{2,1,0:T(1,128)S(1)}) custom-call(f32[128,1,8]{2,1,0:T(1,128)S(1)} %all_to_all.10.shares, f32[4,13,80,128]{3,2,1,0:T(8,128)S(1)} %get-tuple-element.23.moved_in, ...), custom_call_target="tpu_custom_call" | custom-call | tf_op jit(solution)/shard_map/pallas_call | solution.py:539
  67.0 13.8 %all_to_all.11.shares = f32[128,1,8]{2,1,0:T(1,128)S(1)} all-to-all(f32[128,1,8]{2,1,0:T(1,128)S(1)} %get-tuple-element.27), channel_id=1, replica_groups=mesh['along'=64,'cross'=2] {'along','cross'}, dimensions={0} | all-to-all | bytes 8192 | tf_op jit(solution)/shard_map/all_to_all | solution.py:554
  80.8 2.4 %shard_map.97 = (f32[4,32,1536]{2,1,0:T(8,128)}, f32[32,1536]{1,0:T(8,128)}, f32[2,32,1536]{2,1,0:T(8,128)}) custom-call(f32[128,1,8]{2,1,0:T(1,128)S(1)} %all_to_all.11.shares, f32[4,13,80,128]{3,2,1,0:T(8,128)S(1)} %get-tuple-element.28.moved, f32[5,13,80,128]{3,2,1,0:T(8,128)S(1)} %get-tuple-element.24.static, ...), custom_call_target="tpu_custom_call" | custom-call | tf_op jit(solution)/shard_map/pallas_call | solution.py:539
Async XLA Ops:
  0.6 1.1 %copy-start = (f32[4,32,1536]{2,1,0:T(8,128)S(1)}, f32[4,32,1536]{2,1,0:T(8,128)}, u32[]{:S(2)}) copy-start(f32[4,32,1536]{2,1,0:T(8,128)} %vel.1) | copy-start | bytes 2359300
  1.8 0.9 %copy-start.1 = (f32[32,1536]{1,0:T(8,128)S(1)}, f32[32,1536]{1,0:T(8,128)}, u32[]{:S(2)}) copy-start(f32[32,1536]{1,0:T(8,128)} %surface.1) | copy-start | bytes 589828
  2.7 0.9 %copy-start.2 = (s32[32,1536]{1,0:T(8,128)S(1)}, s32[32,1536]{1,0:T(8,128)}, u32[]{:S(2)}) copy-start(s32[32,1536]{1,0:T(8,128)} %wet.1) | copy-start | bytes 589828
  3.6 0.9 %copy-start.3 = (s32[32,1536]{1,0:T(8,128)S(1)}, s32[32,1536]{1,0:T(8,128)}, u32[]{:S(2)}) copy-start(s32[32,1536]{1,0:T(8,128)} %bathy.1) | copy-start | bytes 589828
  4.5 0.7 copy-start.5
  6.0 19.9 %collective-permute-start.1 = (f32[7,16,1536]{2,1,0:T(8,128)S(1)}, f32[7,16,1536]{2,1,0:T(8,128)S(1)}, u32[]{:S(2)}, u32[]{:S(2)}) collective-permute-start(f32[7,16,1536]{2,1,0:T(8,128)S(1)} %get-tuple-element.17.lo), channel_id=1, source_target_pairs={{2,0},{4,2},{6,4},{8,6},{10,8},{12,10},{14,12},{16,14},{18,16},{20... | collective-permute-start | bytes 2064392 | tf_op jit(solution)/shard_map/ppermute | solution.py:574
  9.4 16.6 %collective-permute-start = (f32[7,16,1536]{2,1,0:T(8,128)S(1)}, f32[7,16,1536]{2,1,0:T(8,128)S(1)}, u32[]{:S(2)}, u32[]{:S(2)}) collective-permute-start(f32[7,16,1536]{2,1,0:T(8,128)S(1)} %get-tuple-element.18.hi), channel_id=1, source_target_pairs={{0,2},{2,4},{4,6},{6,8},{8,10},{10,12},{12,14},{14,16},{16,18},{18... | collective-permute-start | bytes 2064392 | tf_op jit(solution)/shard_map/ppermute | solution.py:573
  12.6 13.4 %collective-permute-start.2 = (f32[7,32,128]{2,1,0:T(8,128)S(1)}, f32[7,32,128]{2,1,0:T(8,128)S(1)}, u32[]{:S(2)}, u32[]{:S(2)}) collective-permute-start(f32[7,32,128]{2,1,0:T(8,128)S(1)} %get-tuple-element.19), channel_id=1, source_target_pairs={{0,1},{1,0},{2,3},{3,2},{4,5},{5,4},{6,7},{7,6},{8,9},{9,8},{10,11... | collective-permute-start | bytes 344072 | tf_op jit(solution)/shard_map/ppermute | solution.py:575
  15.4 7.5 %collective-permute-start.3 = (f32[7,16,128]{2,1,0:T(8,128)S(1)}, f32[7,16,128]{2,1,0:T(8,128)S(1)}, u32[]{:S(2)}, u32[]{:S(2)}) collective-permute-start(f32[7,16,128]{2,1,0:T(8,128)S(1)} %get-tuple-element.20), channel_id=1, source_target_pairs={{0,3},{1,2},{2,5},{3,4},{4,7},{5,6},{6,9},{7,8},{8,11},{9,10},{10,... | collective-permute-start | bytes 172040 | tf_op jit(solution)/shard_map/ppermute | solution.py:576
  18.0 7.9 %collective-permute-start.4 = (f32[7,16,128]{2,1,0:T(8,128)S(1)}, f32[7,16,128]{2,1,0:T(8,128)S(1)}, u32[]{:S(2)}, u32[]{:S(2)}) collective-permute-start(f32[7,16,128]{2,1,0:T(8,128)S(1)} %get-tuple-element.21), channel_id=1, source_target_pairs={{2,1},{3,0},{4,3},{5,2},{6,5},{7,4},{8,7},{9,6},{10,9},{11,8},{12,... | collective-permute-start | bytes 172040 | tf_op jit(solution)/shard_map/ppermute | solution.py:577
  25.9 0.7 copy-start.4
  26.6 0.7 copy-start.6

commit v4 on v3

--- a/solution.py
+++ b/solution.py
@@ -20,6 +20,10 @@
 TILE = 8
 GUARD = 8
 HALO = 16
+FIELDS = 7
+SENT = (13, 13, 13, 13, 12, 11, 11)
+OFFSETS = (0, 13, 26, 39, 52, 64, 75)
+SENT_ROWS = 88
 VMEM_BYTES = 24 * 1024 * 1024
 
 
@@ -250,42 +254,66 @@
     put_moments(moments, moments_of(shape, krylov, static))
 
 
-def pack_kernel(shape, vel, surface, wet, bathy, table, lo, hi, side, clo, chi):
+def pack_kernel(
+    shape, vel_in, surface_in, wet_in, bathy_in, table_in,
+    own, side, lo, hi, clo, chi,
+    vel, surface, wet, bathy, table, arrived,
+):
+    copies = [
+        pltpu.make_async_copy(source, target, arrived.at[number])
+        for number, (source, target) in enumerate(
+            (
+                (table_in, table),
+                (bathy_in, bathy),
+                (wet_in, wet),
+                (surface_in, surface),
+                (vel_in, vel),
+            )
+        )
+    ]
+    for copy in copies:
+        copy.start()
     half = lax.axis_index("cross")
     lane = lanes_of()
-    for t in range(shape.rows // TILE):
-        rows = pl.ds(t * TILE, TILE)
-        target, corner = (lo, clo) if t * TILE < HALO else (hi, chi)
-        at = pl.ds(t * TILE % HALO, TILE)
+    for copy in copies:
+        copy.wait()
+
+    def turn(number, carry):
+        rows = pl.ds(pl.multiple_of(number * TILE, TILE), TILE)
         edges = []
         for c in range(shape.own):
             cols = pl.ds(c * LANES, LANES)
             flag = wet[rows, cols]
-            number = bathy[rows, cols]
+            entry = bathy[rows, cols]
             thick = jnp.zeros((TILE, LANES), jnp.float32)
-            for entry in range(CLASSES):
-                thick = jnp.where(number == entry, 0.5 * table[entry], thick)
+            for choice in range(CLASSES):
+                thick = jnp.where(entry == choice, 0.5 * table[choice], thick)
             values = [jnp.where(flag > 0, vel[k, rows, cols], 0.0) for k in range(4)]
             values += [surface[rows, cols], flag.astype(jnp.float32), thick]
             for k, value in enumerate(values):
-                target[k, at, cols] = value
+                own[k, c, rows, :] = value
             if c in (0, shape.own - 1):
                 edges.append(values)
-        for k in range(7):
-            value = jnp.where(
+        for k in range(FIELDS):
+            side[k, 0, rows, :] = jnp.where(
                 half == 0,
                 jnp.where(lane >= LANES // 2, edges[1][k], 0.0),
                 jnp.where(lane < LANES // 2, edges[0][k], 0.0),
             )
-            side[k, rows, :] = value
-            corner[k, at, :] = value
-
-
-def first_kernel(
-    shape, lo, hi, top, bot, side, ctop, cbot, ranges, heads,
-    moved, static, surface, krylov, moments,
-    vel, potential, thick, columns,
-):
+        return carry
+
+    lax.fori_loop(0, shape.rows // TILE, turn, 0)
+    for source, first, last, chunks in ((own, lo, hi, shape.own), (side, clo, chi, 1)):
+        for c in range(chunks):
+            for k in range(FIELDS):
+                for part in (0, SENT[k] - TILE):
+                    to = pl.ds(OFFSETS[k] + part, TILE)
+                    first[c, to, :] = source[k, c, pl.ds(part, TILE), :]
+                    start = shape.rows - SENT[k] + part
+                    last[c, to, :] = source[k, c, pl.ds(start, TILE), :]
+
+
+def head_kernel(shape, ranges, heads, head, columns):
     along = lax.axis_index("along")
     half = lax.axis_index("cross")
     lane = lanes_of()
@@ -298,43 +326,67 @@
         for s in range(SHIPS):
             inside = jnp.logical_and(index >= ranges[2, s], index < ranges[3, s])
             columns[s, c] = jnp.where(inside, gravity * heads[s], 0.0)
-    pieces = [(GUARD, top, ctop, 0), (shape.first, lo, side, 0)]
-    pieces += [(shape.first + HALO, hi, side, HALO), (shape.first + shape.rows, bot, cbot, 0)]
-    for base, wide, narrow, offset in pieces:
-
-        def turn(number, carry, base=base, wide=wide, narrow=narrow, offset=offset):
-            at = pl.multiple_of(number * TILE, TILE)
-            row = base + number * TILE
-            global_row = along * shape.rows + (row - shape.first) + line
-            covered = [
-                jnp.logical_and(global_row >= ranges[0, s], global_row < ranges[1, s])
-                for s in range(SHIPS)
-            ]
+
+    def head_rows(row):
+        global_row = along * shape.rows + (row - shape.first) + line
+        covered = [
+            jnp.logical_and(global_row >= ranges[0, s], global_row < ranges[1, s])
+            for s in range(SHIPS)
+        ]
+        for c in range(shape.chunks):
+            value = jnp.zeros((TILE, LANES), jnp.float32)
+            for s in range(SHIPS):
+                value = value + jnp.where(covered[s], columns[s, c], 0.0)
+            store(head, 0, c, row, value)
+
+    sweep(GUARD, shape.total // TILE - 2, head_rows)
+
+
+def first_kernel(
+    shape, own, side, top, bot, ctop, cbot, head,
+    moved, static, surface, krylov, moments,
+    vel, potential, thick,
+):
+    along = lax.axis_index("along")
+    lane = lanes_of()
+
+    def place(c, row, values):
+        for k in range(4):
+            store(vel, k, c, row, values[k])
+        depth = values[6]
+        inside = depth > 0.0
+        ship = jnp.where(inside, load(head, 0, c, row), 0.0)
+        store(surface, 0, c, row, values[4])
+        store(potential, 0, c, row, gravity * values[4] + ship)
+        store(thick, 0, c, row, depth)
+        store(static, CONDUCT, c, row, values[5] * depth)
+        store(static, HALF_RATE, c, row, 0.5 / jnp.where(inside, depth, 1.0))
+        store(static, HEAD, c, row, ship)
+
+    def own_rows(number, carry):
+        at = number * TILE
+        for c in range(shape.chunks):
+            source, chunk = (own, c) if c < shape.own else (side, 0)
+            values = [load(source, k, chunk, at) for k in range(FIELDS)]
+            place(c, shape.first + at, values)
+        return carry
+
+    lax.fori_loop(0, shape.rows // TILE, own_rows, 0)
+    deepest = SENT[0]
+    for wide, narrow, keep, starts in (
+        (top, ctop, along > 0, (-deepest, -TILE)),
+        (bot, cbot, along < lax.axis_size("along") - 1, (0, deepest - TILE)),
+    ):
+        for start in starts:
             for c in range(shape.chunks):
-                if c < shape.own:
-                    values = [
-                        wide[k, pl.ds(at, TILE), pl.ds(c * LANES, LANES)] for k in range(7)
-                    ]
-                else:
-                    values = [narrow[k, pl.ds(offset + at, TILE), :] for k in range(7)]
-                for k in range(4):
-                    store(vel, k, c, row, values[k])
-                depth = values[6]
-                inside = depth > 0.0
-                depth = jnp.where(inside, depth, 1.0)
-                head = jnp.zeros((TILE, LANES), jnp.float32)
-                for s in range(SHIPS):
-                    head = head + jnp.where(covered[s], columns[s, c], 0.0)
-                head = jnp.where(inside, head, 0.0)
-                store(surface, 0, c, row, values[4])
-                store(potential, 0, c, row, gravity * values[4] + head)
-                store(thick, 0, c, row, values[6])
-                store(static, CONDUCT, c, row, values[5] * values[6])
-                store(static, HALF_RATE, c, row, 0.5 / depth)
-                store(static, HEAD, c, row, head)
-            return carry
-
-        lax.fori_loop(0, HALO // TILE, turn, 0)
+                source, chunk = (wide, c) if c < shape.own else (narrow, 0)
+                values = []
+                for k in range(FIELDS):
+                    at = OFFSETS[k] + (start if start > 0 or starts[0] == 0 else SENT[k] + start)
+                    value = source[chunk, pl.ds(at, TILE), :]
+                    values.append(jnp.where(keep, value, 0.0))
+                base = shape.first + (shape.rows if starts[0] == 0 else 0)
+                place(c, base + start, values)
 
     def diagonal_rows(row):
         sides = {}
@@ -358,10 +410,10 @@
             ring.done(c)
 
     start = GUARD
-    sweep(start + 4, 7, diagonal_rows)
+    sweep(start + 5, 7, diagonal_rows)
     project(
         shape, vel, potential, static, moved, krylov, moments,
-        (start + 4, start + 5, start + 6, start + 7), (7, 7, 7, 7),
+        (start + 5, start + 6, start + 7, start + 8), (7, 7, 7, 6),
     )
 
 
@@ -460,9 +512,9 @@
 ):
     factors = coefficients(shares)
     start = GUARD
-    sweep(start + 7, 7, functools.partial(pressure_rows, shape, factors, krylov_in, pressure))
+    sweep(start + 8, 6, functools.partial(pressure_rows, shape, factors, krylov_in, pressure))
     sweep(
-        start + 8,
+        start + 9,
         6,
         functools.partial(
             move_rows, shape, moved_in, pressure, static, flux, functools.partial(store, vel)
@@ -475,7 +527,7 @@
         store(potential, 0, c, row, gravity * value + load(static, HEAD, c, row))
 
     sweep(
-        start + 9,
+        start + 10,
         6,
         functools.partial(surface_rows, shape, surface_in, flux, shape.chunks, put),
     )
@@ -534,14 +586,14 @@
     )
 
 
-def call(kernel, shape, kinds, outs, scratch, operands):
-    f32 = jnp.float32
+def call(kernel, shape, kinds, outs, scratch, operands, cost=None):
     return pl.pallas_call(
         functools.partial(kernel, shape),
         out_shape=outs,
         in_specs=[pl.BlockSpec(memory_space=kind) for kind in kinds],
         out_specs=[pl.BlockSpec(memory_space=pltpu.VMEM)] * len(outs),
-        scratch_shapes=[pltpu.VMEM(s, f32) for s in scratch],
+        scratch_shapes=scratch,
+        cost_estimate=cost,
         compiler_params=pltpu.CompilerParams(vmem_limit_bytes=VMEM_BYTES),
     )(*operands)
 
@@ -557,17 +609,31 @@
 def shards(velocity, surface, wet_mask, bathy_class, depth_table, hull_ranges, hull_pressure):
     shape = Shape(*surface.shape)
     vmem, smem = pltpu.VMEM, pltpu.SMEM
-    cols = surface.shape[1]
-    wide, narrow = (7, HALO, cols), (7, HALO, LANES)
-    lo, hi, side, clo, chi = call(
-        pack_kernel, shape, [vmem] * 4 + [smem],
-        [pltpu.VMEM(each, jnp.float32) for each in (wide, wide, (7, shape.rows, LANES), narrow, narrow)],
-        [],
-        (velocity, surface, wet_mask, bathy_class, depth_table),
-    )
+    f32, i32 = jnp.float32, jnp.int32
     size = lax.axis_size("along")
+    field = (shape.chunks, shape.total, LANES)
+    fields = lambda count: vmem((count,) + field, f32)
+    sums = jax.ShapeDtypeStruct((2 * size, 1, 8), f32)
+    block = surface.shape
+    wide, narrow = vmem((shape.own, SENT_ROWS, LANES), f32), vmem((1, SENT_ROWS, LANES), f32)
+    own, side, lo, hi, clo, chi = call(
+        pack_kernel, shape, [pl.ANY] * 5,
+        [
+            vmem((FIELDS, shape.own, shape.rows, LANES), f32),
+            vmem((FIELDS, 1, shape.rows, LANES), f32),
+            wide, wide, narrow, narrow,
+        ],
+        [
+            vmem(velocity.shape, f32), vmem(block, f32), vmem(block, i32), vmem(block, i32),
+            smem(depth_table.shape, f32), pltpu.SemaphoreType.DMA((5,)),
+        ],
+        tuple(
+            pltpu.with_memory_space_constraint(x, pltpu.HBM)
+            for x in (velocity, surface, wet_mask, bathy_class, depth_table)
+        ),
+    )
     both = ("along", "cross")
-    up = [(i, i + 1) for i in range(size - 1)]
+    up = [(i, (i + 1) % size) for i in range(size)]
     down = [(j, i) for i, j in up]
     turned = [(0, 1), (1, 0)]
     top = lax.ppermute(hi, "along", up)
@@ -575,21 +641,21 @@
     far = lax.ppermute(side, "cross", turned)
     ctop = lax.ppermute(chi, both, [(2 * i + a, 2 * j + b) for i, j in up for a, b in turned])
     cbot = lax.ppermute(clo, both, [(2 * i + a, 2 * j + b) for i, j in down for a, b in turned])
-
-    field = (shape.chunks, shape.total, LANES)
-    f32 = jnp.float32
-    fields = lambda count: (count,) + field
-    kept = lambda count: pltpu.VMEM(fields(count), f32)
-    sums = jax.ShapeDtypeStruct((2 * size, 1, 8), f32)
+    (head,) = call(
+        head_kernel, shape, [smem] * 2, [fields(1)],
+        [vmem((SHIPS, shape.chunks, TILE, LANES), f32)],
+        (hull_ranges.T, hull_pressure),
+        pl.CostEstimate(flops=2 * 10**6, bytes_accessed=10**6, transcendentals=0),
+    )
     moved, static, level, krylov, moments = call(
-        first_kernel, shape, [vmem] * 7 + [smem] * 2,
-        [kept(4), kept(5), kept(1), kept(6), sums],
-        [fields(4), fields(1), fields(1), (SHIPS, shape.chunks, TILE, LANES)],
-        held(lo, hi, top, bot, far, ctop, cbot) + (hull_ranges.T, hull_pressure),
+        first_kernel, shape, [vmem] * 7,
+        [fields(4), fields(5), fields(1), fields(6), sums],
+        [fields(4), fields(1), fields(1)],
+        held(own, far, top, bot, ctop, cbot, head),
     )
     moved, level, krylov, moments = call(
         second_kernel, shape, [vmem] * 5,
-        [kept(4), kept(1), kept(6), sums],
+        [fields(4), fields(1), fields(6), sums],
         [fields(4), fields(1), fields(2), fields(2)],
         (shared(moments),) + held(moved, static, level, krylov),
     )

time: 83.6 us -> 72.5 us (0.87)
  blocking collectives: 36.6 us -> 31.3 us
  starting transfers between devices: 16.4 us -> 11.6 us
  local copies, waits for them, and re-layouts: 5.89 us -> 1.34 us
  waiting for transfers between devices: 3.46 us -> 6.14 us
  Pallas kernels: 20.1 us -> 21.3 us
    ppermute x1, waiting for transfers between devices: 0.45 us -> 6.13 us  [shards(): lax.ppermute(chi, both, [(2 * i + a, 2 * j + b) for i, j in up for a, b i...]
    all_to_all x2, blocking collectives: 36.6 us -> 31.3 us  [shared(): return lax.all_to_all(moments, ('along', 'cross'), 0, 0, tiled=True)]
    unnamed x14 -> x4, local copies, waits for them, and re-layouts: 5.89 us -> 1.34 us
    ppermute x1, starting transfers between devices: 3.33 us -> 0.01 us  [shards(): bot = lax.ppermute(lo, 'along', down)]
    ppermute x1, waiting for transfers between devices: 3 us -> 0.01 us  [shards(): lax.ppermute(clo, both, [(2 * i + a, 2 * j + b) for i, j in down for a, b...]
    pallas_call x4 -> x5, Pallas kernels: 20.1 us -> 21.3 us  [call(): pl.pallas_call(functools.partial(kernel, shape), out_shape=outs, in_specs...]
  transfers between devices with their start and end apart: 5 -> 5, of which waited for: 2 -> 1; matrix products, arithmetic and copies ran while one was open for 0% -> 0% of each run, Pallas kernels for 0% -> 1%
where the time goes in v4:
time: 72.5 us; the launch traced here: 72.3 us
  blocking collectives  31.3 us (43%)
  Pallas kernels  21.3 us (29%)
  starting transfers between devices  11.6 us (16%)
  waiting for transfers between devices  6.14 us (8%)
  local copies, waits for them, and re-layouts  1.34 us (2%)
    all_to_all x2, blocking collectives, shared(): return lax.all_to_all(moments, ('along', 'cross'), 0, 0, tiled=True)  31.3 us
    pallas_call x5, Pallas kernels, call(): pl.pallas_call(functools.partial(kernel, shape), out_shape=outs, in_specs...  21.3 us
    ppermute x1, waiting for transfers between devices, shards(): lax.ppermute(chi, both, [(2 * i + a, 2 * j + b) for i, j in up for a, b i...  6.13 us
    ppermute x1, starting transfers between devices, shards(): lax.ppermute(clo, both, [(2 * i + a, 2 * j + b) for i, j in down for a, b...  4.18 us
    ppermute x1, starting transfers between devices, shards(): top = lax.ppermute(hi, 'along', up)  2.76 us
    ppermute x1, starting transfers between devices, shards(): far = lax.ppermute(side, 'cross', turned)  2.74 us
    ppermute x1, starting transfers between devices, shards(): lax.ppermute(chi, both, [(2 * i + a, 2 * j + b) for i, j in up for a, b i...  1.97 us
  transfers between devices with their start and end apart: 5, of which 1 were waited for; matrix products, arithmetic and copies ran while one was open for 0% of the time, Pallas kernels for 1%

profile of v4, /device:TPU:1, one launch (start us, length us, event | category | flops | bytes accessed | tf_op | source)
XLA Modules:
  0.0 72.3 jit_solution(880531989428200203)
XLA Ops:
  0.6 1.9 %shard_map.94 = (f32[7,12,32,128]{3,2,1,0:T(8,128)S(1)}, f32[7,1,32,128]{3,2,1,0:T(8,128)S(1)}, f32[12,88,128]{2,1,0:T(8,128)S(1)}, f32[12,88,128]{2,1,0:T(8,128...) custom-call(f32[4,32,1536]{2,1,0:T(8,128)} %vel_in.1, f32[32,1536]{1,0:T(8,128)} %surface_in.1, ...), custom_call_target="tpu_custom_call" | custom-call | tf_op jit(solution)/shard_map/pallas_call | solution.py:590
  2.5 2.8 %collective-permute-start.1 = (f32[12,88,128]{2,1,0:T(8,128)S(1)}, f32[12,88,128]{2,1,0:T(8,128)S(1)}, u32[]{:S(2)}, u32[]{:S(2)}) collective-permute-start(f32[12,88,128]{2,1,0:T(8,128)S(1)} %get-tuple-element.20), channel_id=1, source_target_pairs={{0,2},{2,4},{4,6},{6,8},{8,10},{10,12},{12,14},{14,16},{16,18},{18... | collective-permute-start | bytes 1622024 | tf_op jit(solution)/shard_map/ppermute | solution.py:639
  5.3 0.0 collective-permute-start.2
  5.3 2.7 %collective-permute-start = (f32[7,1,32,128]{3,2,1,0:T(8,128)S(1)}, f32[7,1,32,128]{3,2,1,0:T(8,128)S(1)}, u32[]{:S(2)}, u32[]{:S(2)}) collective-permute-start(f32[7,1,32,128]{3,2,1,0:T(8,128)S(1)} %get-tuple-element.19), channel_id=1, source_target_pairs={{0,1},{1,0},{2,3},{3,2},{4,5},{5,4},{6,7},{7,6},{8,9},{9,8},{10,11... | collective-permute-start | bytes 344072 | tf_op jit(solution)/shard_map/ppermute | solution.py:641
  8.0 2.0 %collective-permute-start.3 = (f32[1,88,128]{2,1,0:T(8,128)S(1)}, f32[1,88,128]{2,1,0:T(8,128)S(1)}, u32[]{:S(2)}, u32[]{:S(2)}) collective-permute-start(f32[1,88,128]{2,1,0:T(8,128)S(1)} %get-tuple-element.22), channel_id=1, source_target_pairs={{0,3},{1,2},{2,5},{3,4},{4,7},{5,6},{6,9},{7,8},{8,11},{9,10},{10,... | collective-permute-start | bytes 135176 | tf_op jit(solution)/shard_map/ppermute | solution.py:642
  10.0 4.2 %collective-permute-start.4 = (f32[1,88,128]{2,1,0:T(8,128)S(1)}, f32[1,88,128]{2,1,0:T(8,128)S(1)}, u32[]{:S(2)}, u32[]{:S(2)}) collective-permute-start(f32[1,88,128]{2,1,0:T(8,128)S(1)} %get-tuple-element.23), channel_id=1, source_target_pairs={{2,1},{3,0},{4,3},{5,2},{6,5},{7,4},{8,7},{9,6},{10,9},{11,8},{12,... | collective-permute-start | bytes 135176 | tf_op jit(solution)/shard_map/ppermute | solution.py:643
  14.2 0.0 copy-start
  14.2 0.7 copy-done
  14.9 0.0 copy-start.1
  14.9 0.7 copy-done.1
  15.5 1.0 %shard_map.95.head = f32[1,13,80,128]{3,2,1,0:T(8,128)S(1)} custom-call(s32[4,8]{1,0:T(4,128)S(1)} %bitcast.1, f32[8]{0:T(128)S(1)} %copy-done.1), custom_call_target="tpu_custom_call" | custom-call | flops 2000000 | bytes 1000000 | tf_op jit(solution)/shard_map/pallas_call | solution.py:590
  16.5 6.1 %collective-permute-done.3.ctop = f32[1,88,128]{2,1,0:T(8,128)S(1)} collective-permute-done((f32[1,88,128]{2,1,0:T(8,128)S(1)}, f32[1,88,128]{2,1,0:T(8,128)S(1)}, u32[]{:S(2)}, u32[]{:S(2)}) %collective-permute-start.3) | collective-permute-done | bytes 45088 | tf_op jit(solution)/shard_map/ppermute | solution.py:642
  22.6 0.0 collective-permute-done.4.cbot
  22.6 0.0 collective-permute-done.side
  22.6 0.0 collective-permute-done.1.top
  22.6 0.0 collective-permute-done.2.bot
  22.6 8.3 %shard_map.96 = (f32[4,13,80,128]{3,2,1,0:T(8,128)S(1)}, f32[5,13,80,128]{3,2,1,0:T(8,128)S(1)}, f32[1,13,80,128]{3,2,1,0:T(8,128)S(1)}, f32[6,13,80,128]{3,2,1,0:T(8,128)S(1)}, f32[128,1,8]{2,1,0:T(1,128)S(1)}) custom-call(f32[7,12,32,128]{3,2,1,0:T(8,128)S(1)} %get-tuple-element.18.own, f32[7,1,32,128]{3,2,1,0:T(8,128)S(1)} %collective-permute-done.side, ...), custom_call_target="tpu_custom_call" | custom-call | tf_op jit(solution)/shard_map/pallas_call | solution.py:590
  30.9 17.5 %all_to_all.10.shares = f32[128,1,8]{2,1,0:T(1,128)S(1)} all-to-all(f32[128,1,8]{2,1,0:T(1,128)S(1)} %get-tuple-element.24), channel_id=1, replica_groups=mesh['along'=64,'cross'=2] {'along','cross'}, dimensions={0} | all-to-all | bytes 8192 | tf_op jit(solution)/shard_map/all_to_all | solution.py:606
  48.4 7.7 %shard_map.97 = (f32[4,13,80,128]{3,2,1,0:T(8,128)S(1)}, f32[1,13,80,128]{3,2,1,0:T(8,128)S(1)}, f32[6,13,80,128]{3,2,1,0:T(8,128)S(1)}, f32[128,1,8]{2,1,0:T(1,128)S(1)}) custom-call(f32[128,1,8]{2,1,0:T(1,128)S(1)} %all_to_all.10.shares, f32[4,13,80,128]{3,2,1,0:T(8,128)S(1)} %get-tuple-element.25.moved_in, ...), custom_call_target="tpu_custom_call" | custom-call | tf_op jit(solution)/shard_map/pallas_call | solution.py:590
  56.1 13.8 %all_to_all.11.shares = f32[128,1,8]{2,1,0:T(1,128)S(1)} all-to-all(f32[128,1,8]{2,1,0:T(1,128)S(1)} %get-tuple-element.29), channel_id=1, replica_groups=mesh['along'=64,'cross'=2] {'along','cross'}, dimensions={0} | all-to-all | bytes 8192 | tf_op jit(solution)/shard_map/all_to_all | solution.py:606
  69.9 2.4 %shard_map.98 = (f32[4,32,1536]{2,1,0:T(8,128)}, f32[32,1536]{1,0:T(8,128)}, f32[2,32,1536]{2,1,0:T(8,128)}) custom-call(f32[128,1,8]{2,1,0:T(1,128)S(1)} %all_to_all.11.shares, f32[4,13,80,128]{3,2,1,0:T(8,128)S(1)} %get-tuple-element.30.moved, f32[5,13,80,128]{3,2,1,0:T(8,128)S(1)} %get-tuple-element.26.static, ...), custom_call_target="tpu_custom_call" | custom-call | tf_op jit(solution)/shard_map/pallas_call | solution.py:590
Async XLA Ops:
  2.5 20.1 %collective-permute-start.1 = (f32[12,88,128]{2,1,0:T(8,128)S(1)}, f32[12,88,128]{2,1,0:T(8,128)S(1)}, u32[]{:S(2)}, u32[]{:S(2)}) collective-permute-start(f32[12,88,128]{2,1,0:T(8,128)S(1)} %get-tuple-element.20), channel_id=1, source_target_pairs={{0,2},{2,4},{4,6},{6,8},{8,10},{10,12},{12,14},{14,16},{16,18},{18... | collective-permute-start | bytes 1622024 | tf_op jit(solution)/shard_map/ppermute | solution.py:639
  5.3 17.3 %collective-permute-start.2 = (f32[12,88,128]{2,1,0:T(8,128)S(1)}, f32[12,88,128]{2,1,0:T(8,128)S(1)}, u32[]{:S(2)}, u32[]{:S(2)}) collective-permute-start(f32[12,88,128]{2,1,0:T(8,128)S(1)} %get-tuple-element.21), channel_id=1, source_target_pairs={{2,0},{4,2},{6,4},{8,6},{10,8},{12,10},{14,12},{16,14},{18,16},{20... | collective-permute-start | bytes 1622024 | tf_op jit(solution)/shard_map/ppermute | solution.py:640
  5.3 17.3 %collective-permute-start = (f32[7,1,32,128]{3,2,1,0:T(8,128)S(1)}, f32[7,1,32,128]{3,2,1,0:T(8,128)S(1)}, u32[]{:S(2)}, u32[]{:S(2)}) collective-permute-start(f32[7,1,32,128]{3,2,1,0:T(8,128)S(1)} %get-tuple-element.19), channel_id=1, source_target_pairs={{0,1},{1,0},{2,3},{3,2},{4,5},{5,4},{6,7},{7,6},{8,9},{9,8},{10,11... | collective-permute-start | bytes 344072 | tf_op jit(solution)/shard_map/ppermute | solution.py:641
  8.0 14.6 %collective-permute-start.3 = (f32[1,88,128]{2,1,0:T(8,128)S(1)}, f32[1,88,128]{2,1,0:T(8,128)S(1)}, u32[]{:S(2)}, u32[]{:S(2)}) collective-permute-start(f32[1,88,128]{2,1,0:T(8,128)S(1)} %get-tuple-element.22), channel_id=1, source_target_pairs={{0,3},{1,2},{2,5},{3,4},{4,7},{5,6},{6,9},{7,8},{8,11},{9,10},{10,... | collective-permute-start | bytes 135176 | tf_op jit(solution)/shard_map/ppermute | solution.py:642
  10.0 12.6 %collective-permute-start.4 = (f32[1,88,128]{2,1,0:T(8,128)S(1)}, f32[1,88,128]{2,1,0:T(8,128)S(1)}, u32[]{:S(2)}, u32[]{:S(2)}) collective-permute-start(f32[1,88,128]{2,1,0:T(8,128)S(1)} %get-tuple-element.23), channel_id=1, source_target_pairs={{2,1},{3,0},{4,3},{5,2},{6,5},{7,4},{8,7},{9,6},{10,9},{11,8},{12,... | collective-permute-start | bytes 135176 | tf_op jit(solution)/shard_map/ppermute | solution.py:643
  14.2 0.7 copy-start
  14.9 0.7 copy-start.1

commit v5 on v4

--- a/solution.py
+++ b/solution.py
@@ -24,6 +24,8 @@
 SENT = (13, 13, 13, 13, 12, 11, 11)
 OFFSETS = (0, 13, 26, 39, 52, 64, 75)
 SENT_ROWS = 88
+EDGE = 16
+SLOTS = LANES // EDGE
 VMEM_BYTES = 24 * 1024 * 1024
 
 
@@ -256,8 +258,8 @@
 
 def pack_kernel(
     shape, vel_in, surface_in, wet_in, bathy_in, table_in,
-    own, side, lo, hi, clo, chi,
-    vel, surface, wet, bathy, table, arrived,
+    own, lo, hi, side, clo, chi,
+    vel, surface, wet, bathy, table, edge, arrived,
 ):
     copies = [
         pltpu.make_async_copy(source, target, arrived.at[number])
@@ -295,22 +297,56 @@
             if c in (0, shape.own - 1):
                 edges.append(values)
         for k in range(FIELDS):
-            side[k, 0, rows, :] = jnp.where(
-                half == 0,
-                jnp.where(lane >= LANES // 2, edges[1][k], 0.0),
-                jnp.where(lane < LANES // 2, edges[0][k], 0.0),
-            )
+            edge[k, rows, :] = jnp.where(half == 0, edges[1][k], edges[0][k])
         return carry
 
     lax.fori_loop(0, shape.rows // TILE, turn, 0)
-    for source, first, last, chunks in ((own, lo, hi, shape.own), (side, clo, chi, 1)):
-        for c in range(chunks):
-            for k in range(FIELDS):
-                for part in (0, SENT[k] - TILE):
-                    to = pl.ds(OFFSETS[k] + part, TILE)
-                    first[c, to, :] = source[k, c, pl.ds(part, TILE), :]
-                    start = shape.rows - SENT[k] + part
-                    last[c, to, :] = source[k, c, pl.ds(start, TILE), :]
+    for c in range(shape.own):
+        for k in range(FIELDS):
+            for part in (0, SENT[k] - TILE):
+                to = pl.ds(OFFSETS[k] + part, TILE)
+                lo[c, to, :] = own[k, c, pl.ds(part, TILE), :]
+                hi[c, to, :] = own[k, c, pl.ds(shape.rows - SENT[k] + part, TILE), :]
+    shift = jnp.where(half == 0, EDGE, 0)
+    squeeze(side, side_tiles(shape, edge), shift)
+    squeeze(clo, corner_tiles(edge, 0), shift)
+    squeeze(chi, corner_tiles(edge, shape.rows), shift)
+
+
+def side_tiles(shape, edge):
+    return [
+        edge.at[k, pl.ds(row, TILE), :] for k in range(FIELDS) for row in range(0, shape.rows, TILE)
+    ]
+
+
+def corner_parts():
+    return [(k, part) for k in range(FIELDS) for part in (0, SENT[k] - TILE)]
+
+
+def corner_tiles(edge, rows):
+    return [
+        edge.at[k, pl.ds(part + (rows - SENT[k] if rows else 0), TILE), :]
+        for k, part in corner_parts()
+    ]
+
+
+def squeeze(out, tiles, shift):
+    slot = lanes_of() // EDGE
+    for first in range(0, len(tiles), SLOTS):
+        value = jnp.zeros((TILE, LANES), jnp.float32)
+        for number, tile in enumerate(tiles[first : first + SLOTS]):
+            moved = pltpu.roll(tile[...], lax.rem(EDGE * number + shift, LANES), 1)
+            value = jnp.where(slot == number, moved, value)
+        out[pl.ds(first, TILE), :] = value
+
+
+def spread(source, number, half):
+    lane = lanes_of()
+    tile = source[pl.ds(number // SLOTS * TILE, TILE), :]
+    amount = LANES - EDGE * (number % SLOTS) - jnp.where(half == 0, 0, EDGE)
+    moved = pltpu.roll(tile, lax.rem(amount + LANES, LANES), 1)
+    wanted = jnp.where(half == 0, lane, LANES - 1 - lane) < EDGE
+    return jnp.where(wanted, moved, 0.0)
 
 
 def head_kernel(shape, ranges, heads, head, columns):
@@ -343,11 +379,18 @@
 
 
 def first_kernel(
-    shape, own, side, top, bot, ctop, cbot, head,
+    shape, own, side_in, top, bot, ctop_in, cbot_in, head,
     moved, static, surface, krylov, moments,
-    vel, potential, thick,
+    vel, potential, thick, side, ctop, cbot,
 ):
     along = lax.axis_index("along")
+    half = lax.axis_index("cross")
+    for number, tile in enumerate(side_tiles(shape, side)):
+        tile[...] = spread(side_in, number, half)
+    for number, (k, part) in enumerate(corner_parts()):
+        to = pl.ds(OFFSETS[k] + part, TILE)
+        ctop[0, to, :] = spread(ctop_in, number, half)
+        cbot[0, to, :] = spread(cbot_in, number, half)
     lane = lanes_of()
 
     def place(c, row, values):
@@ -366,8 +409,10 @@
     def own_rows(number, carry):
         at = number * TILE
         for c in range(shape.chunks):
-            source, chunk = (own, c) if c < shape.own else (side, 0)
-            values = [load(source, k, chunk, at) for k in range(FIELDS)]
+            if c < shape.own:
+                values = [load(own, k, c, at) for k in range(FIELDS)]
+            else:
+                values = [side[k, pl.ds(at, TILE), :] for k in range(FIELDS)]
             place(c, shape.first + at, values)
         return carry
 
@@ -615,17 +660,20 @@
     fields = lambda count: vmem((count,) + field, f32)
     sums = jax.ShapeDtypeStruct((2 * size, 1, 8), f32)
     block = surface.shape
-    wide, narrow = vmem((shape.own, SENT_ROWS, LANES), f32), vmem((1, SENT_ROWS, LANES), f32)
-    own, side, lo, hi, clo, chi = call(
+    wide = vmem((shape.own, SENT_ROWS, LANES), f32)
+    packed = lambda tiles: vmem((-(-tiles // SLOTS) * TILE, LANES), f32)
+    narrow = packed(2 * FIELDS)
+    full = vmem((FIELDS, shape.rows, LANES), f32)
+    corner = vmem((1, SENT_ROWS, LANES), f32)
+    own, lo, hi, side, clo, chi = call(
         pack_kernel, shape, [pl.ANY] * 5,
         [
             vmem((FIELDS, shape.own, shape.rows, LANES), f32),
-            vmem((FIELDS, 1, shape.rows, LANES), f32),
-            wide, wide, narrow, narrow,
+            wide, wide, packed(FIELDS * shape.rows // TILE), narrow, narrow,
         ],
         [
             vmem(velocity.shape, f32), vmem(block, f32), vmem(block, i32), vmem(block, i32),
-            smem(depth_table.shape, f32), pltpu.SemaphoreType.DMA((5,)),
+            smem(depth_table.shape, f32), full, pltpu.SemaphoreType.DMA((5,)),
         ],
         tuple(
             pltpu.with_memory_space_constraint(x, pltpu.HBM)
@@ -650,7 +698,7 @@
     moved, static, level, krylov, moments = call(
         first_kernel, shape, [vmem] * 7,
         [fields(4), fields(5), fields(1), fields(6), sums],
-        [fields(4), fields(1), fields(1)],
+        [fields(4), fields(1), fields(1), full, corner, corner],
         held(own, far, top, bot, ctop, cbot, head),
     )
     moved, level, krylov, moments = call(

time: 72.5 us -> 72.2 us (level)
  waiting for transfers between devices: 6.14 us -> 4.59 us
  blocking collectives: 31.3 us -> 32.4 us
    ppermute x1, waiting for transfers between devices: 6.13 us -> 4.58 us  [shards(): lax.ppermute(chi, both, [(2 * i + a, 2 * j + b) for i, j in up for a, b i...]
    all_to_all x2, blocking collectives: 31.3 us -> 32.4 us  [shared(): return lax.all_to_all(moments, ('along', 'cross'), 0, 0, tiled=True)]
where the time goes in v5:
time: 72.2 us; the launch traced here: 72 us
  blocking collectives  32.4 us (45%)
  Pallas kernels  21.4 us (30%)
  starting transfers between devices  11.6 us (16%)
  waiting for transfers between devices  4.59 us (6%)
  local copies, waits for them, and re-layouts  1.34 us (2%)
    all_to_all x2, blocking collectives, shared(): return lax.all_to_all(moments, ('along', 'cross'), 0, 0, tiled=True)  32.4 us
    pallas_call x5, Pallas kernels, call(): pl.pallas_call(functools.partial(kernel, shape), out_shape=outs, in_specs...  21.4 us
    ppermute x1, waiting for transfers between devices, shards(): lax.ppermute(chi, both, [(2 * i + a, 2 * j + b) for i, j in up for a, b i...  4.58 us
    ppermute x1, starting transfers between devices, shards(): lax.ppermute(clo, both, [(2 * i + a, 2 * j + b) for i, j in down for a, b...  4.18 us
    ppermute x1, starting transfers between devices, shards(): top = lax.ppermute(hi, 'along', up)  2.76 us
    ppermute x1, starting transfers between devices, shards(): far = lax.ppermute(side, 'cross', turned)  2.74 us
    ppermute x1, starting transfers between devices, shards(): lax.ppermute(chi, both, [(2 * i + a, 2 * j + b) for i, j in up for a, b i...  1.97 us
  transfers between devices with their start and end apart: 5, of which 1 were waited for; matrix products, arithmetic and copies ran while one was open for 0% of the time, Pallas kernels for 1%

profile of v5, /device:TPU:1, one launch (start us, length us, event | category | flops | bytes accessed | tf_op | source)
XLA Modules:
  0.0 72.0 jit_solution(8513389240691834025)
XLA Ops:
  0.6 1.9 %shard_map.94 = (f32[7,12,32,128]{3,2,1,0:T(8,128)S(1)}, f32[12,88,128]{2,1,0:T(8,128)S(1)}, f32[12,88,128]{2,1,0:T(8,128)S(1)}, f32[32,128]{1,0:T(8,128)S(1)}, ...) custom-call(f32[4,32,1536]{2,1,0:T(8,128)} %vel_in.1, f32[32,1536]{1,0:T(8,128)} %surface_in.1, s32[32,1536]{1,0:T(8,128)} %wet_in.1, ...), custom_call_target="tpu_custom_call" | custom-call | tf_op jit(solution)/shard_map/pallas_call | solution.py:635
  2.6 2.8 %collective-permute-start.1 = (f32[12,88,128]{2,1,0:T(8,128)S(1)}, f32[12,88,128]{2,1,0:T(8,128)S(1)}, u32[]{:S(2)}, u32[]{:S(2)}) collective-permute-start(f32[12,88,128]{2,1,0:T(8,128)S(1)} %get-tuple-element.20), channel_id=1, source_target_pairs={{0,2},{2,4},{4,6},{6,8},{8,10},{10,12},{12,14},{14,16},{16,18},{18... | collective-permute-start | bytes 1622024 | tf_op jit(solution)/shard_map/ppermute | solution.py:687
  5.3 0.0 collective-permute-start.2
  5.3 2.7 %collective-permute-start = (f32[32,128]{1,0:T(8,128)S(1)}, f32[32,128]{1,0:T(8,128)S(1)}, u32[]{:S(2)}, u32[]{:S(2)}) collective-permute-start(f32[32,128]{1,0:T(8,128)S(1)} %get-tuple-element.19), channel_id=1, source_target_pairs={{0,1},{1,0},{2,3},{3,2},{4,5},{5,4},{6,7},{7,6},{8,9},{9,8},{10,11... | collective-permute-start | bytes 49160 | tf_op jit(solution)/shard_map/ppermute | solution.py:689
  8.1 2.0 %collective-permute-start.3 = (f32[16,128]{1,0:T(8,128)S(1)}, f32[16,128]{1,0:T(8,128)S(1)}, u32[]{:S(2)}, u32[]{:S(2)}) collective-permute-start(f32[16,128]{1,0:T(8,128)S(1)} %get-tuple-element.22), channel_id=1, source_target_pairs={{0,3},{1,2},{2,5},{3,4},{4,7},{5,6},{6,9},{7,8},{8,11},{9,10},{10,... | collective-permute-start | bytes 24584 | tf_op jit(solution)/shard_map/ppermute | solution.py:690
  10.0 4.2 %collective-permute-start.4 = (f32[16,128]{1,0:T(8,128)S(1)}, f32[16,128]{1,0:T(8,128)S(1)}, u32[]{:S(2)}, u32[]{:S(2)}) collective-permute-start(f32[16,128]{1,0:T(8,128)S(1)} %get-tuple-element.23), channel_id=1, source_target_pairs={{2,1},{3,0},{4,3},{5,2},{6,5},{7,4},{8,7},{9,6},{10,9},{11,8},{12,... | collective-permute-start | bytes 24584 | tf_op jit(solution)/shard_map/ppermute | solution.py:691
  14.2 0.0 copy-start
  14.2 0.7 copy-done
  14.9 0.0 copy-start.1
  14.9 0.7 copy-done.1
  15.5 1.0 %shard_map.95.head = f32[1,13,80,128]{3,2,1,0:T(8,128)S(1)} custom-call(s32[4,8]{1,0:T(4,128)S(1)} %bitcast.1, f32[8]{0:T(128)S(1)} %copy-done.1), custom_call_target="tpu_custom_call" | custom-call | flops 2000000 | bytes 1000000 | tf_op jit(solution)/shard_map/pallas_call | solution.py:635
  16.5 4.6 %collective-permute-done.3.ctop_in = f32[16,128]{1,0:T(8,128)S(1)} collective-permute-done((f32[16,128]{1,0:T(8,128)S(1)}, f32[16,128]{1,0:T(8,128)S(1)}, u32[]{:S(2)}, u32[]{:S(2)}) %collective-permute-start.3) | collective-permute-done | bytes 8224 | tf_op jit(solution)/shard_map/ppermute | solution.py:690
  21.1 0.0 collective-permute-done.4.cbot_in
  21.1 0.0 collective-permute-done.side_in
  21.1 0.0 collective-permute-done.1.top
  21.1 0.0 collective-permute-done.2.bot
  21.1 8.4 %shard_map.96 = (f32[4,13,80,128]{3,2,1,0:T(8,128)S(1)}, f32[5,13,80,128]{3,2,1,0:T(8,128)S(1)}, f32[1,13,80,128]{3,2,1,0:T(8,128)S(1)}, f32[6,13,80,128]{3,2,1,0:T(8,128)S(1)}, f32[128,1,8]{2,1,0:T(1,128)S(1)}) custom-call(f32[7,12,32,128]{3,2,1,0:T(8,128)S(1)} %get-tuple-element.18.own, f32[32,128]{1,0:T(8,128)S(1)} %collective-permute-done.side_in, ...), custom_call_target="tpu_custom_call" | custom-call | tf_op jit(solution)/shard_map/pallas_call | solution.py:635
  29.5 18.6 %all_to_all.10.shares = f32[128,1,8]{2,1,0:T(1,128)S(1)} all-to-all(f32[128,1,8]{2,1,0:T(1,128)S(1)} %get-tuple-element.24), channel_id=1, replica_groups=mesh['along'=64,'cross'=2] {'along','cross'}, dimensions={0} | all-to-all | bytes 8192 | tf_op jit(solution)/shard_map/all_to_all | solution.py:651
  48.1 7.7 %shard_map.97 = (f32[4,13,80,128]{3,2,1,0:T(8,128)S(1)}, f32[1,13,80,128]{3,2,1,0:T(8,128)S(1)}, f32[6,13,80,128]{3,2,1,0:T(8,128)S(1)}, f32[128,1,8]{2,1,0:T(1,128)S(1)}) custom-call(f32[128,1,8]{2,1,0:T(1,128)S(1)} %all_to_all.10.shares, f32[4,13,80,128]{3,2,1,0:T(8,128)S(1)} %get-tuple-element.25.moved_in, ...), custom_call_target="tpu_custom_call" | custom-call | tf_op jit(solution)/shard_map/pallas_call | solution.py:635
  55.8 13.8 %all_to_all.11.shares = f32[128,1,8]{2,1,0:T(1,128)S(1)} all-to-all(f32[128,1,8]{2,1,0:T(1,128)S(1)} %get-tuple-element.29), channel_id=1, replica_groups=mesh['along'=64,'cross'=2] {'along','cross'}, dimensions={0} | all-to-all | bytes 8192 | tf_op jit(solution)/shard_map/all_to_all | solution.py:651
  69.6 2.4 %shard_map.98 = (f32[4,32,1536]{2,1,0:T(8,128)}, f32[32,1536]{1,0:T(8,128)}, f32[2,32,1536]{2,1,0:T(8,128)}) custom-call(f32[128,1,8]{2,1,0:T(1,128)S(1)} %all_to_all.11.shares, f32[4,13,80,128]{3,2,1,0:T(8,128)S(1)} %get-tuple-element.30.moved, f32[5,13,80,128]{3,2,1,0:T(8,128)S(1)} %get-tuple-element.26.static, ...), custom_call_target="tpu_custom_call" | custom-call | tf_op jit(solution)/shard_map/pallas_call | solution.py:635
Async XLA Ops:
  2.6 18.5 %collective-permute-start.1 = (f32[12,88,128]{2,1,0:T(8,128)S(1)}, f32[12,88,128]{2,1,0:T(8,128)S(1)}, u32[]{:S(2)}, u32[]{:S(2)}) collective-permute-start(f32[12,88,128]{2,1,0:T(8,128)S(1)} %get-tuple-element.20), channel_id=1, source_target_pairs={{0,2},{2,4},{4,6},{6,8},{8,10},{10,12},{12,14},{14,16},{16,18},{18... | collective-permute-start | bytes 1622024 | tf_op jit(solution)/shard_map/ppermute | solution.py:687
  5.3 15.8 %collective-permute-start.2 = (f32[12,88,128]{2,1,0:T(8,128)S(1)}, f32[12,88,128]{2,1,0:T(8,128)S(1)}, u32[]{:S(2)}, u32[]{:S(2)}) collective-permute-start(f32[12,88,128]{2,1,0:T(8,128)S(1)} %get-tuple-element.21), channel_id=1, source_target_pairs={{2,0},{4,2},{6,4},{8,6},{10,8},{12,10},{14,12},{16,14},{18,16},{20... | collective-permute-start | bytes 1622024 | tf_op jit(solution)/shard_map/ppermute | solution.py:688
  5.3 15.8 %collective-permute-start = (f32[32,128]{1,0:T(8,128)S(1)}, f32[32,128]{1,0:T(8,128)S(1)}, u32[]{:S(2)}, u32[]{:S(2)}) collective-permute-start(f32[32,128]{1,0:T(8,128)S(1)} %get-tuple-element.19), channel_id=1, source_target_pairs={{0,1},{1,0},{2,3},{3,2},{4,5},{5,4},{6,7},{7,6},{8,9},{9,8},{10,11... | collective-permute-start | bytes 49160 | tf_op jit(solution)/shard_map/ppermute | solution.py:689
  8.1 13.0 %collective-permute-start.3 = (f32[16,128]{1,0:T(8,128)S(1)}, f32[16,128]{1,0:T(8,128)S(1)}, u32[]{:S(2)}, u32[]{:S(2)}) collective-permute-start(f32[16,128]{1,0:T(8,128)S(1)} %get-tuple-element.22), channel_id=1, source_target_pairs={{0,3},{1,2},{2,5},{3,4},{4,7},{5,6},{6,9},{7,8},{8,11},{9,10},{10,... | collective-permute-start | bytes 24584 | tf_op jit(solution)/shard_map/ppermute | solution.py:690
  10.0 11.1 %collective-permute-start.4 = (f32[16,128]{1,0:T(8,128)S(1)}, f32[16,128]{1,0:T(8,128)S(1)}, u32[]{:S(2)}, u32[]{:S(2)}) collective-permute-start(f32[16,128]{1,0:T(8,128)S(1)} %get-tuple-element.23), channel_id=1, source_target_pairs={{2,1},{3,0},{4,3},{5,2},{6,5},{7,4},{8,7},{9,6},{10,9},{11,8},{12,... | collective-permute-start | bytes 24584 | tf_op jit(solution)/shard_map/ppermute | solution.py:691
  14.2 0.7 copy-start
  14.9 0.7 copy-start.1

commit v6 on v5

--- a/solution.py
+++ b/solution.py
@@ -24,6 +24,7 @@
 SENT = (13, 13, 13, 13, 12, 11, 11)
 OFFSETS = (0, 13, 26, 39, 52, 64, 75)
 SENT_ROWS = 88
+CORNER_ROWS = 16
 EDGE = 16
 SLOTS = LANES // EDGE
 VMEM_BYTES = 24 * 1024 * 1024
@@ -256,61 +257,93 @@
     put_moments(moments, moments_of(shape, krylov, static))
 
 
-def pack_kernel(
-    shape, vel_in, surface_in, wet_in, bathy_in, table_in,
-    own, lo, hi, side, clo, chi,
-    vel, surface, wet, bathy, table, edge, arrived,
-):
+def fetch(pairs, arrived):
     copies = [
         pltpu.make_async_copy(source, target, arrived.at[number])
-        for number, (source, target) in enumerate(
-            (
-                (table_in, table),
-                (bathy_in, bathy),
-                (wet_in, wet),
-                (surface_in, surface),
-                (vel_in, vel),
-            )
-        )
+        for number, (source, target) in enumerate(pairs)
     ]
     for copy in copies:
         copy.start()
-    half = lax.axis_index("cross")
-    lane = lanes_of()
     for copy in copies:
         copy.wait()
 
+
+def cell_values(vel, surface, wet, bathy, table, rows, cols):
+    flag = wet[rows, cols]
+    entry = bathy[rows, cols]
+    thick = jnp.zeros((TILE, LANES), jnp.float32)
+    for choice in range(CLASSES):
+        thick = jnp.where(entry == choice, 0.5 * table[choice], thick)
+    values = [jnp.where(flag > 0, vel[k, rows, cols], 0.0) for k in range(4)]
+    return values + [surface[rows, cols], flag.astype(jnp.float32), thick]
+
+
+def edge_kernel(
+    shape, vel_in, surface_in, wet_in, bathy_in, table_in, side,
+    vel, surface, wet, bathy, table, edge, arrived,
+):
+    half = lax.axis_index("cross")
+    first = jnp.where(half == 0, (shape.own - 1) * LANES, 0)
+    near = pl.ds(pl.multiple_of(first, LANES), LANES)
+    fetch(
+        (
+            (table_in, table),
+            (bathy_in.at[:, near], bathy),
+            (wet_in.at[:, near], wet),
+            (surface_in.at[:, near], surface),
+            (vel_in.at[:, :, near], vel),
+        ),
+        arrived,
+    )
+    for t in range(shape.rows // TILE):
+        rows = pl.ds(t * TILE, TILE)
+        values = cell_values(vel, surface, wet, bathy, table, rows, pl.ds(0, LANES))
+        for k, value in enumerate(values):
+            edge[k, rows, :] = value
+    squeeze(side, 0, side_tiles(shape, edge), jnp.where(half == 0, EDGE, 0))
+
+
+def pack_kernel(
+    shape, vel_in, surface_in, wet_in, bathy_in, table_in,
+    own, lo, hi,
+    vel, surface, wet, bathy, table, arrived,
+):
+    fetch(
+        (
+            (table_in, table),
+            (bathy_in, bathy),
+            (wet_in, wet),
+            (surface_in, surface),
+            (vel_in, vel),
+        ),
+        arrived,
+    )
+
     def turn(number, carry):
         rows = pl.ds(pl.multiple_of(number * TILE, TILE), TILE)
-        edges = []
         for c in range(shape.own):
             cols = pl.ds(c * LANES, LANES)
-            flag = wet[rows, cols]
-            entry = bathy[rows, cols]
-            thick = jnp.zeros((TILE, LANES), jnp.float32)
-            for choice in range(CLASSES):
-                thick = jnp.where(entry == choice, 0.5 * table[choice], thick)
-            values = [jnp.where(flag > 0, vel[k, rows, cols], 0.0) for k in range(4)]
-            values += [surface[rows, cols], flag.astype(jnp.float32), thick]
+            values = cell_values(vel, surface, wet, bathy, table, rows, cols)
             for k, value in enumerate(values):
                 own[k, c, rows, :] = value
-            if c in (0, shape.own - 1):
-                edges.append(values)
-        for k in range(FIELDS):
-            edge[k, rows, :] = jnp.where(half == 0, edges[1][k], edges[0][k])
         return carry
 
     lax.fori_loop(0, shape.rows // TILE, turn, 0)
     for c in range(shape.own):
         for k in range(FIELDS):
             for part in (0, SENT[k] - TILE):
-                to = pl.ds(OFFSETS[k] + part, TILE)
-                lo[c, to, :] = own[k, c, pl.ds(part, TILE), :]
-                hi[c, to, :] = own[k, c, pl.ds(shape.rows - SENT[k] + part, TILE), :]
-    shift = jnp.where(half == 0, EDGE, 0)
-    squeeze(side, side_tiles(shape, edge), shift)
-    squeeze(clo, corner_tiles(edge, 0), shift)
-    squeeze(chi, corner_tiles(edge, shape.rows), shift)
+                to = pl.ds(c * SENT_ROWS + OFFSETS[k] + part, TILE)
+                lo[to, :] = own[k, c, pl.ds(part, TILE), :]
+                hi[to, :] = own[k, c, pl.ds(shape.rows - SENT[k] + part, TILE), :]
+
+
+def corner_kernel(shape, far, lo_in, hi_in, lo, hi, side):
+    half = lax.axis_index("cross")
+    for number, tile in enumerate(side_tiles(shape, side)):
+        tile[...] = spread(far, 0, number, half)
+    shift = jnp.where(half == 0, 0, EDGE)
+    squeeze(lo, shape.own * SENT_ROWS, corner_tiles(side, 0), shift)
+    squeeze(hi, shape.own * SENT_ROWS, corner_tiles(side, shape.rows), shift)
 
 
 def side_tiles(shape, edge):
@@ -330,26 +363,26 @@
     ]
 
 
-def squeeze(out, tiles, shift):
+def squeeze(out, base, tiles, shift):
     slot = lanes_of() // EDGE
     for first in range(0, len(tiles), SLOTS):
         value = jnp.zeros((TILE, LANES), jnp.float32)
         for number, tile in enumerate(tiles[first : first + SLOTS]):
             moved = pltpu.roll(tile[...], lax.rem(EDGE * number + shift, LANES), 1)
             value = jnp.where(slot == number, moved, value)
-        out[pl.ds(first, TILE), :] = value
-
-
-def spread(source, number, half):
+        out[pl.ds(base + first, TILE), :] = value
+
+
+def spread(source, base, number, half):
     lane = lanes_of()
-    tile = source[pl.ds(number // SLOTS * TILE, TILE), :]
+    tile = source[pl.ds(base + number // SLOTS * TILE, TILE), :]
     amount = LANES - EDGE * (number % SLOTS) - jnp.where(half == 0, 0, EDGE)
     moved = pltpu.roll(tile, lax.rem(amount + LANES, LANES), 1)
     wanted = jnp.where(half == 0, lane, LANES - 1 - lane) < EDGE
     return jnp.where(wanted, moved, 0.0)
 
 
-def head_kernel(shape, ranges, heads, head, columns):
+def head_kernel(shape, ranges, heads, side, head, columns):
     along = lax.axis_index("along")
     half = lax.axis_index("cross")
     lane = lanes_of()
@@ -379,18 +412,16 @@
 
 
 def first_kernel(
-    shape, own, side_in, top, bot, ctop_in, cbot_in, head,
+    shape, own, side, top, bot, head,
     moved, static, surface, krylov, moments,
-    vel, potential, thick, side, ctop, cbot,
+    vel, potential, thick, ctop, cbot,
 ):
     along = lax.axis_index("along")
     half = lax.axis_index("cross")
-    for number, tile in enumerate(side_tiles(shape, side)):
-        tile[...] = spread(side_in, number, half)
     for number, (k, part) in enumerate(corner_parts()):
         to = pl.ds(OFFSETS[k] + part, TILE)
-        ctop[0, to, :] = spread(ctop_in, number, half)
-        cbot[0, to, :] = spread(cbot_in, number, half)
+        ctop[to, :] = spread(top, shape.own * SENT_ROWS, number, half)
+        cbot[to, :] = spread(bot, shape.own * SENT_ROWS, number, half)
     lane = lanes_of()
 
     def place(c, row, values):
@@ -424,11 +455,11 @@
     ):
         for start in starts:
             for c in range(shape.chunks):
-                source, chunk = (wide, c) if c < shape.own else (narrow, 0)
+                source, skip = (wide, c * SENT_ROWS) if c < shape.own else (narrow, 0)
                 values = []
                 for k in range(FIELDS):
                     at = OFFSETS[k] + (start if start > 0 or starts[0] == 0 else SENT[k] + start)
-                    value = source[chunk, pl.ds(at, TILE), :]
+                    value = source[pl.ds(skip + at, TILE), :]
                     values.append(jnp.where(keep, value, 0.0))
                 base = shape.first + (shape.rows if starts[0] == 0 else 0)
                 place(c, base + start, values)
@@ -631,14 +662,19 @@
     )
 
 
-def call(kernel, shape, kinds, outs, scratch, operands, cost=None):
+def cost(flops):
+    return pl.CostEstimate(flops=flops, bytes_accessed=flops, transcendentals=0)
+
+
+def call(kernel, shape, kinds, outs, scratch, operands, estimate=None, aliases={}):
     return pl.pallas_call(
         functools.partial(kernel, shape),
         out_shape=outs,
         in_specs=[pl.BlockSpec(memory_space=kind) for kind in kinds],
         out_specs=[pl.BlockSpec(memory_space=pltpu.VMEM)] * len(outs),
         scratch_shapes=scratch,
-        cost_estimate=cost,
+        cost_estimate=estimate,
+        input_output_aliases=aliases,
         compiler_params=pltpu.CompilerParams(vmem_limit_bytes=VMEM_BYTES),
     )(*operands)
 
@@ -660,46 +696,53 @@
     fields = lambda count: vmem((count,) + field, f32)
     sums = jax.ShapeDtypeStruct((2 * size, 1, 8), f32)
     block = surface.shape
-    wide = vmem((shape.own, SENT_ROWS, LANES), f32)
-    packed = lambda tiles: vmem((-(-tiles // SLOTS) * TILE, LANES), f32)
-    narrow = packed(2 * FIELDS)
+    wide = vmem((shape.own * SENT_ROWS + CORNER_ROWS, LANES), f32)
     full = vmem((FIELDS, shape.rows, LANES), f32)
-    corner = vmem((1, SENT_ROWS, LANES), f32)
-    own, lo, hi, side, clo, chi = call(
+    corner = vmem((SENT_ROWS, LANES), f32)
+    tiles = FIELDS * shape.rows // TILE
+    table = [smem(depth_table.shape, f32)]
+    arrived = [pltpu.SemaphoreType.DMA((5,))]
+    near = (shape.rows, LANES)
+    inputs = tuple(
+        pltpu.with_memory_space_constraint(x, pltpu.HBM)
+        for x in (velocity, surface, wet_mask, bathy_class, depth_table)
+    )
+    (side,) = call(
+        edge_kernel, shape, [pl.ANY] * 5,
+        [vmem((-(-tiles // SLOTS) * TILE, LANES), f32)],
+        [vmem((4,) + near, f32), vmem(near, f32), vmem(near, i32), vmem(near, i32)]
+        + table + [full] + arrived,
+        inputs,
+        cost(10**5),
+    )
+    far = lax.ppermute(side, "cross", [(0, 1), (1, 0)])
+    own, lo, hi = call(
         pack_kernel, shape, [pl.ANY] * 5,
-        [
-            vmem((FIELDS, shape.own, shape.rows, LANES), f32),
-            wide, wide, packed(FIELDS * shape.rows // TILE), narrow, narrow,
-        ],
-        [
-            vmem(velocity.shape, f32), vmem(block, f32), vmem(block, i32), vmem(block, i32),
-            smem(depth_table.shape, f32), full, pltpu.SemaphoreType.DMA((5,)),
-        ],
-        tuple(
-            pltpu.with_memory_space_constraint(x, pltpu.HBM)
-            for x in (velocity, surface, wet_mask, bathy_class, depth_table)
-        ),
-    )
-    both = ("along", "cross")
+        [vmem((FIELDS, shape.own, shape.rows, LANES), f32), wide, wide],
+        [vmem(velocity.shape, f32), vmem(block, f32), vmem(block, i32), vmem(block, i32)]
+        + table + arrived,
+        inputs,
+        cost(4 * 10**6),
+    )
+    lo, hi, side = call(
+        corner_kernel, shape, [vmem] * 3, [wide, wide, full], [], held(far, lo, hi),
+        cost(10**5), {1: 0, 2: 1},
+    )
     up = [(i, (i + 1) % size) for i in range(size)]
     down = [(j, i) for i, j in up]
-    turned = [(0, 1), (1, 0)]
     top = lax.ppermute(hi, "along", up)
     bot = lax.ppermute(lo, "along", down)
-    far = lax.ppermute(side, "cross", turned)
-    ctop = lax.ppermute(chi, both, [(2 * i + a, 2 * j + b) for i, j in up for a, b in turned])
-    cbot = lax.ppermute(clo, both, [(2 * i + a, 2 * j + b) for i, j in down for a, b in turned])
     (head,) = call(
-        head_kernel, shape, [smem] * 2, [fields(1)],
+        head_kernel, shape, [smem] * 2 + [vmem], [fields(1)],
         [vmem((SHIPS, shape.chunks, TILE, LANES), f32)],
-        (hull_ranges.T, hull_pressure),
-        pl.CostEstimate(flops=2 * 10**6, bytes_accessed=10**6, transcendentals=0),
+        (hull_ranges.T, hull_pressure) + held(side),
+        cost(2 * 10**6),
     )
     moved, static, level, krylov, moments = call(
-        first_kernel, shape, [vmem] * 7,
+        first_kernel, shape, [vmem] * 5,
         [fields(4), fields(5), fields(1), fields(6), sums],
-        [fields(4), fields(1), fields(1), full, corner, corner],
-        held(own, far, top, bot, ctop, cbot, head),
+        [fields(4), fields(1), fields(1), corner, corner],
+        held(own, side, top, bot, head),
     )
     moved, level, krylov, moments = call(
         second_kernel, shape, [vmem] * 5,

time: 72.2 us -> 73.2 us (1.014)
  starting transfers between devices: 11.6 us -> 6.18 us
  waiting for transfers between devices: 4.59 us -> 8.19 us
  blocking collectives: 32.4 us -> 35.4 us
  local copies, waits for them, and re-layouts: 1.34 us -> 0.01 us
  Pallas kernels: 21.4 us -> 22.5 us
    ppermute x1, waiting for transfers between devices: 0.01 us -> 5.41 us  [shards(): top = lax.ppermute(hi, 'along', up)]
    ppermute x3 -> x1, starting transfers between devices: 8.89 us -> 3.65 us  [shards(): far = lax.ppermute(side, 'cross', [(0, 1), (1, 0)])]
    ppermute x3 -> x1, waiting for transfers between devices: 4.58 us -> 0.01 us  [shards(): far = lax.ppermute(side, 'cross', [(0, 1), (1, 0)])]
    all_to_all x2, blocking collectives: 32.4 us -> 35.4 us  [shared(): return lax.all_to_all(moments, ('along', 'cross'), 0, 0, tiled=True)]
    ppermute x1, waiting for transfers between devices: 0.01 us -> 2.77 us  [shards(): bot = lax.ppermute(lo, 'along', down)]
    unnamed x4, local copies, waits for them, and re-layouts: 1.34 us -> 0.01 us
    pallas_call x5 -> x7, Pallas kernels: 21.4 us -> 22.5 us  [call(): pl.pallas_call(functools.partial(kernel, shape), out_shape=outs, in_specs...]
  transfers between devices with their start and end apart: 5 -> 3, of which waited for: 1 -> 2; matrix products, arithmetic and copies ran while one was open for 0% -> 0% of each run, Pallas kernels for 1% -> 4%
where the time goes in v6:
time: 73.2 us; the launch traced here: 73 us
  blocking collectives  35.4 us (48%)
  Pallas kernels  22.5 us (31%)
  waiting for transfers between devices  8.19 us (11%)
  starting transfers between devices  6.18 us (8%)
    all_to_all x2, blocking collectives, shared(): return lax.all_to_all(moments, ('along', 'cross'), 0, 0, tiled=True)  35.4 us
    pallas_call x7, Pallas kernels, call(): pl.pallas_call(functools.partial(kernel, shape), out_shape=outs, in_specs...  22.5 us
    ppermute x1, waiting for transfers between devices, shards(): top = lax.ppermute(hi, 'along', up)  5.41 us
    ppermute x1, starting transfers between devices, shards(): far = lax.ppermute(side, 'cross', [(0, 1), (1, 0)])  3.65 us
    ppermute x1, waiting for transfers between devices, shards(): bot = lax.ppermute(lo, 'along', down)  2.77 us
    ppermute x1, starting transfers between devices, shards(): top = lax.ppermute(hi, 'along', up)  2.52 us
  transfers between devices with their start and end apart: 3, of which 2 were waited for; matrix products, arithmetic and copies ran while one was open for 0% of the time, Pallas kernels for 4%

profile of v6, /device:TPU:1, one launch (start us, length us, event | category | flops | bytes accessed | tf_op | source)
XLA Modules:
  0.0 73.0 jit_solution(14290942565959099536)
XLA Ops:
  0.6 0.0 copy-start.1
  0.6 0.0 copy-start
  0.7 1.1 %shard_map.95 = f32[32,128]{1,0:T(8,128)S(1)} custom-call(f32[4,32,1536]{2,1,0:T(8,128)} %vel_in.3, f32[32,1536]{1,0:T(8,128)} %surface_in.3, s32[32,1536]{1,0:T(8,128)} %wet_in.3, s32[32,1536]{1,0:T(8,128)} %bathy_in.3, f32[16]{0:T(128)} %table_in.3), custom_call_target="tpu_custom_call" | custom-call | flops 100000 | bytes 100000 | tf_op jit(solution)/shard_map/pallas_call | solution.py:670
  1.7 3.7 %collective-permute-start = (f32[32,128]{1,0:T(8,128)S(1)}, f32[32,128]{1,0:T(8,128)S(1)}, u32[]{:S(2)}, u32[]{:S(2)}) collective-permute-start(f32[32,128]{1,0:T(8,128)S(1)} %shard_map.95), channel_id=1, source_target_pairs={{0,1},{1,0},{2,3},{3,2},{4,5},{5,4},{6,7},{7,6},{8,9},{9,8},{10,11... | collective-permute-start | bytes 49160 | tf_op jit(solution)/shard_map/ppermute | solution.py:718
  5.4 1.9 %shard_map.94 = (f32[7,12,32,128]{3,2,1,0:T(8,128)S(1)}, f32[1072,128]{1,0:T(8,128)S(1)}, f32[1072,128]{1,0:T(8,128)S(1)}) custom-call(f32[4,32,1536]{2,1,0:T(8,128)} %vel_in.3, f32[32,1536]{1,0:T(8,128)} %surface_in.3, s32[32,1536]{1,0:T(8,128)} %wet_in.3, s32[32,1536]{1,0:T(8,128)} %bathy_in.3, f32[16]{0:T(128)} %table_in.3), custom_call_target="tpu_custom_call" | custom-call | flops 4000000 | bytes 4000000 | tf_op jit(solution)/shard_map/pallas_call | solution.py:670
  7.2 0.0 collective-permute-done.far
  7.3 0.2 shard_map.96
  7.5 2.5 %collective-permute-start.1 = (f32[1072,128]{1,0:T(8,128)S(1)}, f32[1072,128]{1,0:T(8,128)S(1)}, u32[]{:S(2)}, u32[]{:S(2)}) collective-permute-start(f32[1072,128]{1,0:T(8,128)S(1)} %get-tuple-element.22), channel_id=1, source_target_pairs={{0,2},{2,4},{4,6},{6,8},{8,10},{10,12},{12,14},{14,16},{16,18},{18... | collective-permute-start | bytes 1646600 | tf_op jit(solution)/shard_map/ppermute | solution.py:733
  10.0 0.0 collective-permute-start.2
  10.0 0.0 copy-done.1
  10.0 0.0 copy-done
  10.0 1.0 %shard_map.97.head = f32[1,13,80,128]{3,2,1,0:T(8,128)S(1)} custom-call(s32[4,8]{1,0:T(4,128)S(1)} %bitcast.1, f32[8]{0:T(128)S(1)} %copy-done.1, f32[7,32,128]{2,1,0:T(8,128)S(1)} %get-tuple-element.21.side), custom_call_target="tpu_custom_call" | custom-call | flops 2000000 | bytes 2000000 | tf_op jit(solution)/shard_map/pallas_call | solution.py:670
  10.9 5.4 %collective-permute-done.1.top = f32[1072,128]{1,0:T(8,128)S(1)} collective-permute-done((f32[1072,128]{1,0:T(8,128)S(1)}, f32[1072,128]{1,0:T(8,128)S(1)}, u32[]{:S(2)}, u32[]{:S(2)}) %collective-permute-start.1) | collective-permute-done | bytes 548896 | tf_op jit(solution)/shard_map/ppermute | solution.py:733
  16.4 2.8 %collective-permute-done.2.bot = f32[1072,128]{1,0:T(8,128)S(1)} collective-permute-done((f32[1072,128]{1,0:T(8,128)S(1)}, f32[1072,128]{1,0:T(8,128)S(1)}, u32[]{:S(2)}, u32[]{:S(2)}) %collective-permute-start.2) | collective-permute-done | bytes 548896 | tf_op jit(solution)/shard_map/ppermute | solution.py:734
  19.1 8.4 %shard_map.98 = (f32[4,13,80,128]{3,2,1,0:T(8,128)S(1)}, f32[5,13,80,128]{3,2,1,0:T(8,128)S(1)}, f32[1,13,80,128]{3,2,1,0:T(8,128)S(1)}, f32[6,13,80,128]{3,2,1,0:T(8,128)S(1)}, f32[128,1,8]{2,1,0:T(1,128)S(1)}) custom-call(f32[7,12,32,128]{3,2,1,0:T(8,128)S(1)} %get-tuple-element.18.own, f32[7,32,128]{2,1,0:T(8,128)S(1)} %get-tuple-element.21.side, ...), custom_call_target="tpu_custom_call" | custom-call | tf_op jit(solution)/shard_map/pallas_call | solution.py:670
  27.5 21.6 %all_to_all.10.shares = f32[128,1,8]{2,1,0:T(1,128)S(1)} all-to-all(f32[128,1,8]{2,1,0:T(1,128)S(1)} %get-tuple-element.24), channel_id=1, replica_groups=mesh['along'=64,'cross'=2] {'along','cross'}, dimensions={0} | all-to-all | bytes 8192 | tf_op jit(solution)/shard_map/all_to_all | solution.py:687
  49.1 7.7 %shard_map.99 = (f32[4,13,80,128]{3,2,1,0:T(8,128)S(1)}, f32[1,13,80,128]{3,2,1,0:T(8,128)S(1)}, f32[6,13,80,128]{3,2,1,0:T(8,128)S(1)}, f32[128,1,8]{2,1,0:T(1,128)S(1)}) custom-call(f32[128,1,8]{2,1,0:T(1,128)S(1)} %all_to_all.10.shares, f32[4,13,80,128]{3,2,1,0:T(8,128)S(1)} %get-tuple-element.25.moved_in, ...), custom_call_target="tpu_custom_call" | custom-call | tf_op jit(solution)/shard_map/pallas_call | solution.py:670
  56.8 13.8 %all_to_all.11.shares = f32[128,1,8]{2,1,0:T(1,128)S(1)} all-to-all(f32[128,1,8]{2,1,0:T(1,128)S(1)} %get-tuple-element.29), channel_id=1, replica_groups=mesh['along'=64,'cross'=2] {'along','cross'}, dimensions={0} | all-to-all | bytes 8192 | tf_op jit(solution)/shard_map/all_to_all | solution.py:687
  70.6 2.4 %shard_map.100 = (f32[4,32,1536]{2,1,0:T(8,128)}, f32[32,1536]{1,0:T(8,128)}, f32[2,32,1536]{2,1,0:T(8,128)}) custom-call(f32[128,1,8]{2,1,0:T(1,128)S(1)} %all_to_all.11.shares, f32[4,13,80,128]{3,2,1,0:T(8,128)S(1)} %get-tuple-element.30.moved, f32[5,13,80,128]{3,2,1,0:T(8,128)S(1)} %get-tuple-element.26.static, ...), custom_call_target="tpu_custom_call" | custom-call | tf_op jit(solution)/shard_map/pallas_call | solution.py:670
Async XLA Ops:
  0.6 9.3 %copy-start.1 = (f32[8]{0:T(128)S(1)}, f32[8]{0:T(128)}, u32[]{:S(2)}) copy-start(f32[8]{0:T(128)} %heads.1) | copy-start | bytes 100
  0.6 9.3 %copy-start = (s32[8,4]{0,1:T(4,128)S(1)}, s32[8,4]{0,1:T(4,128)}, u32[]{:S(2)}) copy-start(s32[8,4]{0,1:T(4,128)} %param.12) | copy-start | bytes 388
  1.7 5.5 %collective-permute-start = (f32[32,128]{1,0:T(8,128)S(1)}, f32[32,128]{1,0:T(8,128)S(1)}, u32[]{:S(2)}, u32[]{:S(2)}) collective-permute-start(f32[32,128]{1,0:T(8,128)S(1)} %shard_map.95), channel_id=1, source_target_pairs={{0,1},{1,0},{2,3},{3,2},{4,5},{5,4},{6,7},{7,6},{8,9},{9,8},{10,11... | collective-permute-start | bytes 49160 | tf_op jit(solution)/shard_map/ppermute | solution.py:718
  7.5 8.9 %collective-permute-start.1 = (f32[1072,128]{1,0:T(8,128)S(1)}, f32[1072,128]{1,0:T(8,128)S(1)}, u32[]{:S(2)}, u32[]{:S(2)}) collective-permute-start(f32[1072,128]{1,0:T(8,128)S(1)} %get-tuple-element.22), channel_id=1, source_target_pairs={{0,2},{2,4},{4,6},{6,8},{8,10},{10,12},{12,14},{14,16},{16,18},{18... | collective-permute-start | bytes 1646600 | tf_op jit(solution)/shard_map/ppermute | solution.py:733
  10.0 9.2 %collective-permute-start.2 = (f32[1072,128]{1,0:T(8,128)S(1)}, f32[1072,128]{1,0:T(8,128)S(1)}, u32[]{:S(2)}, u32[]{:S(2)}) collective-permute-start(f32[1072,128]{1,0:T(8,128)S(1)} %get-tuple-element.23), channel_id=1, source_target_pairs={{2,0},{4,2},{6,4},{8,6},{10,8},{12,10},{14,12},{16,14},{18,16},{20... | collective-permute-start | bytes 1646600 | tf_op jit(solution)/shard_map/ppermute | solution.py:734

commit v7 on v6

--- a/solution.py
+++ b/solution.py
@@ -305,7 +305,7 @@
 
 def pack_kernel(
     shape, vel_in, surface_in, wet_in, bathy_in, table_in,
-    own, lo, hi,
+    own, out_chip, in_chip,
     vel, surface, wet, bathy, table, arrived,
 ):
     fetch(
@@ -329,21 +329,24 @@
         return carry
 
     lax.fori_loop(0, shape.rows // TILE, turn, 0)
+    core = lax.rem(lax.axis_index("along"), 2)
     for c in range(shape.own):
         for k in range(FIELDS):
             for part in (0, SENT[k] - TILE):
                 to = pl.ds(c * SENT_ROWS + OFFSETS[k] + part, TILE)
-                lo[to, :] = own[k, c, pl.ds(part, TILE), :]
-                hi[to, :] = own[k, c, pl.ds(shape.rows - SENT[k] + part, TILE), :]
-
-
-def corner_kernel(shape, far, lo_in, hi_in, lo, hi, side):
+                last = shape.rows - SENT[k]
+                out_chip[to, :] = own[k, c, pl.ds(part + core * last, TILE), :]
+                in_chip[to, :] = own[k, c, pl.ds(part + (1 - core) * last, TILE), :]
+
+
+def corner_kernel(shape, far, out_in, in_in, out_chip, in_chip, side):
     half = lax.axis_index("cross")
+    core = lax.rem(lax.axis_index("along"), 2)
     for number, tile in enumerate(side_tiles(shape, side)):
         tile[...] = spread(far, 0, number, half)
     shift = jnp.where(half == 0, 0, EDGE)
-    squeeze(lo, shape.own * SENT_ROWS, corner_tiles(side, 0), shift)
-    squeeze(hi, shape.own * SENT_ROWS, corner_tiles(side, shape.rows), shift)
+    squeeze(out_chip, shape.own * SENT_ROWS, corner_tiles(shape, side, core), shift)
+    squeeze(in_chip, shape.own * SENT_ROWS, corner_tiles(shape, side, 1 - core), shift)
 
 
 def side_tiles(shape, edge):
@@ -356,9 +359,9 @@
     return [(k, part) for k in range(FIELDS) for part in (0, SENT[k] - TILE)]
 
 
-def corner_tiles(edge, rows):
+def corner_tiles(shape, edge, last):
     return [
-        edge.at[k, pl.ds(part + (rows - SENT[k] if rows else 0), TILE), :]
+        edge.at[k, pl.ds(part + last * (shape.rows - SENT[k]), TILE), :]
         for k, part in corner_parts()
     ]
 
@@ -412,16 +415,16 @@
 
 
 def first_kernel(
-    shape, own, side, top, bot, head,
+    shape, own, side, out_chip, in_chip, head,
     moved, static, surface, krylov, moments,
-    vel, potential, thick, ctop, cbot,
+    vel, potential, thick, out_corner, in_corner,
 ):
     along = lax.axis_index("along")
     half = lax.axis_index("cross")
     for number, (k, part) in enumerate(corner_parts()):
         to = pl.ds(OFFSETS[k] + part, TILE)
-        ctop[to, :] = spread(top, shape.own * SENT_ROWS, number, half)
-        cbot[to, :] = spread(bot, shape.own * SENT_ROWS, number, half)
+        out_corner[to, :] = spread(out_chip, shape.own * SENT_ROWS, number, half)
+        in_corner[to, :] = spread(in_chip, shape.own * SENT_ROWS, number, half)
     lane = lanes_of()
 
     def place(c, row, values):
@@ -448,21 +451,20 @@
         return carry
 
     lax.fori_loop(0, shape.rows // TILE, own_rows, 0)
+    core = lax.rem(along, 2)
     deepest = SENT[0]
-    for wide, narrow, keep, starts in (
-        (top, ctop, along > 0, (-deepest, -TILE)),
-        (bot, cbot, along < lax.axis_size("along") - 1, (0, deepest - TILE)),
-    ):
-        for start in starts:
+    last = lax.axis_size("along") - 1
+    for wide, narrow, below in ((out_chip, out_corner, core), (in_chip, in_corner, 1 - core)):
+        keep = jnp.where(below == 1, last - along, along) > 0
+        for over, under in ((-deepest, 0), (-TILE, deepest - TILE)):
+            row = shape.first + jnp.where(below == 1, shape.rows + under, over)
             for c in range(shape.chunks):
                 source, skip = (wide, c * SENT_ROWS) if c < shape.own else (narrow, 0)
                 values = []
                 for k in range(FIELDS):
-                    at = OFFSETS[k] + (start if start > 0 or starts[0] == 0 else SENT[k] + start)
-                    value = source[pl.ds(skip + at, TILE), :]
-                    values.append(jnp.where(keep, value, 0.0))
-                base = shape.first + (shape.rows if starts[0] == 0 else 0)
-                place(c, base + start, values)
+                    at = skip + OFFSETS[k] + jnp.where(below == 1, under, SENT[k] + over)
+                    values.append(jnp.where(keep, source[pl.ds(at, TILE), :], 0.0))
+                place(c, row, values)
 
     def diagonal_rows(row):
         sides = {}
@@ -716,7 +718,7 @@
         cost(10**5),
     )
     far = lax.ppermute(side, "cross", [(0, 1), (1, 0)])
-    own, lo, hi = call(
+    own, out_chip, in_chip = call(
         pack_kernel, shape, [pl.ANY] * 5,
         [vmem((FIELDS, shape.own, shape.rows, LANES), f32), wide, wide],
         [vmem(velocity.shape, f32), vmem(block, f32), vmem(block, i32), vmem(block, i32)]
@@ -724,14 +726,14 @@
         inputs,
         cost(4 * 10**6),
     )
-    lo, hi, side = call(
-        corner_kernel, shape, [vmem] * 3, [wide, wide, full], [], held(far, lo, hi),
+    out_chip, in_chip, side = call(
+        corner_kernel, shape, [vmem] * 3, [wide, wide, full], [], held(far, out_chip, in_chip),
         cost(10**5), {1: 0, 2: 1},
     )
-    up = [(i, (i + 1) % size) for i in range(size)]
-    down = [(j, i) for i, j in up]
-    top = lax.ppermute(hi, "along", up)
-    bot = lax.ppermute(lo, "along", down)
+    firsts = [i for i in range(1, size, 2)]
+    trades = lambda pairs: pairs + [(j, i) for i, j in pairs]
+    from_out = lax.ppermute(out_chip, "along", trades([(i, (i + 1) % size) for i in firsts]))
+    from_in = lax.ppermute(in_chip, "along", trades([(i - 1, i) for i in firsts]))
     (head,) = call(
         head_kernel, shape, [smem] * 2 + [vmem], [fields(1)],
         [vmem((SHIPS, shape.chunks, TILE, LANES), f32)],
@@ -742,7 +744,7 @@
         first_kernel, shape, [vmem] * 5,
         [fields(4), fields(5), fields(1), fields(6), sums],
         [fields(4), fields(1), fields(1), corner, corner],
-        held(own, side, top, bot, head),
+        held(own, side, from_out, from_in, head),
     )
     moved, level, krylov, moments = call(
         second_kernel, shape, [vmem] * 5,

time: 73.2 us -> 71.6 us (0.978)
  waiting for transfers between devices: 8.19 us -> 1.93 us
  starting transfers between devices: 6.18 us -> 10.6 us
    ppermute x2, waiting for transfers between devices: 8.19 us -> 1.93 us  [the longest x1 1.93 us: shards(): lax.ppermute(out_chip, 'along', trades([(i, (i + 1) % size) for i in firs...]
    ppermute x2, starting transfers between devices: 2.52 us -> 6.98 us  [the longest x1 4.53 us: shards(): lax.ppermute(in_chip, 'along', trades([(i - 1, i) for i in firsts]))]
  transfers between devices with their start and end apart: 3 -> 3, of which waited for: 2 -> 1; matrix products, arithmetic and copies ran while one was open for 0% -> 0% of each run, Pallas kernels for 4% -> 4%
where the time goes in v7:
time: 71.6 us; the launch traced here: 71.4 us
  blocking collectives  35.5 us (50%)
  Pallas kernels  22.6 us (32%)
  starting transfers between devices  10.6 us (15%)
  waiting for transfers between devices  1.93 us (3%)
    all_to_all x2, blocking collectives, shared(): return lax.all_to_all(moments, ('along', 'cross'), 0, 0, tiled=True)  35.5 us
    pallas_call x7, Pallas kernels, call(): pl.pallas_call(functools.partial(kernel, shape), out_shape=outs, in_specs...  22.6 us
    ppermute x1, starting transfers between devices, shards(): lax.ppermute(in_chip, 'along', trades([(i - 1, i) for i in firsts]))  4.53 us
    ppermute x1, starting transfers between devices, shards(): far = lax.ppermute(side, 'cross', [(0, 1), (1, 0)])  3.65 us
    ppermute x1, starting transfers between devices, shards(): lax.ppermute(out_chip, 'along', trades([(i, (i + 1) % size) for i in firs...  2.45 us
    ppermute x1, waiting for transfers between devices, shards(): lax.ppermute(out_chip, 'along', trades([(i, (i + 1) % size) for i in firs...  1.93 us
  transfers between devices with their start and end apart: 3, of which 1 were waited for; matrix products, arithmetic and copies ran while one was open for 0% of the time, Pallas kernels for 4%

profile of v7, /device:TPU:1, one launch (start us, length us, event | category | flops | bytes accessed | tf_op | source)
XLA Modules:
  0.0 71.4 jit_solution(15853220327862301985)
XLA Ops:
  0.6 0.0 copy-start.1
  0.6 0.0 copy-start
  0.7 1.1 %shard_map.95 = f32[32,128]{1,0:T(8,128)S(1)} custom-call(f32[4,32,1536]{2,1,0:T(8,128)} %vel_in.3, f32[32,1536]{1,0:T(8,128)} %surface_in.3, s32[32,1536]{1,0:T(8,128)} %wet_in.3, s32[32,1536]{1,0:T(8,128)} %bathy_in.3, f32[16]{0:T(128)} %table_in.3), custom_call_target="tpu_custom_call" | custom-call | flops 100000 | bytes 100000 | tf_op jit(solution)/shard_map/pallas_call | solution.py:672
  1.7 3.7 %collective-permute-start = (f32[32,128]{1,0:T(8,128)S(1)}, f32[32,128]{1,0:T(8,128)S(1)}, u32[]{:S(2)}, u32[]{:S(2)}) collective-permute-start(f32[32,128]{1,0:T(8,128)S(1)} %shard_map.95), channel_id=1, source_target_pairs={{0,1},{1,0},{2,3},{3,2},{4,5},{5,4},{6,7},{7,6},{8,9},{9,8},{10,11... | collective-permute-start | bytes 49160 | tf_op jit(solution)/shard_map/ppermute | solution.py:720
  5.4 2.0 %shard_map.94 = (f32[7,12,32,128]{3,2,1,0:T(8,128)S(1)}, f32[1072,128]{1,0:T(8,128)S(1)}, f32[1072,128]{1,0:T(8,128)S(1)}) custom-call(f32[4,32,1536]{2,1,0:T(8,128)} %vel_in.3, f32[32,1536]{1,0:T(8,128)} %surface_in.3, s32[32,1536]{1,0:T(8,128)} %wet_in.3, s32[32,1536]{1,0:T(8,128)} %bathy_in.3, f32[16]{0:T(128)} %table_in.3), custom_call_target="tpu_custom_call" | custom-call | flops 4000000 | bytes 4000000 | tf_op jit(solution)/shard_map/pallas_call | solution.py:672
  7.3 0.0 collective-permute-done.far
  7.3 0.2 shard_map.96
  7.5 2.5 %collective-permute-start.1 = (f32[1072,128]{1,0:T(8,128)S(1)}, f32[1072,128]{1,0:T(8,128)S(1)}, u32[]{:S(2)}, u32[]{:S(2)}) collective-permute-start(f32[1072,128]{1,0:T(8,128)S(1)} %get-tuple-element.22), channel_id=1, source_target_pairs={{2,4},{6,8},{10,12},{14,16},{18,20},{22,24},{26,28},{30,32},{34,36... | collective-permute-start | bytes 1646600 | tf_op jit(solution)/shard_map/ppermute | solution.py:735
  10.0 4.5 %collective-permute-start.2 = (f32[1072,128]{1,0:T(8,128)S(1)}, f32[1072,128]{1,0:T(8,128)S(1)}, u32[]{:S(2)}, u32[]{:S(2)}) collective-permute-start(f32[1072,128]{1,0:T(8,128)S(1)} %get-tuple-element.23), channel_id=1, source_target_pairs={{0,2},{4,6},{8,10},{12,14},{16,18},{20,22},{24,26},{28,30},{32,34}... | collective-permute-start | bytes 1646600 | tf_op jit(solution)/shard_map/ppermute | solution.py:736
  14.5 0.0 copy-done.1
  14.5 0.0 copy-done
  14.5 1.0 %shard_map.97.head = f32[1,13,80,128]{3,2,1,0:T(8,128)S(1)} custom-call(s32[4,8]{1,0:T(4,128)S(1)} %bitcast.1, f32[8]{0:T(128)S(1)} %copy-done.1, f32[7,32,128]{2,1,0:T(8,128)S(1)} %get-tuple-element.21.side), custom_call_target="tpu_custom_call" | custom-call | flops 2000000 | bytes 2000000 | tf_op jit(solution)/shard_map/pallas_call | solution.py:672
  15.5 1.9 %collective-permute-done.1.out_chip = f32[1072,128]{1,0:T(8,128)S(1)} collective-permute-done((f32[1072,128]{1,0:T(8,128)S(1)}, f32[1072,128]{1,0:T(8,128)S(1)}, u32[]{:S(2)}, u32[]{:S(2)}) %collective-permute-start.1) | collective-permute-done | bytes 548896 | tf_op jit(solution)/shard_map/ppermute | solution.py:735
  17.4 0.0 collective-permute-done.2.in_chip
  17.4 8.4 %shard_map.98 = (f32[4,13,80,128]{3,2,1,0:T(8,128)S(1)}, f32[5,13,80,128]{3,2,1,0:T(8,128)S(1)}, f32[1,13,80,128]{3,2,1,0:T(8,128)S(1)}, f32[6,13,80,128]{3,2,1,0:T(8,128)S(1)}, f32[128,1,8]{2,1,0:T(1,128)S(1)}) custom-call(f32[7,12,32,128]{3,2,1,0:T(8,128)S(1)} %get-tuple-element.18.own, f32[7,32,128]{2,1,0:T(8,128)S(1)} %get-tuple-element.21.side, ...), custom_call_target="tpu_custom_call" | custom-call | tf_op jit(solution)/shard_map/pallas_call | solution.py:672
  25.8 21.7 %all_to_all.10.shares = f32[128,1,8]{2,1,0:T(1,128)S(1)} all-to-all(f32[128,1,8]{2,1,0:T(1,128)S(1)} %get-tuple-element.24), channel_id=1, replica_groups=mesh['along'=64,'cross'=2] {'along','cross'}, dimensions={0} | all-to-all | bytes 8192 | tf_op jit(solution)/shard_map/all_to_all | solution.py:689
  47.5 7.7 %shard_map.99 = (f32[4,13,80,128]{3,2,1,0:T(8,128)S(1)}, f32[1,13,80,128]{3,2,1,0:T(8,128)S(1)}, f32[6,13,80,128]{3,2,1,0:T(8,128)S(1)}, f32[128,1,8]{2,1,0:T(1,128)S(1)}) custom-call(f32[128,1,8]{2,1,0:T(1,128)S(1)} %all_to_all.10.shares, f32[4,13,80,128]{3,2,1,0:T(8,128)S(1)} %get-tuple-element.25.moved_in, ...), custom_call_target="tpu_custom_call" | custom-call | tf_op jit(solution)/shard_map/pallas_call | solution.py:672
  55.2 13.8 %all_to_all.11.shares = f32[128,1,8]{2,1,0:T(1,128)S(1)} all-to-all(f32[128,1,8]{2,1,0:T(1,128)S(1)} %get-tuple-element.29), channel_id=1, replica_groups=mesh['along'=64,'cross'=2] {'along','cross'}, dimensions={0} | all-to-all | bytes 8192 | tf_op jit(solution)/shard_map/all_to_all | solution.py:689
  69.0 2.4 %shard_map.100 = (f32[4,32,1536]{2,1,0:T(8,128)}, f32[32,1536]{1,0:T(8,128)}, f32[2,32,1536]{2,1,0:T(8,128)}) custom-call(f32[128,1,8]{2,1,0:T(1,128)S(1)} %all_to_all.11.shares, f32[4,13,80,128]{3,2,1,0:T(8,128)S(1)} %get-tuple-element.30.moved, f32[5,13,80,128]{3,2,1,0:T(8,128)S(1)} %get-tuple-element.26.static, ...), custom_call_target="tpu_custom_call" | custom-call | tf_op jit(solution)/shard_map/pallas_call | solution.py:672
Async XLA Ops:
  0.6 13.9 %copy-start.1 = (f32[8]{0:T(128)S(1)}, f32[8]{0:T(128)}, u32[]{:S(2)}) copy-start(f32[8]{0:T(128)} %heads.1) | copy-start | bytes 100
  0.6 13.9 %copy-start = (s32[8,4]{0,1:T(4,128)S(1)}, s32[8,4]{0,1:T(4,128)}, u32[]{:S(2)}) copy-start(s32[8,4]{0,1:T(4,128)} %param.12) | copy-start | bytes 388
  1.7 5.6 %collective-permute-start = (f32[32,128]{1,0:T(8,128)S(1)}, f32[32,128]{1,0:T(8,128)S(1)}, u32[]{:S(2)}, u32[]{:S(2)}) collective-permute-start(f32[32,128]{1,0:T(8,128)S(1)} %shard_map.95), channel_id=1, source_target_pairs={{0,1},{1,0},{2,3},{3,2},{4,5},{5,4},{6,7},{7,6},{8,9},{9,8},{10,11... | collective-permute-start | bytes 49160 | tf_op jit(solution)/shard_map/ppermute | solution.py:720
  7.5 9.9 %collective-permute-start.1 = (f32[1072,128]{1,0:T(8,128)S(1)}, f32[1072,128]{1,0:T(8,128)S(1)}, u32[]{:S(2)}, u32[]{:S(2)}) collective-permute-start(f32[1072,128]{1,0:T(8,128)S(1)} %get-tuple-element.22), channel_id=1, source_target_pairs={{2,4},{6,8},{10,12},{14,16},{18,20},{22,24},{26,28},{30,32},{34,36... | collective-permute-start | bytes 1646600 | tf_op jit(solution)/shard_map/ppermute | solution.py:735
  10.0 7.4 %collective-permute-start.2 = (f32[1072,128]{1,0:T(8,128)S(1)}, f32[1072,128]{1,0:T(8,128)S(1)}, u32[]{:S(2)}, u32[]{:S(2)}) collective-permute-start(f32[1072,128]{1,0:T(8,128)S(1)} %get-tuple-element.23), channel_id=1, source_target_pairs={{0,2},{4,6},{8,10},{12,14},{16,18},{20,22},{24,26},{28,30},{32,34}... | collective-permute-start | bytes 1646600 | tf_op jit(solution)/shard_map/ppermute | solution.py:736

commit v8 on v7

--- a/solution.py
+++ b/solution.py
@@ -76,12 +76,19 @@
     return lax.broadcasted_iota(jnp.int32, (TILE, LANES), 1)
 
 
-def sweep(first, tiles, body):
+def sweep(span, body, carry=None):
+    first, tiles, split, gap = span if len(span) == 4 else span + (span[1], 0)
+
     def turn(number, carry):
-        body(first + number * TILE)
-        return carry
-
-    lax.fori_loop(0, tiles, turn, 0)
+        row = first + number * TILE
+        if split < tiles:
+            row = row + jnp.where(number >= split, gap, 0)
+        if carry is None:
+            body(row)
+            return None
+        return body(row, carry)
+
+    return lax.fori_loop(0, tiles, turn, carry)
 
 
 def load(ref, index, chunk, row):
@@ -211,11 +218,8 @@
             store(krylov, 2 * level + 2 + layer, c, row, inverse * results[layer])
 
 
-def moments_of(shape, krylov, static):
-    zeros = (jnp.zeros((TILE, LANES), jnp.float32),) * (2 * ITERS)
-
-    def turn(number, sums):
-        row = shape.first + number * TILE
+def moments_of(shape, krylov, static, span, sums):
+    def turn(row, sums):
         sums = list(sums)
         for c, top, results in link_rows(shape, krylov, static, 2, row, True):
             diagonal = load(static, DIAGONAL, c, row)
@@ -234,7 +238,11 @@
                 sums = [a + b for a, b in zip(sums, terms)]
         return tuple(sums)
 
-    return lax.fori_loop(0, shape.rows // TILE, turn, zeros)
+    return sweep(span, turn, tuple(sums))
+
+
+def no_moments():
+    return (jnp.zeros((TILE, LANES), jnp.float32),) * (2 * ITERS)
 
 
 def put_moments(out, sums):
@@ -245,16 +253,12 @@
     out[...] = jnp.broadcast_to(result[0:1, None, 0 : out.shape[2]], out.shape)
 
 
-def project(shape, vel, potential, static, moved, krylov, moments, first, tiles):
-    sweep(first[0], tiles[0], functools.partial(predict_rows, shape, vel, potential, static, moved))
-    sweep(first[1], tiles[1], functools.partial(source_rows, shape, moved, static, krylov))
+def project(shape, vel, potential, static, moved, krylov, spans, sums):
+    sweep(spans[0], functools.partial(predict_rows, shape, vel, potential, static, moved))
+    sweep(spans[1], functools.partial(source_rows, shape, moved, static, krylov))
     for level in range(2):
-        sweep(
-            first[2 + level],
-            tiles[2 + level],
-            functools.partial(krylov_rows, shape, krylov, static, level),
-        )
-    put_moments(moments, moments_of(shape, krylov, static))
+        sweep(spans[2 + level], functools.partial(krylov_rows, shape, krylov, static, level))
+    return moments_of(shape, krylov, static, spans[4], sums)
 
 
 def fetch(pairs, arrived):
@@ -411,46 +415,79 @@
                 value = value + jnp.where(covered[s], columns[s, c], 0.0)
             store(head, 0, c, row, value)
 
-    sweep(GUARD, shape.total // TILE - 2, head_rows)
-
-
-def first_kernel(
-    shape, own, side, out_chip, in_chip, head,
-    moved, static, surface, krylov, moments,
-    vel, potential, thick, out_corner, in_corner,
-):
+    sweep((GUARD, shape.total // TILE - 2), head_rows)
+
+
+def place(refs, head, c, row, values):
+    moved, static, surface, krylov, vel, potential, thick = refs
+    for k in range(4):
+        store(vel, k, c, row, values[k])
+    depth = values[6]
+    inside = depth > 0.0
+    ship = jnp.where(inside, load(head, 0, c, row), 0.0)
+    store(surface, 0, c, row, values[4])
+    store(potential, 0, c, row, gravity * values[4] + ship)
+    store(thick, 0, c, row, depth)
+    store(static, CONDUCT, c, row, values[5] * depth)
+    store(static, HALF_RATE, c, row, 0.5 / jnp.where(inside, depth, 1.0))
+    store(static, HEAD, c, row, ship)
+
+
+def diagonal_rows(shape, static, thick, row):
+    sides = {}
+
+    def make(c):
+        sums = load(static, CONDUCT, c, row - 1) + load(static, CONDUCT, c, row + 1)
+        sides[c] = sums
+        return load(static, CONDUCT, c, row) + corner_weight * sums
+
+    ring = Ring(make, shape.chunks, lanes_of())
+    for c in range(shape.chunks):
+        around = ring.before(c, 1) + ring.after(c, 1) + sides[c]
+        depth = load(thick, 0, c, row)
+        diagonal = (
+            0.5 * (around + 5.0 * load(static, CONDUCT, c, row))
+            + storage * depth
+            + load(static, HALF_RATE, c, row)
+        )
+        store(static, DIAGONAL, c, row, diagonal)
+        store(static, INVERSE, c, row, jnp.where(depth > 0.0, 1.0 / diagonal, 0.0))
+        ring.done(c)
+
+
+def inner_kernel(shape, own, side, head, *refs):
+    refs, partial = refs[:7], refs[7]
+    moved, static, surface, krylov, vel, potential, thick = refs
+
+    def own_rows(row):
+        at = row - shape.first
+        for c in range(shape.chunks):
+            if c < shape.own:
+                values = [load(own, k, c, at) for k in range(FIELDS)]
+            else:
+                values = [side[k, pl.ds(at, TILE), :] for k in range(FIELDS)]
+            place(refs, head, c, row, values)
+
+    sweep((shape.first, shape.rows // TILE), own_rows)
+    middle = (shape.first + 4, shape.rows // TILE - 1)
+    sweep(middle, functools.partial(diagonal_rows, shape, static, thick))
+    spans = (middle,) * 4 + ((shape.first + 8, shape.rows // TILE - 2),)
+    sums = project(shape, vel, potential, static, moved, krylov, spans, no_moments())
+    for number, value in enumerate(sums):
+        partial[number] = value
+
+
+def outer_kernel(shape, out_chip, in_chip, head, partial, *refs):
+    refs = refs[7:]
+    moments, out_corner, in_corner = refs[7:]
+    refs = refs[:7]
+    moved, static, surface, krylov, vel, potential, thick = refs
     along = lax.axis_index("along")
     half = lax.axis_index("cross")
     for number, (k, part) in enumerate(corner_parts()):
         to = pl.ds(OFFSETS[k] + part, TILE)
         out_corner[to, :] = spread(out_chip, shape.own * SENT_ROWS, number, half)
         in_corner[to, :] = spread(in_chip, shape.own * SENT_ROWS, number, half)
-    lane = lanes_of()
-
-    def place(c, row, values):
-        for k in range(4):
-            store(vel, k, c, row, values[k])
-        depth = values[6]
-        inside = depth > 0.0
-        ship = jnp.where(inside, load(head, 0, c, row), 0.0)
-        store(surface, 0, c, row, values[4])
-        store(potential, 0, c, row, gravity * values[4] + ship)
-        store(thick, 0, c, row, depth)
-        store(static, CONDUCT, c, row, values[5] * depth)
-        store(static, HALF_RATE, c, row, 0.5 / jnp.where(inside, depth, 1.0))
-        store(static, HEAD, c, row, ship)
-
-    def own_rows(number, carry):
-        at = number * TILE
-        for c in range(shape.chunks):
-            if c < shape.own:
-                values = [load(own, k, c, at) for k in range(FIELDS)]
-            else:
-                values = [side[k, pl.ds(at, TILE), :] for k in range(FIELDS)]
-            place(c, shape.first + at, values)
-        return carry
-
-    lax.fori_loop(0, shape.rows // TILE, own_rows, 0)
     core = lax.rem(along, 2)
     deepest = SENT[0]
     last = lax.axis_size("along") - 1
@@ -464,35 +501,16 @@
                 for k in range(FIELDS):
                     at = skip + OFFSETS[k] + jnp.where(below == 1, under, SENT[k] + over)
                     values.append(jnp.where(keep, source[pl.ds(at, TILE), :], 0.0))
-                place(c, row, values)
-
-    def diagonal_rows(row):
-        sides = {}
-
-        def make(c):
-            sums = load(static, CONDUCT, c, row - 1) + load(static, CONDUCT, c, row + 1)
-            sides[c] = sums
-            return load(static, CONDUCT, c, row) + corner_weight * sums
-
-        ring = Ring(make, shape.chunks, lane)
-        for c in range(shape.chunks):
-            around = ring.before(c, 1) + ring.after(c, 1) + sides[c]
-            depth = load(thick, 0, c, row)
-            diagonal = (
-                0.5 * (around + 5.0 * load(static, CONDUCT, c, row))
-                + storage * depth
-                + load(static, HALF_RATE, c, row)
-            )
-            store(static, DIAGONAL, c, row, diagonal)
-            store(static, INVERSE, c, row, jnp.where(depth > 0.0, 1.0 / diagonal, 0.0))
-            ring.done(c)
-
-    start = GUARD
-    sweep(start + 5, 7, diagonal_rows)
-    project(
-        shape, vel, potential, static, moved, krylov, moments,
-        (start + 5, start + 6, start + 7, start + 8), (7, 7, 7, 6),
-    )
+                place(refs, head, c, row, values)
+
+    def both(halo):
+        return (shape.first - halo, 4, 2, shape.rows + 2 * halo - 4 * TILE)
+
+    sweep(both(11), functools.partial(diagonal_rows, shape, static, thick))
+    spans = tuple(both(halo) for halo in (11, 10, 9, 8))
+    spans += ((shape.first, 2, 1, shape.rows - 2 * TILE),)
+    sums = [partial[number] for number in range(2 * ITERS)]
+    put_moments(moments, project(shape, vel, potential, static, moved, krylov, spans, sums))
 
 
 def coefficients(shares):
@@ -590,13 +608,11 @@
 ):
     factors = coefficients(shares)
     start = GUARD
-    sweep(start + 8, 6, functools.partial(pressure_rows, shape, factors, krylov_in, pressure))
+    sweep((start + 8, 6), functools.partial(pressure_rows, shape, factors, krylov_in, pressure))
+    put_vel = functools.partial(store, vel)
     sweep(
-        start + 9,
-        6,
-        functools.partial(
-            move_rows, shape, moved_in, pressure, static, flux, functools.partial(store, vel)
-        ),
+        (start + 9, 6),
+        functools.partial(move_rows, shape, moved_in, pressure, static, flux, put_vel),
     )
 
     def put(c, row, value):
@@ -605,13 +621,13 @@
         store(potential, 0, c, row, gravity * value + load(static, HEAD, c, row))
 
     sweep(
-        start + 10,
-        6,
+        (start + 10, 6),
         functools.partial(surface_rows, shape, surface_in, flux, shape.chunks, put),
     )
-    project(
-        shape, vel, potential, static, moved, krylov, moments,
-        (start + 11, start + 12, start + 13, start + 14), (6, 5, 5, 5),
+    spans = ((start + 11, 6), (start + 12, 5), (start + 13, 5), (start + 14, 5))
+    spans += ((shape.first, shape.rows // TILE),)
+    put_moments(
+        moments, project(shape, vel, potential, static, moved, krylov, spans, no_moments())
     )
 
 
@@ -622,7 +638,7 @@
 ):
     factors = coefficients(shares)
     start = shape.first
-    sweep(start - 2, 5, functools.partial(pressure_rows, shape, factors, krylov, pressure))
+    sweep((start - 2, 5), functools.partial(pressure_rows, shape, factors, krylov, pressure))
 
     def put_vel(part, c, row, value):
         if c < shape.own:
@@ -634,8 +650,7 @@
                 )
 
     sweep(
-        start,
-        shape.rows // TILE,
+        (start, shape.rows // TILE),
         functools.partial(move_rows, shape, moved, pressure, static, flux, put_vel),
     )
     for row in (start - 1, start + shape.rows):
@@ -658,8 +673,7 @@
         new_surface[pl.ds(at, TILE), pl.ds(c * LANES, LANES)] = value
 
     sweep(
-        start,
-        shape.rows // TILE,
+        (start, shape.rows // TILE),
         functools.partial(surface_rows, shape, surface, flux, shape.own, put),
     )
 
@@ -732,7 +746,8 @@
     )
     firsts = [i for i in range(1, size, 2)]
     trades = lambda pairs: pairs + [(j, i) for i, j in pairs]
-    from_out = lax.ppermute(out_chip, "along", trades([(i, (i + 1) % size) for i in firsts]))
+    out_pairs = trades([(i, i + 1) for i in firsts[:-1]]) + [(0, 0), (size - 1, size - 1)]
+    from_out = lax.ppermute(out_chip, "along", out_pairs)
     from_in = lax.ppermute(in_chip, "along", trades([(i - 1, i) for i in firsts]))
     (head,) = call(
         head_kernel, shape, [smem] * 2 + [vmem], [fields(1)],
@@ -740,11 +755,17 @@
         (hull_ranges.T, hull_pressure) + held(side),
         cost(2 * 10**6),
     )
-    moved, static, level, krylov, moments = call(
-        first_kernel, shape, [vmem] * 5,
-        [fields(4), fields(5), fields(1), fields(6), sums],
-        [fields(4), fields(1), fields(1), corner, corner],
-        held(own, side, from_out, from_in, head),
+    state = [fields(count) for count in (4, 5, 1, 6, 4, 1, 1)]
+    partial = vmem((2 * ITERS, TILE, LANES), f32)
+    *inner, partial = call(
+        inner_kernel, shape, [vmem] * 3, state + [partial], [],
+        held(own, side, head),
+        cost(10**7),
+    )
+    moved, static, level, krylov, _, _, _, moments = call(
+        outer_kernel, shape, [vmem] * 11, state + [sums], [corner, corner],
+        held(from_out, from_in, head, partial, *inner),
+        cost(10**7), {4 + number: number for number in range(7)},
     )
     moved, level, krylov, moments = call(
         second_kernel, shape, [vmem] * 5,

time: 71.6 us -> 72.6 us (1.014)
  Pallas kernels: 22.6 us -> 26.9 us
  starting transfers between devices: 10.6 us -> 8.02 us
  blocking collectives: 35.5 us -> 34.4 us
    ppermute x1, starting transfers between devices: 4.53 us -> 0.09 us  [shards(): lax.ppermute(in_chip, 'along', trades([(i - 1, i) for i in firsts]))]
    pallas_call x7 -> x8, Pallas kernels: 22.6 us -> 26.9 us  [call(): pl.pallas_call(functools.partial(kernel, shape), out_shape=outs, in_specs...]
    ppermute x1, starting transfers between devices: 2.45 us -> 4.28 us  [shards(): from_out = lax.ppermute(out_chip, 'along', out_pairs)]
    all_to_all x2, blocking collectives: 35.5 us -> 34.4 us  [shared(): return lax.all_to_all(moments, ('along', 'cross'), 0, 0, tiled=True)]
  transfers between devices with their start and end apart: 3 -> 3, of which waited for: 1 -> 1; matrix products, arithmetic and copies ran while one was open for 0% -> 0% of each run, Pallas kernels for 4% -> 9%
where the time goes in v8:
time: 72.6 us; the launch traced here: 72.4 us
  blocking collectives  34.4 us (47%)
  Pallas kernels  26.9 us (37%)
  starting transfers between devices  8.02 us (11%)
  waiting for transfers between devices  2.34 us (3%)
  between operations  0.74 us (1%)
    all_to_all x2, blocking collectives, shared(): return lax.all_to_all(moments, ('along', 'cross'), 0, 0, tiled=True)  34.4 us
    pallas_call x8, Pallas kernels, call(): pl.pallas_call(functools.partial(kernel, shape), out_shape=outs, in_specs...  26.9 us
    ppermute x1, starting transfers between devices, shards(): from_out = lax.ppermute(out_chip, 'along', out_pairs)  4.28 us
    ppermute x1, starting transfers between devices, shards(): far = lax.ppermute(side, 'cross', [(0, 1), (1, 0)])  3.65 us
    ppermute x1, waiting for transfers between devices, shards(): from_out = lax.ppermute(out_chip, 'along', out_pairs)  2.34 us
  transfers between devices with their start and end apart: 3, of which 1 were waited for; matrix products, arithmetic and copies ran while one was open for 0% of the time, Pallas kernels for 9%

profile of v8, /device:TPU:1, one launch (start us, length us, event | category | flops | bytes accessed | tf_op | source)
XLA Modules:
  0.0 72.4 jit_solution(11325664479741234211)
XLA Ops:
  0.6 0.0 copy-start.1
  0.6 0.0 copy-start
  0.7 1.1 %shard_map.94 = f32[32,128]{1,0:T(8,128)S(1)} custom-call(f32[4,32,1536]{2,1,0:T(8,128)} %vel_in.3, f32[32,1536]{1,0:T(8,128)} %surface_in.3, s32[32,1536]{1,0:T(8,128)} %wet_in.3, s32[32,1536]{1,0:T(8,128)} %bathy_in.3, f32[16]{0:T(128)} %table_in.3), custom_call_target="tpu_custom_call" | custom-call | flops 100000 | bytes 100000 | tf_op jit(solution)/shard_map/pallas_call | solution.py:686
  1.7 3.7 %collective-permute-start = (f32[32,128]{1,0:T(8,128)S(1)}, f32[32,128]{1,0:T(8,128)S(1)}, u32[]{:S(2)}, u32[]{:S(2)}) collective-permute-start(f32[32,128]{1,0:T(8,128)S(1)} %shard_map.94), channel_id=1, source_target_pairs={{0,1},{1,0},{2,3},{3,2},{4,5},{5,4},{6,7},{7,6},{8,9},{9,8},{10,11... | collective-permute-start | bytes 49160 | tf_op jit(solution)/shard_map/ppermute | solution.py:734
  5.4 2.0 %shard_map.95 = (f32[7,12,32,128]{3,2,1,0:T(8,128)S(1)}, f32[1072,128]{1,0:T(8,128)S(1)}, f32[1072,128]{1,0:T(8,128)S(1)}) custom-call(f32[4,32,1536]{2,1,0:T(8,128)} %vel_in.3, f32[32,1536]{1,0:T(8,128)} %surface_in.3, s32[32,1536]{1,0:T(8,128)} %wet_in.3, s32[32,1536]{1,0:T(8,128)} %bathy_in.3, f32[16]{0:T(128)} %table_in.3), custom_call_target="tpu_custom_call" | custom-call | flops 4000000 | bytes 4000000 | tf_op jit(solution)/shard_map/pallas_call | solution.py:686
  7.3 0.0 collective-permute-done.far
  7.3 0.2 shard_map.96
  7.5 4.3 %collective-permute-start.1 = (f32[1072,128]{1,0:T(8,128)S(1)}, f32[1072,128]{1,0:T(8,128)S(1)}, u32[]{:S(2)}, u32[]{:S(2)}) collective-permute-start(f32[1072,128]{1,0:T(8,128)S(1)} %get-tuple-element.28), channel_id=1, source_target_pairs={{2,4},{6,8},{10,12},{14,16},{18,20},{22,24},{26,28},{30,32},{34,36... | collective-permute-start | bytes 1646600 | tf_op jit(solution)/shard_map/ppermute | solution.py:750
  11.8 0.1 collective-permute-start.2
  11.9 0.0 copy-done.1
  11.9 0.0 copy-done
  11.9 1.0 %shard_map.97.head = f32[1,13,80,128]{3,2,1,0:T(8,128)S(1)} custom-call(s32[4,8]{1,0:T(4,128)S(1)} %bitcast.1, f32[8]{0:T(128)S(1)} %copy-done.1, f32[7,32,128]{2,1,0:T(8,128)S(1)} %get-tuple-element.30.side), custom_call_target="tpu_custom_call" | custom-call | flops 2000000 | bytes 2000000 | tf_op jit(solution)/shard_map/pallas_call | solution.py:686
  12.9 3.7 %shard_map.98 = (f32[4,13,80,128]{3,2,1,0:T(8,128)S(1)}, f32[5,13,80,128]{3,2,1,0:T(8,128)S(1)}, f32[1,13,80,128]{3,2,1,0:T(8,128)S(1)}, f32[6,13,80,128]{3,2,1,...) custom-call(f32[7,12,32,128]{3,2,1,0:T(8,128)S(1)} %get-tuple-elemen, ...), custom_call_target="tpu_custom_call" | custom-call | flops 10000000 | bytes 10000000 | tf_op jit(solution)/shard_map/pallas_call | solution.py:686
  16.6 2.3 %collective-permute-done.1.out_chip = f32[1072,128]{1,0:T(8,128)S(1)} collective-permute-done((f32[1072,128]{1,0:T(8,128)S(1)}, f32[1072,128]{1,0:T(8,128)S(1)}, u32[]{:S(2)}, u32[]{:S(2)}) %collective-permute-start.1) | collective-permute-done | bytes 548896 | tf_op jit(solution)/shard_map/ppermute | solution.py:750
  18.9 0.0 collective-permute-done.2.in_chip
  18.9 8.9 %shard_map.99 = (f32[4,13,80,128]{3,2,1,0:T(8,128)S(1)}, f32[5,13,80,128]{3,2,1,0:T(8,128)S(1)}, f32[1,13,80,128]{3,2,1,0:T(8,128)S(1)}, f32[6,13,80,128]{3,2,1,...) custom-call(f32[1072,128]{1,0:T(8,128)S(1)} %collective-permute-done, ...), custom_call_target="tpu_custom_call", output_to_operand_aliasing={{0}: (4, {}), {1}: (5, {}), {2}: (6, {}), {3}: (7, {}), {4}... | custom-call | flops 10000000 | bytes 10000000 | tf_op jit(solution)/shard_map/pallas_call | solution.py:686
  27.9 20.6 %all_to_all.10.shares = f32[128,1,8]{2,1,0:T(1,128)S(1)} all-to-all(f32[128,1,8]{2,1,0:T(1,128)S(1)} %get-tuple-element.40), channel_id=1, replica_groups=mesh['along'=64,'cross'=2] {'along','cross'}, dimensions={0} | all-to-all | bytes 8192 | tf_op jit(solution)/shard_map/all_to_all | solution.py:703
  48.5 7.7 %shard_map.100 = (f32[4,13,80,128]{3,2,1,0:T(8,128)S(1)}, f32[1,13,80,128]{3,2,1,0:T(8,128)S(1)}, f32[6,13,80,128]{3,2,1,0:T(8,128)S(1)}, f32[128,1,8]{2,1,0:T(1,128)S(1)}) custom-call(f32[128,1,8]{2,1,0:T(1,128)S(1)} %all_to_all.10.shares, f32[4,13,80,128]{3,2,1,0:T(8,128)S(1)} %get-tuple-element.41.moved_in, ...), custom_call_target="tpu_custom_call" | custom-call | tf_op jit(solution)/shard_map/pallas_call | solution.py:686
  56.2 13.8 %all_to_all.11.shares = f32[128,1,8]{2,1,0:T(1,128)S(1)} all-to-all(f32[128,1,8]{2,1,0:T(1,128)S(1)} %get-tuple-element.45), channel_id=1, replica_groups=mesh['along'=64,'cross'=2] {'along','cross'}, dimensions={0} | all-to-all | bytes 8192 | tf_op jit(solution)/shard_map/all_to_all | solution.py:703
  70.0 2.4 %shard_map.101 = (f32[4,32,1536]{2,1,0:T(8,128)}, f32[32,1536]{1,0:T(8,128)}, f32[2,32,1536]{2,1,0:T(8,128)}) custom-call(f32[128,1,8]{2,1,0:T(1,128)S(1)} %all_to_all.11.shares, f32[4,13,80,128]{3,2,1,0:T(8,128)S(1)} %get-tuple-element.46.moved, f32[5,13,80,128]{3,2,1,0:T(8,128)S(1)} %get-tuple-element.42.static, ...), custom_call_target="tpu_custom_call" | custom-call | tf_op jit(solution)/shard_map/pallas_call | solution.py:686
Async XLA Ops:
  0.6 11.3 %copy-start.1 = (f32[8]{0:T(128)S(1)}, f32[8]{0:T(128)}, u32[]{:S(2)}) copy-start(f32[8]{0:T(128)} %heads.1) | copy-start | bytes 100
  0.6 11.3 %copy-start = (s32[8,4]{0,1:T(4,128)S(1)}, s32[8,4]{0,1:T(4,128)}, u32[]{:S(2)}) copy-start(s32[8,4]{0,1:T(4,128)} %param.12) | copy-start | bytes 388
  1.7 5.6 %collective-permute-start = (f32[32,128]{1,0:T(8,128)S(1)}, f32[32,128]{1,0:T(8,128)S(1)}, u32[]{:S(2)}, u32[]{:S(2)}) collective-permute-start(f32[32,128]{1,0:T(8,128)S(1)} %shard_map.94), channel_id=1, source_target_pairs={{0,1},{1,0},{2,3},{3,2},{4,5},{5,4},{6,7},{7,6},{8,9},{9,8},{10,11... | collective-permute-start | bytes 49160 | tf_op jit(solution)/shard_map/ppermute | solution.py:734
  7.5 11.4 %collective-permute-start.1 = (f32[1072,128]{1,0:T(8,128)S(1)}, f32[1072,128]{1,0:T(8,128)S(1)}, u32[]{:S(2)}, u32[]{:S(2)}) collective-permute-start(f32[1072,128]{1,0:T(8,128)S(1)} %get-tuple-element.28), channel_id=1, source_target_pairs={{2,4},{6,8},{10,12},{14,16},{18,20},{22,24},{26,28},{30,32},{34,36... | collective-permute-start | bytes 1646600 | tf_op jit(solution)/shard_map/ppermute | solution.py:750
  11.8 7.1 %collective-permute-start.2 = (f32[1072,128]{1,0:T(8,128)S(1)}, f32[1072,128]{1,0:T(8,128)S(1)}, u32[]{:S(2)}, u32[]{:S(2)}) collective-permute-start(f32[1072,128]{1,0:T(8,128)S(1)} %get-tuple-element.29), channel_id=1, source_target_pairs={{0,2},{4,6},{8,10},{12,14},{16,18},{20,22},{24,26},{28,30},{32,34}... | collective-permute-start | bytes 1646600 | tf_op jit(solution)/shard_map/ppermute | solution.py:751

commit v9 on v8

--- a/solution.py
+++ b/solution.py
@@ -76,19 +76,18 @@
     return lax.broadcasted_iota(jnp.int32, (TILE, LANES), 1)
 
 
-def sweep(span, body, carry=None):
-    first, tiles, split, gap = span if len(span) == 4 else span + (span[1], 0)
-
-    def turn(number, carry):
-        row = first + number * TILE
-        if split < tiles:
-            row = row + jnp.where(number >= split, gap, 0)
-        if carry is None:
-            body(row)
-            return None
-        return body(row, carry)
-
-    return lax.fori_loop(0, tiles, turn, carry)
+def sweep(spans, body, carry=None):
+    for first, tiles in spans:
+
+        def turn(number, carry, first=first):
+            row = first + number * TILE
+            if carry is None:
+                body(row)
+                return None
+            return body(row, carry)
+
+        carry = lax.fori_loop(0, tiles, turn, carry)
+    return carry
 
 
 def load(ref, index, chunk, row):
@@ -415,7 +414,7 @@
                 value = value + jnp.where(covered[s], columns[s, c], 0.0)
             store(head, 0, c, row, value)
 
-    sweep((GUARD, shape.total // TILE - 2), head_rows)
+    sweep([(GUARD, shape.total // TILE - 2)], head_rows)
 
 
 def place(refs, head, c, row, values):
@@ -468,10 +467,10 @@
                 values = [side[k, pl.ds(at, TILE), :] for k in range(FIELDS)]
             place(refs, head, c, row, values)
 
-    sweep((shape.first, shape.rows // TILE), own_rows)
-    middle = (shape.first + 4, shape.rows // TILE - 1)
+    sweep([(shape.first, shape.rows // TILE)], own_rows)
+    middle = [(shape.first + 4, shape.rows // TILE - 1)]
     sweep(middle, functools.partial(diagonal_rows, shape, static, thick))
-    spans = (middle,) * 4 + ((shape.first + 8, shape.rows // TILE - 2),)
+    spans = [middle] * 4 + [[(shape.first + 8, shape.rows // TILE - 2)]]
     sums = project(shape, vel, potential, static, moved, krylov, spans, no_moments())
     for number, value in enumerate(sums):
         partial[number] = value
@@ -488,27 +487,34 @@
         to = pl.ds(OFFSETS[k] + part, TILE)
         out_corner[to, :] = spread(out_chip, shape.own * SENT_ROWS, number, half)
         in_corner[to, :] = spread(in_chip, shape.own * SENT_ROWS, number, half)
-    core = lax.rem(along, 2)
     deepest = SENT[0]
     last = lax.axis_size("along") - 1
-    for wide, narrow, below in ((out_chip, out_corner, core), (in_chip, in_corner, 1 - core)):
-        keep = jnp.where(below == 1, last - along, along) > 0
-        for over, under in ((-deepest, 0), (-TILE, deepest - TILE)):
-            row = shape.first + jnp.where(below == 1, shape.rows + under, over)
+
+    def place_piece(wide, narrow, below):
+        keep = (last - along if below else along) > 0
+        for start in (0, deepest - TILE) if below else (-deepest, -TILE):
             for c in range(shape.chunks):
                 source, skip = (wide, c * SENT_ROWS) if c < shape.own else (narrow, 0)
                 values = []
                 for k in range(FIELDS):
-                    at = skip + OFFSETS[k] + jnp.where(below == 1, under, SENT[k] + over)
+                    at = skip + OFFSETS[k] + start + (0 if below else SENT[k])
                     values.append(jnp.where(keep, source[pl.ds(at, TILE), :], 0.0))
-                place(refs, head, c, row, values)
+                place(refs, head, c, shape.first + start + (shape.rows if below else 0), values)
+
+    core = lax.rem(along, 2)
+    for which in range(2):
+
+        @pl.when(core == which)
+        def _(which=which):
+            place_piece(out_chip, out_corner, which == 1)
+            place_piece(in_chip, in_corner, which == 0)
 
     def both(halo):
-        return (shape.first - halo, 4, 2, shape.rows + 2 * halo - 4 * TILE)
+        return [(shape.first - halo, 2), (shape.first + shape.rows + halo - 2 * TILE, 2)]
 
     sweep(both(11), functools.partial(diagonal_rows, shape, static, thick))
-    spans = tuple(both(halo) for halo in (11, 10, 9, 8))
-    spans += ((shape.first, 2, 1, shape.rows - 2 * TILE),)
+    spans = [both(halo) for halo in (11, 10, 9, 8)]
+    spans += [[(shape.first, 1), (shape.first + shape.rows - TILE, 1)]]
     sums = [partial[number] for number in range(2 * ITERS)]
     put_moments(moments, project(shape, vel, potential, static, moved, krylov, spans, sums))
 
@@ -608,10 +614,10 @@
 ):
     factors = coefficients(shares)
     start = GUARD
-    sweep((start + 8, 6), functools.partial(pressure_rows, shape, factors, krylov_in, pressure))
+    sweep([(start + 8, 6)], functools.partial(pressure_rows, shape, factors, krylov_in, pressure))
     put_vel = functools.partial(store, vel)
     sweep(
-        (start + 9, 6),
+        [(start + 9, 6)],
         functools.partial(move_rows, shape, moved_in, pressure, static, flux, put_vel),
     )
 
@@ -621,11 +627,11 @@
         store(potential, 0, c, row, gravity * value + load(static, HEAD, c, row))
 
     sweep(
-        (start + 10, 6),
+        [(start + 10, 6)],
         functools.partial(surface_rows, shape, surface_in, flux, shape.chunks, put),
     )
-    spans = ((start + 11, 6), (start + 12, 5), (start + 13, 5), (start + 14, 5))
-    spans += ((shape.first, shape.rows // TILE),)
+    spans = [[(start + 11, 6)], [(start + 12, 5)], [(start + 13, 5)], [(start + 14, 5)]]
+    spans += [[(shape.first, shape.rows // TILE)]]
     put_moments(
         moments, project(shape, vel, potential, static, moved, krylov, spans, no_moments())
     )
@@ -638,7 +644,7 @@
 ):
     factors = coefficients(shares)
     start = shape.first
-    sweep((start - 2, 5), functools.partial(pressure_rows, shape, factors, krylov, pressure))
+    sweep([(start - 2, 5)], functools.partial(pressure_rows, shape, factors, krylov, pressure))
 
     def put_vel(part, c, row, value):
         if c < shape.own:
@@ -650,7 +656,7 @@
                 )
 
     sweep(
-        (start, shape.rows // TILE),
+        [(start, shape.rows // TILE)],
         functools.partial(move_rows, shape, moved, pressure, static, flux, put_vel),
     )
     for row in (start - 1, start + shape.rows):
@@ -673,7 +679,7 @@
         new_surface[pl.ds(at, TILE), pl.ds(c * LANES, LANES)] = value
 
     sweep(
-        (start, shape.rows // TILE),
+        [(start, shape.rows // TILE)],
         functools.partial(surface_rows, shape, surface, flux, shape.own, put),
     )
 
@@ -746,8 +752,9 @@
     )
     firsts = [i for i in range(1, size, 2)]
     trades = lambda pairs: pairs + [(j, i) for i, j in pairs]
-    out_pairs = trades([(i, i + 1) for i in firsts[:-1]]) + [(0, 0), (size - 1, size - 1)]
-    from_out = lax.ppermute(out_chip, "along", out_pairs)
+    ends = [(0, 1), (2 * size - 2, 2 * size - 1)]
+    next_chip = [(2 * i + j, 2 * i + 2 + j) for i in firsts[:-1] for j in range(2)]
+    from_out = lax.ppermute(out_chip, ("along", "cross"), trades(next_chip + ends))
     from_in = lax.ppermute(in_chip, "along", trades([(i - 1, i) for i in firsts]))
     (head,) = call(
         head_kernel, shape, [smem] * 2 + [vmem], [fields(1)],

time: 72.6 us -> 66.8 us (0.920)
  Pallas kernels: 26.9 us -> 22.9 us
  waiting for transfers between devices: 2.34 us -> 0.92 us
    pallas_call x8, Pallas kernels: 26.9 us -> 22.9 us  [call(): pl.pallas_call(functools.partial(kernel, shape), out_shape=outs, in_specs...]
    ppermute x1, starting transfers between devices: 4.28 us -> 2.45 us  [shards(): lax.ppermute(out_chip, ('along', 'cross'), trades(next_chip + ends))]
    ppermute x1, starting transfers between devices: 0.09 us -> 1.84 us  [shards(): lax.ppermute(in_chip, 'along', trades([(i - 1, i) for i in firsts]))]
    ppermute x1, waiting for transfers between devices: 2.34 us -> 0.91 us  [shards(): lax.ppermute(out_chip, ('along', 'cross'), trades(next_chip + ends))]
  transfers between devices with their start and end apart: 3 -> 3, of which waited for: 1 -> 1; matrix products, arithmetic and copies ran while one was open for 0% -> 0% of each run, Pallas kernels for 9% -> 10%
where the time goes in v9:
time: 66.8 us; the launch traced here: 66.6 us
  blocking collectives  34.1 us (51%)
  Pallas kernels  22.9 us (34%)
  starting transfers between devices  7.94 us (12%)
  waiting for transfers between devices  0.92 us (1%)
  between operations  0.71 us (1%)
    all_to_all x2, blocking collectives, shared(): return lax.all_to_all(moments, ('along', 'cross'), 0, 0, tiled=True)  34.1 us
    pallas_call x8, Pallas kernels, call(): pl.pallas_call(functools.partial(kernel, shape), out_shape=outs, in_specs...  22.9 us
    ppermute x1, starting transfers between devices, shards(): far = lax.ppermute(side, 'cross', [(0, 1), (1, 0)])  3.65 us
    ppermute x1, starting transfers between devices, shards(): lax.ppermute(out_chip, ('along', 'cross'), trades(next_chip + ends))  2.45 us
    ppermute x1, starting transfers between devices, shards(): lax.ppermute(in_chip, 'along', trades([(i - 1, i) for i in firsts]))  1.84 us
  transfers between devices with their start and end apart: 3, of which 1 were waited for; matrix products, arithmetic and copies ran while one was open for 0% of the time, Pallas kernels for 10%

profile of v9, /device:TPU:1, one launch (start us, length us, event | category | flops | bytes accessed | tf_op | source)
XLA Modules:
  0.0 66.6 jit_solution(17996227731924834175)
XLA Ops:
  0.6 0.0 copy-start.1
  0.6 0.0 copy-start
  0.7 1.1 %shard_map.94 = f32[32,128]{1,0:T(8,128)S(1)} custom-call(f32[4,32,1536]{2,1,0:T(8,128)} %vel_in.3, f32[32,1536]{1,0:T(8,128)} %surface_in.3, s32[32,1536]{1,0:T(8,128)} %wet_in.3, s32[32,1536]{1,0:T(8,128)} %bathy_in.3, f32[16]{0:T(128)} %table_in.3), custom_call_target="tpu_custom_call" | custom-call | flops 100000 | bytes 100000 | tf_op jit(solution)/shard_map/pallas_call | solution.py:692
  1.7 3.7 %collective-permute-start = (f32[32,128]{1,0:T(8,128)S(1)}, f32[32,128]{1,0:T(8,128)S(1)}, u32[]{:S(2)}, u32[]{:S(2)}) collective-permute-start(f32[32,128]{1,0:T(8,128)S(1)} %shard_map.94), channel_id=1, source_target_pairs={{0,1},{1,0},{2,3},{3,2},{4,5},{5,4},{6,7},{7,6},{8,9},{9,8},{10,11... | collective-permute-start | bytes 49160 | tf_op jit(solution)/shard_map/ppermute | solution.py:740
  5.4 2.0 %shard_map.95 = (f32[7,12,32,128]{3,2,1,0:T(8,128)S(1)}, f32[1072,128]{1,0:T(8,128)S(1)}, f32[1072,128]{1,0:T(8,128)S(1)}) custom-call(f32[4,32,1536]{2,1,0:T(8,128)} %vel_in.3, f32[32,1536]{1,0:T(8,128)} %surface_in.3, s32[32,1536]{1,0:T(8,128)} %wet_in.3, s32[32,1536]{1,0:T(8,128)} %bathy_in.3, f32[16]{0:T(128)} %table_in.3), custom_call_target="tpu_custom_call" | custom-call | flops 4000000 | bytes 4000000 | tf_op jit(solution)/shard_map/pallas_call | solution.py:692
  7.3 0.0 collective-permute-done.far
  7.3 0.2 shard_map.96
  7.5 2.4 %collective-permute-start.1 = (f32[1072,128]{1,0:T(8,128)S(1)}, f32[1072,128]{1,0:T(8,128)S(1)}, u32[]{:S(2)}, u32[]{:S(2)}) collective-permute-start(f32[1072,128]{1,0:T(8,128)S(1)} %get-tuple-element.28), channel_id=1, source_target_pairs={{2,4},{3,5},{6,8},{7,9},{10,12},{11,13},{14,16},{15,17},{18,20},{1... | collective-permute-start | bytes 1646600 | tf_op jit(solution)/shard_map/ppermute | solution.py:757
  10.0 1.8 %collective-permute-start.2 = (f32[1072,128]{1,0:T(8,128)S(1)}, f32[1072,128]{1,0:T(8,128)S(1)}, u32[]{:S(2)}, u32[]{:S(2)}) collective-permute-start(f32[1072,128]{1,0:T(8,128)S(1)} %get-tuple-element.29), channel_id=1, source_target_pairs={{0,2},{4,6},{8,10},{12,14},{16,18},{20,22},{24,26},{28,30},{32,34}... | collective-permute-start | bytes 1646600 | tf_op jit(solution)/shard_map/ppermute | solution.py:758
  11.8 0.0 copy-done.1
  11.8 0.0 copy-done
  11.8 1.0 %shard_map.97.head = f32[1,13,80,128]{3,2,1,0:T(8,128)S(1)} custom-call(s32[4,8]{1,0:T(4,128)S(1)} %bitcast.1, f32[8]{0:T(128)S(1)} %copy-done.1, f32[7,32,128]{2,1,0:T(8,128)S(1)} %get-tuple-element.30.side), custom_call_target="tpu_custom_call" | custom-call | flops 2000000 | bytes 2000000 | tf_op jit(solution)/shard_map/pallas_call | solution.py:692
  12.8 3.7 %shard_map.98 = (f32[4,13,80,128]{3,2,1,0:T(8,128)S(1)}, f32[5,13,80,128]{3,2,1,0:T(8,128)S(1)}, f32[1,13,80,128]{3,2,1,0:T(8,128)S(1)}, f32[6,13,80,128]{3,2,1,...) custom-call(f32[7,12,32,128]{3,2,1,0:T(8,128)S(1)} %get-tuple-elemen, ...), custom_call_target="tpu_custom_call" | custom-call | flops 10000000 | bytes 10000000 | tf_op jit(solution)/shard_map/pallas_call | solution.py:692
  16.5 0.9 %collective-permute-done.1.out_chip = f32[1072,128]{1,0:T(8,128)S(1)} collective-permute-done((f32[1072,128]{1,0:T(8,128)S(1)}, f32[1072,128]{1,0:T(8,128)S(1)}, u32[]{:S(2)}, u32[]{:S(2)}) %collective-permute-start.1) | collective-permute-done | bytes 548896 | tf_op jit(solution)/shard_map/ppermute | solution.py:757
  17.4 0.0 collective-permute-done.2.in_chip
  17.4 4.9 %shard_map.99 = (f32[4,13,80,128]{3,2,1,0:T(8,128)S(1)}, f32[5,13,80,128]{3,2,1,0:T(8,128)S(1)}, f32[1,13,80,128]{3,2,1,0:T(8,128)S(1)}, f32[6,13,80,128]{3,2,1,...) custom-call(f32[1072,128]{1,0:T(8,128)S(1)} %collective-permute-done, ...), custom_call_target="tpu_custom_call", output_to_operand_aliasing={{0}: (4, {}), {1}: (5, {}), {2}: (6, {}), {3}: (7, {}), {4}... | custom-call | flops 10000000 | bytes 10000000 | tf_op jit(solution)/shard_map/pallas_call | solution.py:692
  22.3 20.3 %all_to_all.10.shares = f32[128,1,8]{2,1,0:T(1,128)S(1)} all-to-all(f32[128,1,8]{2,1,0:T(1,128)S(1)} %get-tuple-element.40), channel_id=1, replica_groups=mesh['along'=64,'cross'=2] {'along','cross'}, dimensions={0} | all-to-all | bytes 8192 | tf_op jit(solution)/shard_map/all_to_all | solution.py:709
  42.6 7.7 %shard_map.100 = (f32[4,13,80,128]{3,2,1,0:T(8,128)S(1)}, f32[1,13,80,128]{3,2,1,0:T(8,128)S(1)}, f32[6,13,80,128]{3,2,1,0:T(8,128)S(1)}, f32[128,1,8]{2,1,0:T(1,128)S(1)}) custom-call(f32[128,1,8]{2,1,0:T(1,128)S(1)} %all_to_all.10.shares, f32[4,13,80,128]{3,2,1,0:T(8,128)S(1)} %get-tuple-element.41.moved_in, ...), custom_call_target="tpu_custom_call" | custom-call | tf_op jit(solution)/shard_map/pallas_call | solution.py:692
  50.4 13.8 %all_to_all.11.shares = f32[128,1,8]{2,1,0:T(1,128)S(1)} all-to-all(f32[128,1,8]{2,1,0:T(1,128)S(1)} %get-tuple-element.45), channel_id=1, replica_groups=mesh['along'=64,'cross'=2] {'along','cross'}, dimensions={0} | all-to-all | bytes 8192 | tf_op jit(solution)/shard_map/all_to_all | solution.py:709
  64.2 2.4 %shard_map.101 = (f32[4,32,1536]{2,1,0:T(8,128)}, f32[32,1536]{1,0:T(8,128)}, f32[2,32,1536]{2,1,0:T(8,128)}) custom-call(f32[128,1,8]{2,1,0:T(1,128)S(1)} %all_to_all.11.shares, f32[4,13,80,128]{3,2,1,0:T(8,128)S(1)} %get-tuple-element.46.moved, f32[5,13,80,128]{3,2,1,0:T(8,128)S(1)} %get-tuple-element.42.static, ...), custom_call_target="tpu_custom_call" | custom-call | tf_op jit(solution)/shard_map/pallas_call | solution.py:692
Async XLA Ops:
  0.6 11.2 %copy-start.1 = (f32[8]{0:T(128)S(1)}, f32[8]{0:T(128)}, u32[]{:S(2)}) copy-start(f32[8]{0:T(128)} %heads.1) | copy-start | bytes 100
  0.6 11.2 %copy-start = (s32[8,4]{0,1:T(4,128)S(1)}, s32[8,4]{0,1:T(4,128)}, u32[]{:S(2)}) copy-start(s32[8,4]{0,1:T(4,128)} %param.12) | copy-start | bytes 388
  1.7 5.6 %collective-permute-start = (f32[32,128]{1,0:T(8,128)S(1)}, f32[32,128]{1,0:T(8,128)S(1)}, u32[]{:S(2)}, u32[]{:S(2)}) collective-permute-start(f32[32,128]{1,0:T(8,128)S(1)} %shard_map.94), channel_id=1, source_target_pairs={{0,1},{1,0},{2,3},{3,2},{4,5},{5,4},{6,7},{7,6},{8,9},{9,8},{10,11... | collective-permute-start | bytes 49160 | tf_op jit(solution)/shard_map/ppermute | solution.py:740
  7.5 9.9 %collective-permute-start.1 = (f32[1072,128]{1,0:T(8,128)S(1)}, f32[1072,128]{1,0:T(8,128)S(1)}, u32[]{:S(2)}, u32[]{:S(2)}) collective-permute-start(f32[1072,128]{1,0:T(8,128)S(1)} %get-tuple-element.28), channel_id=1, source_target_pairs={{2,4},{3,5},{6,8},{7,9},{10,12},{11,13},{14,16},{15,17},{18,20},{1... | collective-permute-start | bytes 1646600 | tf_op jit(solution)/shard_map/ppermute | solution.py:757
  10.0 7.4 %collective-permute-start.2 = (f32[1072,128]{1,0:T(8,128)S(1)}, f32[1072,128]{1,0:T(8,128)S(1)}, u32[]{:S(2)}, u32[]{:S(2)}) collective-permute-start(f32[1072,128]{1,0:T(8,128)S(1)} %get-tuple-element.29), channel_id=1, source_target_pairs={{0,2},{4,6},{8,10},{12,14},{16,18},{20,22},{24,26},{28,30},{32,34}... | collective-permute-start | bytes 1646600 | tf_op jit(solution)/shard_map/ppermute | solution.py:758

commit v10 on v9

--- a/solution.py
+++ b/solution.py
@@ -476,47 +476,52 @@
         partial[number] = value
 
 
-def outer_kernel(shape, out_chip, in_chip, head, partial, *refs):
+def halo_kernel(shape, from_chip, received, head, partial, *refs):
     refs = refs[7:]
-    moments, out_corner, in_corner = refs[7:]
+    out, narrow = refs[7:]
     refs = refs[:7]
     moved, static, surface, krylov, vel, potential, thick = refs
     along = lax.axis_index("along")
     half = lax.axis_index("cross")
     for number, (k, part) in enumerate(corner_parts()):
         to = pl.ds(OFFSETS[k] + part, TILE)
-        out_corner[to, :] = spread(out_chip, shape.own * SENT_ROWS, number, half)
-        in_corner[to, :] = spread(in_chip, shape.own * SENT_ROWS, number, half)
+        narrow[to, :] = spread(received, shape.own * SENT_ROWS, number, half)
     deepest = SENT[0]
     last = lax.axis_size("along") - 1
 
-    def place_piece(wide, narrow, below):
+    def work(below):
         keep = (last - along if below else along) > 0
         for start in (0, deepest - TILE) if below else (-deepest, -TILE):
             for c in range(shape.chunks):
-                source, skip = (wide, c * SENT_ROWS) if c < shape.own else (narrow, 0)
+                source, skip = (received, c * SENT_ROWS) if c < shape.own else (narrow, 0)
                 values = []
                 for k in range(FIELDS):
                     at = skip + OFFSETS[k] + start + (0 if below else SENT[k])
                     values.append(jnp.where(keep, source[pl.ds(at, TILE), :], 0.0))
                 place(refs, head, c, shape.first + start + (shape.rows if below else 0), values)
 
+        def rows(halo):
+            return [
+                (shape.first + shape.rows + halo - 2 * TILE if below else shape.first - halo, 2)
+            ]
+
+        sweep(rows(11), functools.partial(diagonal_rows, shape, static, thick))
+        spans = [rows(halo) for halo in (11, 10, 9, 8)]
+        spans += [[(shape.first + shape.rows - TILE if below else shape.first, 1)]]
+        sums = [partial[number] for number in range(2 * ITERS)]
+        sums = project(shape, vel, potential, static, moved, krylov, spans, sums)
+        if from_chip:
+            put_moments(out, sums)
+        else:
+            for number, value in enumerate(sums):
+                out[number] = value
+
     core = lax.rem(along, 2)
     for which in range(2):
 
         @pl.when(core == which)
         def _(which=which):
-            place_piece(out_chip, out_corner, which == 1)
-            place_piece(in_chip, in_corner, which == 0)
-
-    def both(halo):
-        return [(shape.first - halo, 2), (shape.first + shape.rows + halo - 2 * TILE, 2)]
-
-    sweep(both(11), functools.partial(diagonal_rows, shape, static, thick))
-    spans = [both(halo) for halo in (11, 10, 9, 8)]
-    spans += [[(shape.first, 1), (shape.first + shape.rows - TILE, 1)]]
-    sums = [partial[number] for number in range(2 * ITERS)]
-    put_moments(moments, project(shape, vel, potential, static, moved, krylov, spans, sums))
+            work((which == 1) == from_chip)
 
 
 def coefficients(shares):
@@ -763,16 +768,26 @@
         cost(2 * 10**6),
     )
     state = [fields(count) for count in (4, 5, 1, 6, 4, 1, 1)]
-    partial = vmem((2 * ITERS, TILE, LANES), f32)
+    partials = vmem((2 * ITERS, TILE, LANES), f32)
     *inner, partial = call(
-        inner_kernel, shape, [vmem] * 3, state + [partial], [],
+        inner_kernel, shape, [vmem] * 3, state + [partials], [],
         held(own, side, head),
         cost(10**7),
     )
+    aliases = {3 + number: number for number in range(7)}
+    near_kernel, next_kernel = (
+        functools.partial(lambda chip, shape, *refs: halo_kernel(shape, chip, *refs), chip)
+        for chip in (False, True)
+    )
+    *inner, partial = call(
+        near_kernel, shape, [vmem] * 10, state + [partials], [corner],
+        held(from_in, head, partial, *inner),
+        cost(5 * 10**6), aliases,
+    )
     moved, static, level, krylov, _, _, _, moments = call(
-        outer_kernel, shape, [vmem] * 11, state + [sums], [corner, corner],
-        held(from_out, from_in, head, partial, *inner),
-        cost(10**7), {4 + number: number for number in range(7)},
+        next_kernel, shape, [vmem] * 10, state + [sums], [corner],
+        held(from_out, head, partial, *inner),
+        cost(5 * 10**6), aliases,
     )
     moved, level, krylov, moments = call(
         second_kernel, shape, [vmem] * 5,

time: 66.8 us -> 66.3 us (level)
  starting transfers between devices: 7.94 us -> 6.19 us
  blocking collectives: 34.1 us -> 35.5 us
    all_to_all x2, blocking collectives: 34.1 us -> 35.5 us  [shared(): return lax.all_to_all(moments, ('along', 'cross'), 0, 0, tiled=True)]
    ppermute x1, starting transfers between devices: 2.45 us -> 1.36 us  [shards(): lax.ppermute(out_chip, ('along', 'cross'), trades(next_chip + ends))]
    pallas_call x8 -> x9, Pallas kernels: 22.9 us -> 23 us  [call(): pl.pallas_call(functools.partial(kernel, shape), out_shape=outs, in_specs...]
  transfers between devices with their start and end apart: 3 -> 3, of which waited for: 1 -> 1; matrix products, arithmetic and copies ran while one was open for 0% -> 0% of each run, Pallas kernels for 10% -> 14%
where the time goes in v10:
time: 66.3 us; the launch traced here: 66 us
  blocking collectives  35.5 us (54%)
  Pallas kernels  23 us (35%)
  starting transfers between devices  6.19 us (9%)
  between operations  0.72 us (1%)
  waiting for transfers between devices  0.69 us (1%)
    all_to_all x2, blocking collectives, shared(): return lax.all_to_all(moments, ('along', 'cross'), 0, 0, tiled=True)  35.5 us
    pallas_call x9, Pallas kernels, call(): pl.pallas_call(functools.partial(kernel, shape), out_shape=outs, in_specs...  23 us
    ppermute x1, starting transfers between devices, shards(): far = lax.ppermute(side, 'cross', [(0, 1), (1, 0)])  3.65 us
    ppermute x1, starting transfers between devices, shards(): lax.ppermute(out_chip, ('along', 'cross'), trades(next_chip + ends))  1.36 us
  transfers between devices with their start and end apart: 3, of which 1 were waited for; matrix products, arithmetic and copies ran while one was open for 0% of the time, Pallas kernels for 14%

profile of v10, /device:TPU:1, one launch (start us, length us, event | category | flops | bytes accessed | tf_op | source)
XLA Modules:
  0.0 66.0 jit_solution(748846882855464931)
XLA Ops:
  0.6 0.0 copy-start.1
  0.6 0.0 copy-start
  0.7 1.1 %shard_map.94 = f32[32,128]{1,0:T(8,128)S(1)} custom-call(f32[4,32,1536]{2,1,0:T(8,128)} %vel_in.3, f32[32,1536]{1,0:T(8,128)} %surface_in.3, s32[32,1536]{1,0:T(8,128)} %wet_in.3, s32[32,1536]{1,0:T(8,128)} %bathy_in.3, f32[16]{0:T(128)} %table_in.3), custom_call_target="tpu_custom_call" | custom-call | flops 100000 | bytes 100000 | tf_op jit(solution)/shard_map/pallas_call | solution.py:697
  1.7 3.7 %collective-permute-start = (f32[32,128]{1,0:T(8,128)S(1)}, f32[32,128]{1,0:T(8,128)S(1)}, u32[]{:S(2)}, u32[]{:S(2)}) collective-permute-start(f32[32,128]{1,0:T(8,128)S(1)} %shard_map.94), channel_id=1, source_target_pairs={{0,1},{1,0},{2,3},{3,2},{4,5},{5,4},{6,7},{7,6},{8,9},{9,8},{10,11... | collective-permute-start | bytes 49160 | tf_op jit(solution)/shard_map/ppermute | solution.py:745
  5.4 2.0 %shard_map.95 = (f32[7,12,32,128]{3,2,1,0:T(8,128)S(1)}, f32[1072,128]{1,0:T(8,128)S(1)}, f32[1072,128]{1,0:T(8,128)S(1)}) custom-call(f32[4,32,1536]{2,1,0:T(8,128)} %vel_in.3, f32[32,1536]{1,0:T(8,128)} %surface_in.3, s32[32,1536]{1,0:T(8,128)} %wet_in.3, s32[32,1536]{1,0:T(8,128)} %bathy_in.3, f32[16]{0:T(128)} %table_in.3), custom_call_target="tpu_custom_call" | custom-call | flops 4000000 | bytes 4000000 | tf_op jit(solution)/shard_map/pallas_call | solution.py:697
  7.3 0.0 collective-permute-done.far
  7.3 0.2 shard_map.96
  7.5 1.2 %collective-permute-start.2 = (f32[1072,128]{1,0:T(8,128)S(1)}, f32[1072,128]{1,0:T(8,128)S(1)}, u32[]{:S(2)}, u32[]{:S(2)}) collective-permute-start(f32[1072,128]{1,0:T(8,128)S(1)} %get-tuple-element.38), channel_id=1, source_target_pairs={{0,2},{4,6},{8,10},{12,14},{16,18},{20,22},{24,26},{28,30},{32,34}... | collective-permute-start | bytes 1646600 | tf_op jit(solution)/shard_map/ppermute | solution.py:763
  8.7 1.4 %collective-permute-start.1 = (f32[1072,128]{1,0:T(8,128)S(1)}, f32[1072,128]{1,0:T(8,128)S(1)}, u32[]{:S(2)}, u32[]{:S(2)}) collective-permute-start(f32[1072,128]{1,0:T(8,128)S(1)} %get-tuple-element.36), channel_id=1, source_target_pairs={{2,4},{3,5},{6,8},{7,9},{10,12},{11,13},{14,16},{15,17},{18,20},{1... | collective-permute-start | bytes 1646600 | tf_op jit(solution)/shard_map/ppermute | solution.py:762
  10.1 0.0 copy-done.1
  10.1 0.0 copy-done
  10.1 1.0 %shard_map.97.head.refs_1_ = f32[1,13,80,128]{3,2,1,0:T(8,128)S(1)} custom-call(s32[4,8]{1,0:T(4,128)S(1)} %bitcast.1, f32[8]{0:T(128)S(1)} %copy-done.1, f32[7,32,128]{2,1,0:T(8,128)S(1)} %get-tuple-element.37.side), custom_call_target="tpu_custom_call" | custom-call | flops 2000000 | bytes 2000000 | tf_op jit(solution)/shard_map/pallas_call | solution.py:697
  11.1 3.7 %shard_map.98 = (f32[4,13,80,128]{3,2,1,0:T(8,128)S(1)}, f32[5,13,80,128]{3,2,1,0:T(8,128)S(1)}, f32[1,13,80,128]{3,2,1,0:T(8,128)S(1)}, f32[6,13,80,128]{3,2,1,...) custom-call(f32[7,12,32,128]{3,2,1,0:T(8,128)S(1)} %get-tuple-elemen, ...), custom_call_target="tpu_custom_call" | custom-call | flops 10000000 | bytes 10000000 | tf_op jit(solution)/shard_map/pallas_call | solution.py:697
  14.8 0.0 collective-permute-done.2.refs_0_
  14.8 2.4 %shard_map.99 = (f32[4,13,80,128]{3,2,1,0:T(8,128)S(1)}, f32[5,13,80,128]{3,2,1,0:T(8,128)S(1)}, f32[1,13,80,128]{3,2,1,0:T(8,128)S(1)}, f32[6,13,80,128]{3,2,1,...) custom-call(f32[1072,128]{1,0:T(8,128)S(1)} %collective-permute-done, ...), custom_call_target="tpu_custom_call", output_to_operand_aliasing={{0}: (3, {}), {1}: (4, {}), {2}: (5, {}), {3}: (6, {}), {4}... | custom-call | flops 5000000 | bytes 5000000 | tf_op jit(solution)/shard_map/pallas_call | solution.py:697
  17.2 0.7 %collective-permute-done.1.refs_0_ = f32[1072,128]{1,0:T(8,128)S(1)} collective-permute-done((f32[1072,128]{1,0:T(8,128)S(1)}, f32[1072,128]{1,0:T(8,128)S(1)}, u32[]{:S(2)}, u32[]{:S(2)}) %collective-permute-start.1) | collective-permute-done | bytes 548896 | tf_op jit(solution)/shard_map/ppermute | solution.py:762
  17.9 2.6 %shard_map.100 = (f32[4,13,80,128]{3,2,1,0:T(8,128)S(1)}, f32[5,13,80,128]{3,2,1,0:T(8,128)S(1)}, f32[1,13,80,128]{3,2,1,0:T(8,128)S(1)}, f32[6,13,80,128]{3,2,1...) custom-call(f32[1072,128]{1,0:T(8,128)S(1)} %collective-permute-done, ...), custom_call_target="tpu_custom_call", output_to_operand_aliasing={{0}: (3, {}), {1}: (4, {}), {2}: (5, {}), {3}: (6, {}), {4}... | custom-call | flops 5000000 | bytes 5000000 | tf_op jit(solution)/shard_map/pallas_call | solution.py:697
  20.5 21.7 %all_to_all.10.shares = f32[128,1,8]{2,1,0:T(1,128)S(1)} all-to-all(f32[128,1,8]{2,1,0:T(1,128)S(1)} %get-tuple-element.56), channel_id=1, replica_groups=mesh['along'=64,'cross'=2] {'along','cross'}, dimensions={0} | all-to-all | bytes 8192 | tf_op jit(solution)/shard_map/all_to_all | solution.py:714
  42.1 7.7 %shard_map.101 = (f32[4,13,80,128]{3,2,1,0:T(8,128)S(1)}, f32[1,13,80,128]{3,2,1,0:T(8,128)S(1)}, f32[6,13,80,128]{3,2,1,0:T(8,128)S(1)}, f32[128,1,8]{2,1,0:T(1,128)S(1)}) custom-call(f32[128,1,8]{2,1,0:T(1,128)S(1)} %all_to_all.10.shares, f32[4,13,80,128]{3,2,1,0:T(8,128)S(1)} %get-tuple-element.57.moved_in, ...), custom_call_target="tpu_custom_call" | custom-call | tf_op jit(solution)/shard_map/pallas_call | solution.py:697
  49.9 13.8 %all_to_all.11.shares = f32[128,1,8]{2,1,0:T(1,128)S(1)} all-to-all(f32[128,1,8]{2,1,0:T(1,128)S(1)} %get-tuple-element.61), channel_id=1, replica_groups=mesh['along'=64,'cross'=2] {'along','cross'}, dimensions={0} | all-to-all | bytes 8192 | tf_op jit(solution)/shard_map/all_to_all | solution.py:714
  63.7 2.4 %shard_map.102 = (f32[4,32,1536]{2,1,0:T(8,128)}, f32[32,1536]{1,0:T(8,128)}, f32[2,32,1536]{2,1,0:T(8,128)}) custom-call(f32[128,1,8]{2,1,0:T(1,128)S(1)} %all_to_all.11.shares, f32[4,13,80,128]{3,2,1,0:T(8,128)S(1)} %get-tuple-element.62.moved, f32[5,13,80,128]{3,2,1,0:T(8,128)S(1)} %get-tuple-element.58.static, ...), custom_call_target="tpu_custom_call" | custom-call | tf_op jit(solution)/shard_map/pallas_call | solution.py:697
Async XLA Ops:
  0.6 9.5 %copy-start.1 = (f32[8]{0:T(128)S(1)}, f32[8]{0:T(128)}, u32[]{:S(2)}) copy-start(f32[8]{0:T(128)} %heads.1) | copy-start | bytes 100
  0.6 9.5 %copy-start = (s32[8,4]{0,1:T(4,128)S(1)}, s32[8,4]{0,1:T(4,128)}, u32[]{:S(2)}) copy-start(s32[8,4]{0,1:T(4,128)} %param.12) | copy-start | bytes 388
  1.7 5.6 %collective-permute-start = (f32[32,128]{1,0:T(8,128)S(1)}, f32[32,128]{1,0:T(8,128)S(1)}, u32[]{:S(2)}, u32[]{:S(2)}) collective-permute-start(f32[32,128]{1,0:T(8,128)S(1)} %shard_map.94), channel_id=1, source_target_pairs={{0,1},{1,0},{2,3},{3,2},{4,5},{5,4},{6,7},{7,6},{8,9},{9,8},{10,11... | collective-permute-start | bytes 49160 | tf_op jit(solution)/shard_map/ppermute | solution.py:745
  7.5 7.2 %collective-permute-start.2 = (f32[1072,128]{1,0:T(8,128)S(1)}, f32[1072,128]{1,0:T(8,128)S(1)}, u32[]{:S(2)}, u32[]{:S(2)}) collective-permute-start(f32[1072,128]{1,0:T(8,128)S(1)} %get-tuple-element.38), channel_id=1, source_target_pairs={{0,2},{4,6},{8,10},{12,14},{16,18},{20,22},{24,26},{28,30},{32,34}... | collective-permute-start | bytes 1646600 | tf_op jit(solution)/shard_map/ppermute | solution.py:763
  8.7 9.2 %collective-permute-start.1 = (f32[1072,128]{1,0:T(8,128)S(1)}, f32[1072,128]{1,0:T(8,128)S(1)}, u32[]{:S(2)}, u32[]{:S(2)}) collective-permute-start(f32[1072,128]{1,0:T(8,128)S(1)} %get-tuple-element.36), channel_id=1, source_target_pairs={{2,4},{3,5},{6,8},{7,9},{10,12},{11,13},{14,16},{15,17},{18,20},{1... | collective-permute-start | bytes 1646600 | tf_op jit(solution)/shard_map/ppermute | solution.py:762

commit v11 on v10

--- a/solution.py
+++ b/solution.py
@@ -69,7 +69,8 @@
         return jnp.where(self.lane >= amount, self.rolled(other, amount), self.rolled(chunk, amount))
 
     def done(self, chunk):
-        self.held.pop((chunk - 1) % self.chunks, None)
+        if chunk > 1:
+            self.held.pop(chunk - 1, None)
 
 
 def lanes_of():
@@ -98,7 +99,8 @@
     ref[index, chunk, pl.ds(row, TILE), :] = value
 
 
-CONDUCT, HALF_RATE, INVERSE, HEAD, DIAGONAL = range(5)
+CONDUCT, HALF_RATE, INVERSE, HEAD, DIAGONAL, PRIOR, NEXT = range(7)
+STATICS = 7
 
 
 def predict_rows(shape, vel, head_pressure, static, moved, row):
@@ -172,42 +174,45 @@
 
 def link_rows(shape, krylov, static, level, row, own_only):
     lane = lanes_of()
-
-    def plain(layer, c):
-        values = [load(krylov, 2 * level + layer, c, row + d) for d in (-1, 0, 1)]
-        return values[1], values[0] + values[2]
-
-    def weighted(layer, c):
-        values = [
-            load(static, CONDUCT, c, row + d) * load(krylov, 2 * level + layer, c, row + d)
-            for d in (-1, 0, 1)
-        ]
-        return values[1], values[0] + values[2]
-
-    sides = {}
-
-    def ring_of(kind, layer):
-        def make(c):
-            middle, sums = kind(layer, c)
-            sides[kind, layer, c] = sums
-            return middle + corner_weight * sums
-
-        return Ring(make, shape.chunks, lane)
-
-    rings = [(ring_of(plain, layer), ring_of(weighted, layer)) for layer in range(2)]
+    held = {}
+
+    def terms(layer, c):
+        if c not in held:
+            conduct = [load(static, CONDUCT, c, row + d) for d in (-1, 0, 1)]
+            prior, following = load(static, PRIOR, c, row), load(static, NEXT, c, row)
+            held[c] = []
+            for k in range(2):
+                y = [load(krylov, 2 * level + k, c, row + d) for d in (-1, 0, 1)]
+                sums = y[0] + y[2]
+                flows = conduct[0] * y[0] + conduct[2] * y[2]
+                middle = y[1] + corner_weight * sums
+                scaled = conduct[1] * y[1] + corner_weight * flows
+                held[c].append(
+                    (
+                        y[1],
+                        conduct[1] * sums + flows,
+                        following * middle + scaled,
+                        prior * middle + scaled,
+                    )
+                )
+        return held[c][layer]
+
+    rings = [
+        [Ring(lambda c, k=k, side=side: terms(k, c)[side], shape.chunks, lane) for side in (2, 3)]
+        for k in range(2)
+    ]
     for c in range(shape.own if own_only else shape.chunks):
-        conduct = load(static, CONDUCT, c, row)
         rate = load(static, HALF_RATE, c, row)
-        centre = [load(krylov, 2 * level + layer, c, row) for layer in range(2)]
         results = []
         for layer in range(2):
-            ring, scaled = rings[layer]
-            around = (ring.before(c, 1) + ring.after(c, 1)) + sides[plain, layer, c]
-            flows = (scaled.before(c, 1) + scaled.after(c, 1)) + sides[weighted, layer, c]
-            results.append(0.5 * (conduct * around + flows) + rate * centre[1 - layer])
+            left, right = rings[layer]
+            total = terms(layer, c)[1] + (left.before(c, 1) + right.after(c, 1))
+            results.append(0.5 * total + rate * terms(1 - layer, c)[0])
+        yield c, [terms(layer, c)[0] for layer in range(2)], results
+        for ring in rings[0] + rings[1]:
             ring.done(c)
-            scaled.done(c)
-        yield c, centre, results
+        if c > 1:
+            held.pop(c - 1)
 
 
 def krylov_rows(shape, krylov, static, level, row):
@@ -441,7 +446,11 @@
         return load(static, CONDUCT, c, row) + corner_weight * sums
 
     ring = Ring(make, shape.chunks, lanes_of())
+    plain = Ring(lambda c: load(static, CONDUCT, c, row), shape.chunks, lanes_of())
     for c in range(shape.chunks):
+        store(static, PRIOR, c, row, plain.before(c, 1))
+        store(static, NEXT, c, row, plain.after(c, 1))
+        plain.done(c)
         around = ring.before(c, 1) + ring.after(c, 1) + sides[c]
         depth = load(thick, 0, c, row)
         diagonal = (
@@ -767,7 +776,7 @@
         (hull_ranges.T, hull_pressure) + held(side),
         cost(2 * 10**6),
     )
-    state = [fields(count) for count in (4, 5, 1, 6, 4, 1, 1)]
+    state = [fields(count) for count in (4, STATICS, 1, 6, 4, 1, 1)]
     partials = vmem((2 * ITERS, TILE, LANES), f32)
     *inner, partial = call(
         inner_kernel, shape, [vmem] * 3, state + [partials], [],

time: 66.3 us -> 65.3 us (0.985)
  Pallas kernels: 23 us -> 21.3 us
    pallas_call x9, Pallas kernels: 23 us -> 21.3 us  [call(): pl.pallas_call(functools.partial(kernel, shape), out_shape=outs, in_specs...]
  transfers between devices with their start and end apart: 3 -> 3, of which waited for: 1 -> 1; matrix products, arithmetic and copies ran while one was open for 0% -> 0% of each run, Pallas kernels for 14% -> 13%
where the time goes in v11:
time: 65.3 us; the launch traced here: 65.1 us
  blocking collectives  35.5 us (54%)
  Pallas kernels  21.3 us (33%)
  starting transfers between devices  6.19 us (9%)
  waiting for transfers between devices  1.34 us (2%)
  between operations  0.72 us (1%)
    all_to_all x2, blocking collectives, shared(): return lax.all_to_all(moments, ('along', 'cross'), 0, 0, tiled=True)  35.5 us
    pallas_call x9, Pallas kernels, call(): pl.pallas_call(functools.partial(kernel, shape), out_shape=outs, in_specs...  21.3 us
    ppermute x1, starting transfers between devices, shards(): far = lax.ppermute(side, 'cross', [(0, 1), (1, 0)])  3.65 us
    ppermute x1, starting transfers between devices, shards(): lax.ppermute(out_chip, ('along', 'cross'), trades(next_chip + ends))  1.36 us
    ppermute x1, waiting for transfers between devices, shards(): lax.ppermute(out_chip, ('along', 'cross'), trades(next_chip + ends))  1.33 us
  transfers between devices with their start and end apart: 3, of which 1 were waited for; matrix products, arithmetic and copies ran while one was open for 0% of the time, Pallas kernels for 13%

profile of v11, /device:TPU:1, one launch (start us, length us, event | category | flops | bytes accessed | tf_op | source)
XLA Modules:
  0.0 65.1 jit_solution(17518053822836840241)
XLA Ops:
  0.6 0.0 copy-start.1
  0.6 0.0 copy-start
  0.7 1.1 %shard_map.94 = f32[32,128]{1,0:T(8,128)S(1)} custom-call(f32[4,32,1536]{2,1,0:T(8,128)} %vel_in.3, f32[32,1536]{1,0:T(8,128)} %surface_in.3, s32[32,1536]{1,0:T(8,128)} %wet_in.3, s32[32,1536]{1,0:T(8,128)} %bathy_in.3, f32[16]{0:T(128)} %table_in.3), custom_call_target="tpu_custom_call" | custom-call | flops 100000 | bytes 100000 | tf_op jit(solution)/shard_map/pallas_call | solution.py:706
  1.7 3.7 %collective-permute-start = (f32[32,128]{1,0:T(8,128)S(1)}, f32[32,128]{1,0:T(8,128)S(1)}, u32[]{:S(2)}, u32[]{:S(2)}) collective-permute-start(f32[32,128]{1,0:T(8,128)S(1)} %shard_map.94), channel_id=1, source_target_pairs={{0,1},{1,0},{2,3},{3,2},{4,5},{5,4},{6,7},{7,6},{8,9},{9,8},{10,11... | collective-permute-start | bytes 49160 | tf_op jit(solution)/shard_map/ppermute | solution.py:754
  5.4 2.0 %shard_map.95 = (f32[7,12,32,128]{3,2,1,0:T(8,128)S(1)}, f32[1072,128]{1,0:T(8,128)S(1)}, f32[1072,128]{1,0:T(8,128)S(1)}) custom-call(f32[4,32,1536]{2,1,0:T(8,128)} %vel_in.3, f32[32,1536]{1,0:T(8,128)} %surface_in.3, s32[32,1536]{1,0:T(8,128)} %wet_in.3, s32[32,1536]{1,0:T(8,128)} %bathy_in.3, f32[16]{0:T(128)} %table_in.3), custom_call_target="tpu_custom_call" | custom-call | flops 4000000 | bytes 4000000 | tf_op jit(solution)/shard_map/pallas_call | solution.py:706
  7.3 0.0 collective-permute-done.far
  7.3 0.2 shard_map.96
  7.5 1.2 %collective-permute-start.2 = (f32[1072,128]{1,0:T(8,128)S(1)}, f32[1072,128]{1,0:T(8,128)S(1)}, u32[]{:S(2)}, u32[]{:S(2)}) collective-permute-start(f32[1072,128]{1,0:T(8,128)S(1)} %get-tuple-element.38), channel_id=1, source_target_pairs={{0,2},{4,6},{8,10},{12,14},{16,18},{20,22},{24,26},{28,30},{32,34}... | collective-permute-start | bytes 1646600 | tf_op jit(solution)/shard_map/ppermute | solution.py:772
  8.7 1.4 %collective-permute-start.1 = (f32[1072,128]{1,0:T(8,128)S(1)}, f32[1072,128]{1,0:T(8,128)S(1)}, u32[]{:S(2)}, u32[]{:S(2)}) collective-permute-start(f32[1072,128]{1,0:T(8,128)S(1)} %get-tuple-element.36), channel_id=1, source_target_pairs={{2,4},{3,5},{6,8},{7,9},{10,12},{11,13},{14,16},{15,17},{18,20},{1... | collective-permute-start | bytes 1646600 | tf_op jit(solution)/shard_map/ppermute | solution.py:771
  10.1 0.0 copy-done.1
  10.1 0.0 copy-done
  10.1 1.0 %shard_map.97.head.refs_1_ = f32[1,13,80,128]{3,2,1,0:T(8,128)S(1)} custom-call(s32[4,8]{1,0:T(4,128)S(1)} %bitcast.1, f32[8]{0:T(128)S(1)} %copy-done.1, f32[7,32,128]{2,1,0:T(8,128)S(1)} %get-tuple-element.37.side), custom_call_target="tpu_custom_call" | custom-call | flops 2000000 | bytes 2000000 | tf_op jit(solution)/shard_map/pallas_call | solution.py:706
  11.1 3.3 %shard_map.98 = (f32[4,13,80,128]{3,2,1,0:T(8,128)S(1)}, f32[7,13,80,128]{3,2,1,0:T(8,128)S(1)}, f32[1,13,80,128]{3,2,1,0:T(8,128)S(1)}, f32[6,13,80,128]{3,2,1,...) custom-call(f32[7,12,32,128]{3,2,1,0:T(8,128)S(1)} %get-tuple-elemen, ...), custom_call_target="tpu_custom_call" | custom-call | flops 10000000 | bytes 10000000 | tf_op jit(solution)/shard_map/pallas_call | solution.py:706
  14.4 0.0 collective-permute-done.2.refs_0_
  14.4 2.2 %shard_map.99 = (f32[4,13,80,128]{3,2,1,0:T(8,128)S(1)}, f32[7,13,80,128]{3,2,1,0:T(8,128)S(1)}, f32[1,13,80,128]{3,2,1,0:T(8,128)S(1)}, f32[6,13,80,128]{3,2,1,...) custom-call(f32[1072,128]{1,0:T(8,128)S(1)} %collective-permute-done, ...), custom_call_target="tpu_custom_call", output_to_operand_aliasing={{0}: (3, {}), {1}: (4, {}), {2}: (5, {}), {3}: (6, {}), {4}... | custom-call | flops 5000000 | bytes 5000000 | tf_op jit(solution)/shard_map/pallas_call | solution.py:706
  16.6 1.3 %collective-permute-done.1.refs_0_ = f32[1072,128]{1,0:T(8,128)S(1)} collective-permute-done((f32[1072,128]{1,0:T(8,128)S(1)}, f32[1072,128]{1,0:T(8,128)S(1)}, u32[]{:S(2)}, u32[]{:S(2)}) %collective-permute-start.1) | collective-permute-done | bytes 548896 | tf_op jit(solution)/shard_map/ppermute | solution.py:771
  17.9 2.3 %shard_map.100 = (f32[4,13,80,128]{3,2,1,0:T(8,128)S(1)}, f32[7,13,80,128]{3,2,1,0:T(8,128)S(1)}, f32[1,13,80,128]{3,2,1,0:T(8,128)S(1)}, f32[6,13,80,128]{3,2,1...) custom-call(f32[1072,128]{1,0:T(8,128)S(1)} %collective-permute-done, ...), custom_call_target="tpu_custom_call", output_to_operand_aliasing={{0}: (3, {}), {1}: (4, {}), {2}: (5, {}), {3}: (6, {}), {4}... | custom-call | flops 5000000 | bytes 5000000 | tf_op jit(solution)/shard_map/pallas_call | solution.py:706
  20.2 21.7 %all_to_all.10.shares = f32[128,1,8]{2,1,0:T(1,128)S(1)} all-to-all(f32[128,1,8]{2,1,0:T(1,128)S(1)} %get-tuple-element.56), channel_id=1, replica_groups=mesh['along'=64,'cross'=2] {'along','cross'}, dimensions={0} | all-to-all | bytes 8192 | tf_op jit(solution)/shard_map/all_to_all | solution.py:723
  41.9 7.0 %shard_map.101 = (f32[4,13,80,128]{3,2,1,0:T(8,128)S(1)}, f32[1,13,80,128]{3,2,1,0:T(8,128)S(1)}, f32[6,13,80,128]{3,2,1,0:T(8,128)S(1)}, f32[128,1,8]{2,1,0:T(1,128)S(1)}) custom-call(f32[128,1,8]{2,1,0:T(1,128)S(1)} %all_to_all.10.shares, f32[4,13,80,128]{3,2,1,0:T(8,128)S(1)} %get-tuple-element.57.moved_in, ...), custom_call_target="tpu_custom_call" | custom-call | tf_op jit(solution)/shard_map/pallas_call | solution.py:706
  48.9 13.8 %all_to_all.11.shares = f32[128,1,8]{2,1,0:T(1,128)S(1)} all-to-all(f32[128,1,8]{2,1,0:T(1,128)S(1)} %get-tuple-element.61), channel_id=1, replica_groups=mesh['along'=64,'cross'=2] {'along','cross'}, dimensions={0} | all-to-all | bytes 8192 | tf_op jit(solution)/shard_map/all_to_all | solution.py:723
  62.7 2.4 %shard_map.102 = (f32[4,32,1536]{2,1,0:T(8,128)}, f32[32,1536]{1,0:T(8,128)}, f32[2,32,1536]{2,1,0:T(8,128)}) custom-call(f32[128,1,8]{2,1,0:T(1,128)S(1)} %all_to_all.11.shares, f32[4,13,80,128]{3,2,1,0:T(8,128)S(1)} %get-tuple-element.62.moved, f32[7,13,80,128]{3,2,1,0:T(8,128)S(1)} %get-tuple-element.58.static, ...), custom_call_target="tpu_custom_call" | custom-call | tf_op jit(solution)/shard_map/pallas_call | solution.py:706
Async XLA Ops:
  0.6 9.5 %copy-start.1 = (f32[8]{0:T(128)S(1)}, f32[8]{0:T(128)}, u32[]{:S(2)}) copy-start(f32[8]{0:T(128)} %heads.1) | copy-start | bytes 100
  0.6 9.5 %copy-start = (s32[8,4]{0,1:T(4,128)S(1)}, s32[8,4]{0,1:T(4,128)}, u32[]{:S(2)}) copy-start(s32[8,4]{0,1:T(4,128)} %param.12) | copy-start | bytes 388
  1.7 5.6 %collective-permute-start = (f32[32,128]{1,0:T(8,128)S(1)}, f32[32,128]{1,0:T(8,128)S(1)}, u32[]{:S(2)}, u32[]{:S(2)}) collective-permute-start(f32[32,128]{1,0:T(8,128)S(1)} %shard_map.94), channel_id=1, source_target_pairs={{0,1},{1,0},{2,3},{3,2},{4,5},{5,4},{6,7},{7,6},{8,9},{9,8},{10,11... | collective-permute-start | bytes 49160 | tf_op jit(solution)/shard_map/ppermute | solution.py:754
  7.5 6.8 %collective-permute-start.2 = (f32[1072,128]{1,0:T(8,128)S(1)}, f32[1072,128]{1,0:T(8,128)S(1)}, u32[]{:S(2)}, u32[]{:S(2)}) collective-permute-start(f32[1072,128]{1,0:T(8,128)S(1)} %get-tuple-element.38), channel_id=1, source_target_pairs={{0,2},{4,6},{8,10},{12,14},{16,18},{20,22},{24,26},{28,30},{32,34}... | collective-permute-start | bytes 1646600 | tf_op jit(solution)/shard_map/ppermute | solution.py:772
  8.7 9.2 %collective-permute-start.1 = (f32[1072,128]{1,0:T(8,128)S(1)}, f32[1072,128]{1,0:T(8,128)S(1)}, u32[]{:S(2)}, u32[]{:S(2)}) collective-permute-start(f32[1072,128]{1,0:T(8,128)S(1)} %get-tuple-element.36), channel_id=1, source_target_pairs={{2,4},{3,5},{6,8},{7,9},{10,12},{11,13},{14,16},{15,17},{18,20},{1... | collective-permute-start | bytes 1646600 | tf_op jit(solution)/shard_map/ppermute | solution.py:771

commit v12 on v11

--- a/solution.py
+++ b/solution.py
@@ -313,7 +313,7 @@
 
 def pack_kernel(
     shape, vel_in, surface_in, wet_in, bathy_in, table_in,
-    own, out_chip, in_chip,
+    own, out_chip, in_chip, in_rest,
     vel, surface, wet, bathy, table, arrived,
 ):
     fetch(
@@ -344,7 +344,9 @@
                 to = pl.ds(c * SENT_ROWS + OFFSETS[k] + part, TILE)
                 last = shape.rows - SENT[k]
                 out_chip[to, :] = own[k, c, pl.ds(part + core * last, TILE), :]
-                in_chip[to, :] = own[k, c, pl.ds(part + (1 - core) * last, TILE), :]
+                target = in_chip if c < shape.own // 2 else in_rest
+                to = pl.ds(c % (shape.own // 2) * SENT_ROWS + OFFSETS[k] + part, TILE)
+                target[to, :] = own[k, c, pl.ds(part + (1 - core) * last, TILE), :]
 
 
 def corner_kernel(shape, far, out_in, in_in, out_chip, in_chip, side):
@@ -354,7 +356,7 @@
         tile[...] = spread(far, 0, number, half)
     shift = jnp.where(half == 0, 0, EDGE)
     squeeze(out_chip, shape.own * SENT_ROWS, corner_tiles(shape, side, core), shift)
-    squeeze(in_chip, shape.own * SENT_ROWS, corner_tiles(shape, side, 1 - core), shift)
+    squeeze(in_chip, shape.own // 2 * SENT_ROWS, corner_tiles(shape, side, 1 - core), shift)
 
 
 def side_tiles(shape, edge):
@@ -485,16 +487,20 @@
         partial[number] = value
 
 
-def halo_kernel(shape, from_chip, received, head, partial, *refs):
-    refs = refs[7:]
+def halo_kernel(shape, from_chip, *refs):
+    parts = 1 if from_chip else 2
+    received = refs[:parts]
+    head, partial = refs[parts : parts + 2]
+    refs = refs[parts + 9 :]
     out, narrow = refs[7:]
     refs = refs[:7]
+    share = shape.own // parts
     moved, static, surface, krylov, vel, potential, thick = refs
     along = lax.axis_index("along")
     half = lax.axis_index("cross")
     for number, (k, part) in enumerate(corner_parts()):
         to = pl.ds(OFFSETS[k] + part, TILE)
-        narrow[to, :] = spread(received, shape.own * SENT_ROWS, number, half)
+        narrow[to, :] = spread(received[-1], share * SENT_ROWS, number, half)
     deepest = SENT[0]
     last = lax.axis_size("along") - 1
 
@@ -502,7 +508,9 @@
         keep = (last - along if below else along) > 0
         for start in (0, deepest - TILE) if below else (-deepest, -TILE):
             for c in range(shape.chunks):
-                source, skip = (received, c * SENT_ROWS) if c < shape.own else (narrow, 0)
+                source, skip = narrow, 0
+                if c < shape.own:
+                    source, skip = received[c // share], c % share * SENT_ROWS
                 values = []
                 for k in range(FIELDS):
                     at = skip + OFFSETS[k] + start + (0 if below else SENT[k])
@@ -752,16 +760,20 @@
         cost(10**5),
     )
     far = lax.ppermute(side, "cross", [(0, 1), (1, 0)])
-    own, out_chip, in_chip = call(
+    half_rows = shape.own // 2 * SENT_ROWS
+    first_half = vmem((half_rows, LANES), f32)
+    second_half = vmem((half_rows + CORNER_ROWS, LANES), f32)
+    own, out_chip, in_chip, in_rest = call(
         pack_kernel, shape, [pl.ANY] * 5,
-        [vmem((FIELDS, shape.own, shape.rows, LANES), f32), wide, wide],
+        [vmem((FIELDS, shape.own, shape.rows, LANES), f32), wide, first_half, second_half],
         [vmem(velocity.shape, f32), vmem(block, f32), vmem(block, i32), vmem(block, i32)]
         + table + arrived,
         inputs,
         cost(4 * 10**6),
     )
-    out_chip, in_chip, side = call(
-        corner_kernel, shape, [vmem] * 3, [wide, wide, full], [], held(far, out_chip, in_chip),
+    out_chip, in_rest, side = call(
+        corner_kernel, shape, [vmem] * 3, [wide, second_half, full], [],
+        held(far, out_chip, in_rest),
         cost(10**5), {1: 0, 2: 1},
     )
     firsts = [i for i in range(1, size, 2)]
@@ -769,7 +781,8 @@
     ends = [(0, 1), (2 * size - 2, 2 * size - 1)]
     next_chip = [(2 * i + j, 2 * i + 2 + j) for i in firsts[:-1] for j in range(2)]
     from_out = lax.ppermute(out_chip, ("along", "cross"), trades(next_chip + ends))
-    from_in = lax.ppermute(in_chip, "along", trades([(i - 1, i) for i in firsts]))
+    same_chip = trades([(i - 1, i) for i in firsts])
+    from_in = [lax.ppermute(piece, "along", same_chip) for piece in (in_chip, in_rest)]
     (head,) = call(
         head_kernel, shape, [smem] * 2 + [vmem], [fields(1)],
         [vmem((SHIPS, shape.chunks, TILE, LANES), f32)],
@@ -783,20 +796,19 @@
         held(own, side, head),
         cost(10**7),
     )
-    aliases = {3 + number: number for number in range(7)}
     near_kernel, next_kernel = (
         functools.partial(lambda chip, shape, *refs: halo_kernel(shape, chip, *refs), chip)
         for chip in (False, True)
     )
     *inner, partial = call(
-        near_kernel, shape, [vmem] * 10, state + [partials], [corner],
-        held(from_in, head, partial, *inner),
-        cost(5 * 10**6), aliases,
+        near_kernel, shape, [vmem] * 11, state + [partials], [corner],
+        held(*from_in, head, partial, *inner),
+        cost(5 * 10**6), {4 + number: number for number in range(7)},
     )
     moved, static, level, krylov, _, _, _, moments = call(
         next_kernel, shape, [vmem] * 10, state + [sums], [corner],
         held(from_out, head, partial, *inner),
-        cost(5 * 10**6), aliases,
+        cost(5 * 10**6), {3 + number: number for number in range(7)},
     )
     moved, level, krylov, moments = call(
         second_kernel, shape, [vmem] * 5,

time: 65.3 us -> 63.5 us (0.972)
  blocking collectives: 35.5 us -> 33.2 us
  starting transfers between devices: 6.19 us -> 7.95 us
  waiting for transfers between devices: 1.34 us -> 0.01 us
    all_to_all x2, blocking collectives: 35.5 us -> 33.2 us  [shared(): return lax.all_to_all(moments, ('along', 'cross'), 0, 0, tiled=True)]
    ppermute x1, waiting for transfers between devices: 1.33 us -> 0.01 us  [shards(): lax.ppermute(out_chip, ('along', 'cross'), trades(next_chip + ends))]
    ppermute x1, starting transfers between devices: 1.36 us -> 2.45 us  [shards(): lax.ppermute(out_chip, ('along', 'cross'), trades(next_chip + ends))]
    ppermute x1 -> x2, starting transfers between devices: 1.18 us -> 1.84 us  [shards(): lax.ppermute(piece, 'along', same_chip)]
  transfers between devices with their start and end apart: 3 -> 4, of which waited for: 1 -> 0; matrix products, arithmetic and copies ran while one was open for 0% -> 0% of each run, Pallas kernels for 13% -> 13%
where the time goes in v12:
time: 63.5 us; the launch traced here: 63.3 us
  blocking collectives  33.2 us (52%)
  Pallas kernels  21.4 us (34%)
  starting transfers between devices  7.95 us (13%)
  between operations  0.74 us (1%)
    all_to_all x2, blocking collectives, shared(): return lax.all_to_all(moments, ('along', 'cross'), 0, 0, tiled=True)  33.2 us
    pallas_call x9, Pallas kernels, call(): pl.pallas_call(functools.partial(kernel, shape), out_shape=outs, in_specs...  21.4 us
    ppermute x1, starting transfers between devices, shards(): far = lax.ppermute(side, 'cross', [(0, 1), (1, 0)])  3.65 us
    ppermute x1, starting transfers between devices, shards(): lax.ppermute(out_chip, ('along', 'cross'), trades(next_chip + ends))  2.45 us
    ppermute x2, starting transfers between devices, shards(): lax.ppermute(piece, 'along', same_chip)  1.84 us
  transfers between devices with their start and end apart: 4, of which 0 were waited for; matrix products, arithmetic and copies ran while one was open for 0% of the time, Pallas kernels for 13%

profile of v12, /device:TPU:1, one launch (start us, length us, event | category | flops | bytes accessed | tf_op | source)
XLA Modules:
  0.0 63.3 jit_solution(4205284768278337411)
XLA Ops:
  0.6 0.0 copy-start.1
  0.6 0.0 copy-start
  0.7 1.1 %shard_map.94 = f32[32,128]{1,0:T(8,128)S(1)} custom-call(f32[4,32,1536]{2,1,0:T(8,128)} %vel_in.3, f32[32,1536]{1,0:T(8,128)} %surface_in.3, s32[32,1536]{1,0:T(8,128)} %wet_in.3, s32[32,1536]{1,0:T(8,128)} %bathy_in.3, f32[16]{0:T(128)} %table_in.3), custom_call_target="tpu_custom_call" | custom-call | flops 100000 | bytes 100000 | tf_op jit(solution)/shard_map/pallas_call | solution.py:714
  1.7 3.7 %collective-permute-start = (f32[32,128]{1,0:T(8,128)S(1)}, f32[32,128]{1,0:T(8,128)S(1)}, u32[]{:S(2)}, u32[]{:S(2)}) collective-permute-start(f32[32,128]{1,0:T(8,128)S(1)} %shard_map.94), channel_id=1, source_target_pairs={{0,1},{1,0},{2,3},{3,2},{4,5},{5,4},{6,7},{7,6},{8,9},{9,8},{10,11... | collective-permute-start | bytes 49160 | tf_op jit(solution)/shard_map/ppermute | solution.py:762
  5.4 2.0 %shard_map.95 = (f32[7,12,32,128]{3,2,1,0:T(8,128)S(1)}, f32[1072,128]{1,0:T(8,128)S(1)}, f32[528,128]{1,0:T(8,128)S(1)}, f32[544,128]{1,0:T(8,128)S(1)}) custom-call(f32[4,32,1536]{2,1,0:T(8,128)} %vel_in.3, f32[32,1536]{1,0:T(8,128)} %surface_in.3, s32[32,1536]{1,0:T(8,128)} %wet_in.3, s32[32,1536]{1,0:T(8,128)} %bathy_in.3, f32[16]{0:T(128)} %table_in.3), custom_call_target="tpu_custom_call" | custom-call | flops 4000000 | bytes 4000000 | tf_op jit(solution)/shard_map/pallas_call | solution.py:714
  7.3 0.0 collective-permute-done.far
  7.3 0.2 shard_map.96
  7.5 2.4 %collective-permute-start.1 = (f32[1072,128]{1,0:T(8,128)S(1)}, f32[1072,128]{1,0:T(8,128)S(1)}, u32[]{:S(2)}, u32[]{:S(2)}) collective-permute-start(f32[1072,128]{1,0:T(8,128)S(1)} %get-tuple-element.37), channel_id=1, source_target_pairs={{2,4},{3,5},{6,8},{7,9},{10,12},{11,13},{14,16},{15,17},{18,20},{1... | collective-permute-start | bytes 1646600 | tf_op jit(solution)/shard_map/ppermute | solution.py:783
  10.0 1.8 %collective-permute-start.3 = (f32[544,128]{1,0:T(8,128)S(1)}, f32[544,128]{1,0:T(8,128)S(1)}, u32[]{:S(2)}, u32[]{:S(2)}) collective-permute-start(f32[544,128]{1,0:T(8,128)S(1)} %get-tuple-element.40), channel_id=1, source_target_pairs={{0,2},{4,6},{8,10},{12,14},{16,18},{20,22},{24,26},{28,30},{32,34}... | collective-permute-start | bytes 835592 | tf_op jit(solution)/shard_map/ppermute | solution.py:785
  11.8 0.0 collective-permute-start.2
  11.8 0.0 copy-done.1
  11.8 0.0 copy-done
  11.8 1.0 %shard_map.97.head.refs_2_.refs_1_ = f32[1,13,80,128]{3,2,1,0:T(8,128)S(1)} custom-call(s32[4,8]{1,0:T(4,128)S(1)} %bitcast.1, f32[8]{0:T(128)S(1)} %copy-done.1, f32[7,32,128]{2,1,0:T(8,128)S(1)} %get-tuple-element.38.side), custom_call_target="tpu_custom_call" | custom-call | flops 2000000 | bytes 2000000 | tf_op jit(solution)/shard_map/pallas_call | solution.py:714
  12.8 3.3 %shard_map.98 = (f32[4,13,80,128]{3,2,1,0:T(8,128)S(1)}, f32[7,13,80,128]{3,2,1,0:T(8,128)S(1)}, f32[1,13,80,128]{3,2,1,0:T(8,128)S(1)}, f32[6,13,80,128]{3,2,1,...) custom-call(f32[7,12,32,128]{3,2,1,0:T(8,128)S(1)} %get-tuple-elemen, ...), custom_call_target="tpu_custom_call" | custom-call | flops 10000000 | bytes 10000000 | tf_op jit(solution)/shard_map/pallas_call | solution.py:714
  16.1 0.0 collective-permute-done.2.refs_0_
  16.1 0.0 collective-permute-done.3.refs_1_
  16.1 2.2 %shard_map.99 = (f32[4,13,80,128]{3,2,1,0:T(8,128)S(1)}, f32[7,13,80,128]{3,2,1,0:T(8,128)S(1)}, f32[1,13,80,128]{3,2,1,0:T(8,128)S(1)}, f32[6,13,80,128]{3,2,1,...) custom-call(f32[528,128]{1,0:T(8,128)S(1)} %collective-permute-done., ...), custom_call_target="tpu_custom_call", output_to_operand_aliasing={{0}: (4, {}), {1}: (5, {}), {2}: (6, {}), {3}: (7, {}), {4}... | custom-call | flops 5000000 | bytes 5000000 | tf_op jit(solution)/shard_map/pallas_call | solution.py:714
  18.3 0.0 collective-permute-done.1.refs_0_
  18.3 2.3 %shard_map.100 = (f32[4,13,80,128]{3,2,1,0:T(8,128)S(1)}, f32[7,13,80,128]{3,2,1,0:T(8,128)S(1)}, f32[1,13,80,128]{3,2,1,0:T(8,128)S(1)}, f32[6,13,80,128]{3,2,1...) custom-call(f32[1072,128]{1,0:T(8,128)S(1)} %collective-permute-done, ...), custom_call_target="tpu_custom_call", output_to_operand_aliasing={{0}: (3, {}), {1}: (4, {}), {2}: (5, {}), {3}: (6, {}), {4}... | custom-call | flops 5000000 | bytes 5000000 | tf_op jit(solution)/shard_map/pallas_call | solution.py:714
  20.7 19.4 %all_to_all.10.shares = f32[128,1,8]{2,1,0:T(1,128)S(1)} all-to-all(f32[128,1,8]{2,1,0:T(1,128)S(1)} %get-tuple-element.58), channel_id=1, replica_groups=mesh['along'=64,'cross'=2] {'along','cross'}, dimensions={0} | all-to-all | bytes 8192 | tf_op jit(solution)/shard_map/all_to_all | solution.py:731
  40.1 7.0 %shard_map.101 = (f32[4,13,80,128]{3,2,1,0:T(8,128)S(1)}, f32[1,13,80,128]{3,2,1,0:T(8,128)S(1)}, f32[6,13,80,128]{3,2,1,0:T(8,128)S(1)}, f32[128,1,8]{2,1,0:T(1,128)S(1)}) custom-call(f32[128,1,8]{2,1,0:T(1,128)S(1)} %all_to_all.10.shares, f32[4,13,80,128]{3,2,1,0:T(8,128)S(1)} %get-tuple-element.59.moved_in, ...), custom_call_target="tpu_custom_call" | custom-call | tf_op jit(solution)/shard_map/pallas_call | solution.py:714
  47.1 13.8 %all_to_all.11.shares = f32[128,1,8]{2,1,0:T(1,128)S(1)} all-to-all(f32[128,1,8]{2,1,0:T(1,128)S(1)} %get-tuple-element.63), channel_id=1, replica_groups=mesh['along'=64,'cross'=2] {'along','cross'}, dimensions={0} | all-to-all | bytes 8192 | tf_op jit(solution)/shard_map/all_to_all | solution.py:731
  60.9 2.4 %shard_map.102 = (f32[4,32,1536]{2,1,0:T(8,128)}, f32[32,1536]{1,0:T(8,128)}, f32[2,32,1536]{2,1,0:T(8,128)}) custom-call(f32[128,1,8]{2,1,0:T(1,128)S(1)} %all_to_all.11.shares, f32[4,13,80,128]{3,2,1,0:T(8,128)S(1)} %get-tuple-element.64.moved, f32[7,13,80,128]{3,2,1,0:T(8,128)S(1)} %get-tuple-element.60.static, ...), custom_call_target="tpu_custom_call" | custom-call | tf_op jit(solution)/shard_map/pallas_call | solution.py:714
Async XLA Ops:
  0.6 11.2 %copy-start.1 = (f32[8]{0:T(128)S(1)}, f32[8]{0:T(128)}, u32[]{:S(2)}) copy-start(f32[8]{0:T(128)} %heads.1) | copy-start | bytes 100
  0.6 11.2 %copy-start = (s32[8,4]{0,1:T(4,128)S(1)}, s32[8,4]{0,1:T(4,128)}, u32[]{:S(2)}) copy-start(s32[8,4]{0,1:T(4,128)} %param.12) | copy-start | bytes 388
  1.7 5.6 %collective-permute-start = (f32[32,128]{1,0:T(8,128)S(1)}, f32[32,128]{1,0:T(8,128)S(1)}, u32[]{:S(2)}, u32[]{:S(2)}) collective-permute-start(f32[32,128]{1,0:T(8,128)S(1)} %shard_map.94), channel_id=1, source_target_pairs={{0,1},{1,0},{2,3},{3,2},{4,5},{5,4},{6,7},{7,6},{8,9},{9,8},{10,11... | collective-permute-start | bytes 49160 | tf_op jit(solution)/shard_map/ppermute | solution.py:762
  7.5 10.8 %collective-permute-start.1 = (f32[1072,128]{1,0:T(8,128)S(1)}, f32[1072,128]{1,0:T(8,128)S(1)}, u32[]{:S(2)}, u32[]{:S(2)}) collective-permute-start(f32[1072,128]{1,0:T(8,128)S(1)} %get-tuple-element.37), channel_id=1, source_target_pairs={{2,4},{3,5},{6,8},{7,9},{10,12},{11,13},{14,16},{15,17},{18,20},{1... | collective-permute-start | bytes 1646600 | tf_op jit(solution)/shard_map/ppermute | solution.py:783
  10.0 6.1 %collective-permute-start.3 = (f32[544,128]{1,0:T(8,128)S(1)}, f32[544,128]{1,0:T(8,128)S(1)}, u32[]{:S(2)}, u32[]{:S(2)}) collective-permute-start(f32[544,128]{1,0:T(8,128)S(1)} %get-tuple-element.40), channel_id=1, source_target_pairs={{0,2},{4,6},{8,10},{12,14},{16,18},{20,22},{24,26},{28,30},{32,34}... | collective-permute-start | bytes 835592 | tf_op jit(solution)/shard_map/ppermute | solution.py:785
  11.8 4.3 %collective-permute-start.2 = (f32[528,128]{1,0:T(8,128)S(1)}, f32[528,128]{1,0:T(8,128)S(1)}, u32[]{:S(2)}, u32[]{:S(2)}) collective-permute-start(f32[528,128]{1,0:T(8,128)S(1)} %get-tuple-element.39), channel_id=1, source_target_pairs={{0,2},{4,6},{8,10},{12,14},{16,18},{20,22},{24,26},{28,30},{32,34}... | collective-permute-start | bytes 811016 | tf_op jit(solution)/shard_map/ppermute | solution.py:785

commit v13 on v12

--- a/solution.py
+++ b/solution.py
@@ -77,17 +77,28 @@
     return lax.broadcasted_iota(jnp.int32, (TILE, LANES), 1)
 
 
+UNROLL = 4
+
+
 def sweep(spans, body, carry=None):
     for first, tiles in spans:
 
-        def turn(number, carry, first=first):
-            row = first + number * TILE
-            if carry is None:
-                body(row)
-                return None
-            return body(row, carry)
-
-        carry = lax.fori_loop(0, tiles, turn, carry)
+        def turn(number, carry, first=first, count=UNROLL, skipped=0):
+            for tile in range(count):
+                row = first + number * (UNROLL * TILE) + (skipped + tile) * TILE
+                if carry is None:
+                    body(row)
+                else:
+                    carry = body(row, carry)
+            return carry
+
+        turns = tiles // UNROLL
+        if turns == 1:
+            carry = turn(0, carry)
+        elif turns:
+            carry = lax.fori_loop(0, turns, turn, carry)
+        if tiles % UNROLL:
+            carry = turn(0, carry, count=tiles % UNROLL, skipped=turns * UNROLL)
     return carry
 
 

time: 63.5 us -> 60.2 us (0.948)
  Pallas kernels: 21.4 us -> 16.7 us
  blocking collectives: 33.2 us -> 34.1 us
    pallas_call x9, Pallas kernels: 21.4 us -> 16.7 us  [call(): pl.pallas_call(functools.partial(kernel, shape), out_shape=outs, in_specs...]
    all_to_all x2, blocking collectives: 33.2 us -> 34.1 us  [shared(): return lax.all_to_all(moments, ('along', 'cross'), 0, 0, tiled=True)]
  transfers between devices with their start and end apart: 4 -> 4, of which waited for: 0 -> 1; matrix products, arithmetic and copies ran while one was open for 0% -> 0% of each run, Pallas kernels for 13% -> 12%
where the time goes in v13:
time: 60.2 us; the launch traced here: 60 us
  blocking collectives  34.1 us (57%)
  Pallas kernels  16.7 us (28%)
  starting transfers between devices  7.95 us (13%)
  between operations  0.73 us (1%)
    all_to_all x2, blocking collectives, shared(): return lax.all_to_all(moments, ('along', 'cross'), 0, 0, tiled=True)  34.1 us
    pallas_call x9, Pallas kernels, call(): pl.pallas_call(functools.partial(kernel, shape), out_shape=outs, in_specs...  16.7 us
    ppermute x1, starting transfers between devices, shards(): far = lax.ppermute(side, 'cross', [(0, 1), (1, 0)])  3.65 us
    ppermute x1, starting transfers between devices, shards(): lax.ppermute(out_chip, ('along', 'cross'), trades(next_chip + ends))  2.45 us
    ppermute x2, starting transfers between devices, shards(): lax.ppermute(piece, 'along', same_chip)  1.84 us
  transfers between devices with their start and end apart: 4, of which 1 were waited for; matrix products, arithmetic and copies ran while one was open for 0% of the time, Pallas kernels for 12%

profile of v13, /device:TPU:1, one launch (start us, length us, event | category | flops | bytes accessed | tf_op | source)
XLA Modules:
  0.0 60.0 jit_solution(4214503775510319222)
XLA Ops:
  0.6 0.0 copy-start.1
  0.6 0.0 copy-start
  0.7 1.1 %shard_map.94 = f32[32,128]{1,0:T(8,128)S(1)} custom-call(f32[4,32,1536]{2,1,0:T(8,128)} %vel_in.3, f32[32,1536]{1,0:T(8,128)} %surface_in.3, s32[32,1536]{1,0:T(8,128)} %wet_in.3, s32[32,1536]{1,0:T(8,128)} %bathy_in.3, f32[16]{0:T(128)} %table_in.3), custom_call_target="tpu_custom_call" | custom-call | flops 100000 | bytes 100000 | tf_op jit(solution)/shard_map/pallas_call | solution.py:725
  1.7 3.7 %collective-permute-start = (f32[32,128]{1,0:T(8,128)S(1)}, f32[32,128]{1,0:T(8,128)S(1)}, u32[]{:S(2)}, u32[]{:S(2)}) collective-permute-start(f32[32,128]{1,0:T(8,128)S(1)} %shard_map.94), channel_id=1, source_target_pairs={{0,1},{1,0},{2,3},{3,2},{4,5},{5,4},{6,7},{7,6},{8,9},{9,8},{10,11... | collective-permute-start | bytes 49160 | tf_op jit(solution)/shard_map/ppermute | solution.py:773
  5.4 2.0 %shard_map.95 = (f32[7,12,32,128]{3,2,1,0:T(8,128)S(1)}, f32[1072,128]{1,0:T(8,128)S(1)}, f32[528,128]{1,0:T(8,128)S(1)}, f32[544,128]{1,0:T(8,128)S(1)}) custom-call(f32[4,32,1536]{2,1,0:T(8,128)} %vel_in.3, f32[32,1536]{1,0:T(8,128)} %surface_in.3, s32[32,1536]{1,0:T(8,128)} %wet_in.3, s32[32,1536]{1,0:T(8,128)} %bathy_in.3, f32[16]{0:T(128)} %table_in.3), custom_call_target="tpu_custom_call" | custom-call | flops 4000000 | bytes 4000000 | tf_op jit(solution)/shard_map/pallas_call | solution.py:725
  7.3 0.0 collective-permute-done.far
  7.3 0.2 shard_map.96
  7.5 2.4 %collective-permute-start.1 = (f32[1072,128]{1,0:T(8,128)S(1)}, f32[1072,128]{1,0:T(8,128)S(1)}, u32[]{:S(2)}, u32[]{:S(2)}) collective-permute-start(f32[1072,128]{1,0:T(8,128)S(1)} %get-tuple-element.37), channel_id=1, source_target_pairs={{2,4},{3,5},{6,8},{7,9},{10,12},{11,13},{14,16},{15,17},{18,20},{1... | collective-permute-start | bytes 1646600 | tf_op jit(solution)/shard_map/ppermute | solution.py:794
  10.0 1.8 %collective-permute-start.3 = (f32[544,128]{1,0:T(8,128)S(1)}, f32[544,128]{1,0:T(8,128)S(1)}, u32[]{:S(2)}, u32[]{:S(2)}) collective-permute-start(f32[544,128]{1,0:T(8,128)S(1)} %get-tuple-element.40), channel_id=1, source_target_pairs={{0,2},{4,6},{8,10},{12,14},{16,18},{20,22},{24,26},{28,30},{32,34}... | collective-permute-start | bytes 835592 | tf_op jit(solution)/shard_map/ppermute | solution.py:796
  11.8 0.0 collective-permute-start.2
  11.8 0.0 copy-done.1
  11.8 0.0 copy-done
  11.8 0.9 %shard_map.97.head.refs_2_.refs_1_ = f32[1,13,80,128]{3,2,1,0:T(8,128)S(1)} custom-call(s32[4,8]{1,0:T(4,128)S(1)} %bitcast.1, f32[8]{0:T(128)S(1)} %copy-done.1, f32[7,32,128]{2,1,0:T(8,128)S(1)} %get-tuple-element.38.side), custom_call_target="tpu_custom_call" | custom-call | flops 2000000 | bytes 2000000 | tf_op jit(solution)/shard_map/pallas_call | solution.py:725
  12.8 2.3 %shard_map.98 = (f32[4,13,80,128]{3,2,1,0:T(8,128)S(1)}, f32[7,13,80,128]{3,2,1,0:T(8,128)S(1)}, f32[1,13,80,128]{3,2,1,0:T(8,128)S(1)}, f32[6,13,80,128]{3,2,1,...) custom-call(f32[7,12,32,128]{3,2,1,0:T(8,128)S(1)} %get-tuple-elemen, ...), custom_call_target="tpu_custom_call" | custom-call | flops 10000000 | bytes 10000000 | tf_op jit(solution)/shard_map/pallas_call | solution.py:725
  15.1 0.0 collective-permute-done.2.refs_0_
  15.1 0.0 collective-permute-done.3.refs_1_
  15.1 1.8 %shard_map.99 = (f32[4,13,80,128]{3,2,1,0:T(8,128)S(1)}, f32[7,13,80,128]{3,2,1,0:T(8,128)S(1)}, f32[1,13,80,128]{3,2,1,0:T(8,128)S(1)}, f32[6,13,80,128]{3,2,1,...) custom-call(f32[528,128]{1,0:T(8,128)S(1)} %collective-permute-done., ...), custom_call_target="tpu_custom_call", output_to_operand_aliasing={{0}: (4, {}), {1}: (5, {}), {2}: (6, {}), {3}: (7, {}), {4}... | custom-call | flops 5000000 | bytes 5000000 | tf_op jit(solution)/shard_map/pallas_call | solution.py:725
  16.9 0.5 collective-permute-done.1.refs_0_
  17.4 1.7 %shard_map.100 = (f32[4,13,80,128]{3,2,1,0:T(8,128)S(1)}, f32[7,13,80,128]{3,2,1,0:T(8,128)S(1)}, f32[1,13,80,128]{3,2,1,0:T(8,128)S(1)}, f32[6,13,80,128]{3,2,1...) custom-call(f32[1072,128]{1,0:T(8,128)S(1)} %collective-permute-done, ...), custom_call_target="tpu_custom_call", output_to_operand_aliasing={{0}: (3, {}), {1}: (4, {}), {2}: (5, {}), {3}: (6, {}), {4}... | custom-call | flops 5000000 | bytes 5000000 | tf_op jit(solution)/shard_map/pallas_call | solution.py:725
  19.1 20.3 %all_to_all.10.shares = f32[128,1,8]{2,1,0:T(1,128)S(1)} all-to-all(f32[128,1,8]{2,1,0:T(1,128)S(1)} %get-tuple-element.58), channel_id=1, replica_groups=mesh['along'=64,'cross'=2] {'along','cross'}, dimensions={0} | all-to-all | bytes 8192 | tf_op jit(solution)/shard_map/all_to_all | solution.py:742
  39.5 5.0 %shard_map.101 = (f32[4,13,80,128]{3,2,1,0:T(8,128)S(1)}, f32[1,13,80,128]{3,2,1,0:T(8,128)S(1)}, f32[6,13,80,128]{3,2,1,0:T(8,128)S(1)}, f32[128,1,8]{2,1,0:T(1,128)S(1)}) custom-call(f32[128,1,8]{2,1,0:T(1,128)S(1)} %all_to_all.10.shares, f32[4,13,80,128]{3,2,1,0:T(8,128)S(1)} %get-tuple-element.59.moved_in, ...), custom_call_target="tpu_custom_call" | custom-call | tf_op jit(solution)/shard_map/pallas_call | solution.py:725
  44.4 13.8 %all_to_all.11.shares = f32[128,1,8]{2,1,0:T(1,128)S(1)} all-to-all(f32[128,1,8]{2,1,0:T(1,128)S(1)} %get-tuple-element.63), channel_id=1, replica_groups=mesh['along'=64,'cross'=2] {'along','cross'}, dimensions={0} | all-to-all | bytes 8192 | tf_op jit(solution)/shard_map/all_to_all | solution.py:742
  58.3 1.8 %shard_map.102 = (f32[4,32,1536]{2,1,0:T(8,128)}, f32[32,1536]{1,0:T(8,128)}, f32[2,32,1536]{2,1,0:T(8,128)}) custom-call(f32[128,1,8]{2,1,0:T(1,128)S(1)} %all_to_all.11.shares, f32[4,13,80,128]{3,2,1,0:T(8,128)S(1)} %get-tuple-element.64.moved, f32[7,13,80,128]{3,2,1,0:T(8,128)S(1)} %get-tuple-element.60.static, ...), custom_call_target="tpu_custom_call" | custom-call | tf_op jit(solution)/shard_map/pallas_call | solution.py:725
Async XLA Ops:
  0.6 11.2 %copy-start.1 = (f32[8]{0:T(128)S(1)}, f32[8]{0:T(128)}, u32[]{:S(2)}) copy-start(f32[8]{0:T(128)} %heads.1) | copy-start | bytes 100
  0.6 11.2 %copy-start = (s32[8,4]{0,1:T(4,128)S(1)}, s32[8,4]{0,1:T(4,128)}, u32[]{:S(2)}) copy-start(s32[8,4]{0,1:T(4,128)} %param.12) | copy-start | bytes 388
  1.7 5.6 %collective-permute-start = (f32[32,128]{1,0:T(8,128)S(1)}, f32[32,128]{1,0:T(8,128)S(1)}, u32[]{:S(2)}, u32[]{:S(2)}) collective-permute-start(f32[32,128]{1,0:T(8,128)S(1)} %shard_map.94), channel_id=1, source_target_pairs={{0,1},{1,0},{2,3},{3,2},{4,5},{5,4},{6,7},{7,6},{8,9},{9,8},{10,11... | collective-permute-start | bytes 49160 | tf_op jit(solution)/shard_map/ppermute | solution.py:773
  7.5 9.9 %collective-permute-start.1 = (f32[1072,128]{1,0:T(8,128)S(1)}, f32[1072,128]{1,0:T(8,128)S(1)}, u32[]{:S(2)}, u32[]{:S(2)}) collective-permute-start(f32[1072,128]{1,0:T(8,128)S(1)} %get-tuple-element.37), channel_id=1, source_target_pairs={{2,4},{3,5},{6,8},{7,9},{10,12},{11,13},{14,16},{15,17},{18,20},{1... | collective-permute-start | bytes 1646600 | tf_op jit(solution)/shard_map/ppermute | solution.py:794
  10.0 5.1 %collective-permute-start.3 = (f32[544,128]{1,0:T(8,128)S(1)}, f32[544,128]{1,0:T(8,128)S(1)}, u32[]{:S(2)}, u32[]{:S(2)}) collective-permute-start(f32[544,128]{1,0:T(8,128)S(1)} %get-tuple-element.40), channel_id=1, source_target_pairs={{0,2},{4,6},{8,10},{12,14},{16,18},{20,22},{24,26},{28,30},{32,34}... | collective-permute-start | bytes 835592 | tf_op jit(solution)/shard_map/ppermute | solution.py:796
  11.8 3.3 %collective-permute-start.2 = (f32[528,128]{1,0:T(8,128)S(1)}, f32[528,128]{1,0:T(8,128)S(1)}, u32[]{:S(2)}, u32[]{:S(2)}) collective-permute-start(f32[528,128]{1,0:T(8,128)S(1)} %get-tuple-element.39), channel_id=1, source_target_pairs={{0,2},{4,6},{8,10},{12,14},{16,18},{20,22},{24,26},{28,30},{32,34}... | collective-permute-start | bytes 811016 | tf_op jit(solution)/shard_map/ppermute | solution.py:796
